TPU v7x, 768 devices: a whole 4x8x12 slice. The times are simulated.
768 devices in a mesh: region: 12 (over z), local: 64 (over x, y, core).
Axes of the slice: x: 4, y: 8, z: 12, core: 2. Of those that a mesh axis runs over, the one named last changes fastest.
Arguments:
- populations: float32 [19, 256, 192, 256], P(None, 'local', 'region'), may hold values from 0.005 to 0.5, as said below
- fluid_mask: int32 [256, 192, 256], P('local', 'region'), may hold values from 0 to 1, as said below
Outputs:
- advanced: float32 [19, 256, 192, 256], P(None, 'local', 'region')
Inputs may be any that keep to these rules, and one draw needn't show every extreme that they name: `fluid_mask`: 1 marks fluid and 0 wall; the fluid sites form one vessel along the second dimension whose rough wall runs close to the grid's sides in the first and third dimensions. `populations`: positive distributions near a local equilibrium.
All inputs are finite; a program needn't handle non-finite values.
Results may differ from a plain program's by a relative error of at most 0.0003.
Values sent between devices are 32-bit elements; how exact they have to be, the bound alone decides.
No kernel may reach another device: no remote copies, remote signals or barrier semaphores. Data moves between devices by JAX's collectives and lax.ppermute only.
A program may use at most 32 MiB of HBM per device.

v0:
```python
import jax
import jax.numpy as jnp
from jax import lax
from jax.sharding import PartitionSpec as P

STEPS = 2


VELOCITIES = (
    (0, 0, 0),
    (1, 0, 0),
    (-1, 0, 0),
    (0, 1, 0),
    (0, -1, 0),
    (0, 0, 1),
    (0, 0, -1),
    (1, 1, 0),
    (-1, -1, 0),
    (1, -1, 0),
    (-1, 1, 0),
    (1, 0, 1),
    (-1, 0, -1),
    (1, 0, -1),
    (-1, 0, 1),
    (0, 1, 1),
    (0, -1, -1),
    (0, 1, -1),
    (0, -1, 1),
)
WEIGHTS = (1.0 / 3.0,) + (1.0 / 18.0,) * 6 + (1.0 / 36.0,) * 12
RELAX = 0.8
GAIN_RATE = 2.0
TARGET_SPEED = 0.05


def with_halo(block, sides, width):
    for axis, dim in sides:
        count = lax.axis_size(axis)
        forward = [(i, i + 1) for i in range(count - 1)]
        backward = [(target, source) for source, target in forward]
        low = lax.ppermute(
            lax.slice_in_dim(block, block.shape[dim] - width, None, axis=dim), axis, forward
        )
        high = lax.ppermute(lax.slice_in_dim(block, 0, width, axis=dim), axis, backward)
        block = jnp.concatenate([low, block, high], axis=dim)
    return block


def opposite_of(number):
    if number == 0:
        return 0
    return number + 1 if number % 2 == 1 else number - 1


def moments(current):
    density = jnp.sum(current, axis=0)
    flux_x = current[1] - current[2]
    flux_y = current[3] - current[4]
    flux_z = current[5] - current[6]
    for number in range(7, 19):
        move_x, move_y, move_z = VELOCITIES[number]
        if move_x != 0:
            flux_x = flux_x + move_x * current[number]
        if move_y != 0:
            flux_y = flux_y + move_y * current[number]
        if move_z != 0:
            flux_z = flux_z + move_z * current[number]
    return (density, flux_x, flux_y, flux_z)


def collide(current, fluid, forcing):
    density, flux_x, flux_y, flux_z = moments(current)
    safe = density + (1.0 - fluid)
    speed_x = flux_x / safe
    speed_y = flux_y / safe + RELAX * forcing
    speed_z = flux_z / safe
    square = speed_x * speed_x + speed_y * speed_y + speed_z * speed_z
    result = []
    for number in range(19):
        move_x, move_y, move_z = VELOCITIES[number]
        projected = move_x * speed_x + move_y * speed_y + move_z * speed_z
        equil = (
            WEIGHTS[number]
            * density
            * (1.0 + 3.0 * projected + 4.5 * projected * projected - 1.5 * square)
        )
        result.append(fluid * (current[number] - (current[number] - equil) / RELAX))
    return jnp.stack(result)


def stream(post, fluid):
    size_x = post.shape[1] - 2
    size_y = post.shape[2] - 2
    size_z = post.shape[3]
    padded = jnp.pad(post, ((0, 0), (0, 0), (0, 0), (1, 1)))
    padded_fluid = jnp.pad(fluid, ((0, 0), (0, 0), (1, 1)))
    center = padded_fluid[1 : 1 + size_x, 1 : 1 + size_y, 1 : 1 + size_z]
    result = []
    for number in range(19):
        move_x, move_y, move_z = VELOCITIES[number]
        source = padded[
            number,
            1 - move_x : 1 - move_x + size_x,
            1 - move_y : 1 - move_y + size_y,
            1 - move_z : 1 - move_z + size_z,
        ]
        source_fluid = padded_fluid[
            1 - move_x : 1 - move_x + size_x,
            1 - move_y : 1 - move_y + size_y,
            1 - move_z : 1 - move_z + size_z,
        ]
        own = post[opposite_of(number), 1 : 1 + size_x, 1 : 1 + size_y, :]
        result.append(center * (source_fluid * source + (1.0 - source_fluid) * own))
    return (jnp.stack(result), center)


def driving(current, fluid):
    density, flux_x, flux_y, flux_z = moments(current)
    totals = lax.psum((jnp.sum(fluid * flux_y), jnp.sum(fluid * density)), ("region", "local"))
    return GAIN_RATE * (TARGET_SPEED - totals[0] / totals[1])


def on_device(populations, fluid_mask):
    fluid = fluid_mask.astype(jnp.float32)
    current = populations
    for step in range(STEPS):
        forcing = driving(current, fluid)
        post = collide(current, fluid, forcing)
        stacked = jnp.concatenate([post, fluid[None]], axis=0)
        widened = with_halo(stacked, (("region", 2), ("local", 1)), 1)
        current, center = stream(widened[:19], widened[19])
    return current


def solution(mesh):
    return jax.shard_map(
        on_device,
        mesh=mesh,
        in_specs=(P(None, "local", "region", None), P("local", "region", None)),
        out_specs=P(None, "local", "region", None),
        check_vma=False,
    )
```

profile of v0, /device:TPU:1, one launch (start us, length us, event | category | flops | bytes accessed | tf_op | source)
XLA Modules:
  0.0 294.4 jit_solution(12996592119537646749)
XLA Ops:
  0.0 1.5 reduce_sum.111
  1.5 0.2 copy-done.1
  1.7 0.7 multiply_reduce_fusion.2
  2.4 120.5 %all-reduce.5 = (f32[]{:T(128)}, f32[]{:T(128)}) all-reduce(f32[]{:T(128)} %get-tuple-element.8, f32[]{:T(128)} %get-tuple-element.7), channel_id=1, replica_groups=mesh['region'=12,'local'=64] {'region','local'}, use_global_device_ids=true, to_apply=%region_2.0 | all-reduce | flops 2 | bytes 16 | tf_op jit(solution)/shard_map/psum | solution.py:119
  126.0 2.2 collective-permute-start
  128.1 1.3 collective-permute-start.1
  129.6 3.7 %collective-permute-done.1 = f32[20,4,1,256]{3,2,1,0:T(1,128)S(1)} collective-permute-done((f32[20,4,1,256]{3,2,1,0:T(1,128)S(1)}, f32[20,4,1,256]{3,2,1,0:T(1,128)S(1)}, u32[]{:S(2)}, u32[]{:S(2)}) %collective-permute-start.1) | collective-permute-done | bytes 81952 | tf_op jit(solution)/shard_map/ppermute | solution.py:44
  133.5 2.2 collective-permute-start.2
  135.7 3.2 %collective-permute-start.3 = (f32[20,1,18,256]{3,2,1,0:T(8,128)S(1)}, f32[20,1,18,256]{3,2,1,0:T(8,128)S(1)}, u32[]{:S(2)}, u32[]{:S(2)}) collective-permute-start(f32[20,1,18,256]{3,2,1,0:T(8,128)S(1)} %get-tuple-element.117), channel_id=1, source_target_pairs={{1,0},{2,1},{3,2},{4,3},{5,4},{6,5},{7,6},{8,7},{9,8},{10,9},{11,1... | collective-permute-start | bytes 1105928 | tf_op jit(solution)/shard_map/ppermute | solution.py:44
  138.8 2.6 collective-permute-done.2
  141.4 4.4 %collective-permute-done.3 = f32[20,1,18,256]{3,2,1,0:T(8,128)S(1)} collective-permute-done((f32[20,1,18,256]{3,2,1,0:T(8,128)S(1)}, f32[20,1,18,256]{3,2,1,0:T(8,128)S(1)}, u32[]{:S(2)}, u32[]{:S(2)}) %collective-permute-start.3) | collective-permute-done | bytes 368672 | tf_op jit(solution)/shard_map/ppermute | solution.py:44
  145.8 4.8 %select_maximum_fusion.4 = f32[19,6,18,258]{3,2,1,0:T(8,128)S(1)} fusion(f32[20,1,18,256]{3,2,1,0:T(8,128)S(1)} %collective-permute-done.3, f32[20,1,18,256]{3,2,1,0:T(8,128)S(1)} %collective-permute-done.2, f32[20,4,1,256]{3,2,1,0:T(1,128)S(1)} %collective-permute-done.1, f32[20,4,16,256]{3,2,1,0:T(8,128)S(1)} %constant_dynamic-update-slice_fusion, ...), kind=kLoop, calls=%fused_computation.6 | loop fusion | flops 6352992 | bytes 4329504 | tf_op jit(solution)/shard_map/concatenate | solution.py:45
  150.6 1.3 multiply_reduce_fusion
  151.9 111.0 %all-reduce.4 = (f32[]{:T(128)}, f32[]{:T(128)}) all-reduce(f32[]{:T(128)} %get-tuple-element.6, f32[]{:T(128)} %get-tuple-element.5), channel_id=1, replica_groups=mesh['region'=12,'local'=64] {'region','local'}, use_global_device_ids=true, to_apply=%region_6.7 | all-reduce | flops 2 | bytes 16 | tf_op jit(solution)/shard_map/psum | solution.py:119
  266.1 2.8 collective-permute-start.4
  268.9 1.3 collective-permute-start.5
  270.3 3.7 %collective-permute-done.5 = f32[20,4,1,256]{3,2,1,0:T(1,128)S(1)} collective-permute-done((f32[20,4,1,256]{3,2,1,0:T(1,128)S(1)}, f32[20,4,1,256]{3,2,1,0:T(1,128)S(1)}, u32[]{:S(2)}, u32[]{:S(2)}) %collective-permute-start.5) | collective-permute-done | bytes 81952 | tf_op jit(solution)/shard_map/ppermute | solution.py:44
  274.2 2.2 collective-permute-start.6
  276.4 3.3 %collective-permute-start.7 = (f32[20,1,18,256]{3,2,1,0:T(8,128)S(1)}, f32[20,1,18,256]{3,2,1,0:T(8,128)S(1)}, u32[]{:S(2)}, u32[]{:S(2)}) collective-permute-start(f32[20,1,18,256]{3,2,1,0:T(8,128)S(1)} %get-tuple-element.115), channel_id=1, source_target_pairs={{1,0},{2,1},{3,2},{4,3},{5,4},{6,5},{7,6},{8,7},{9,8},{10,9},{11,1... | collective-permute-start | bytes 1105928 | tf_op jit(solution)/shard_map/ppermute | solution.py:44
  279.7 2.4 collective-permute-done.6
  282.1 4.4 %collective-permute-done.7 = f32[20,1,18,256]{3,2,1,0:T(8,128)S(1)} collective-permute-done((f32[20,1,18,256]{3,2,1,0:T(8,128)S(1)}, f32[20,1,18,256]{3,2,1,0:T(8,128)S(1)}, u32[]{:S(2)}, u32[]{:S(2)}) %collective-permute-start.7) | collective-permute-done | bytes 368672 | tf_op jit(solution)/shard_map/ppermute | solution.py:44
  286.6 4.8 %select_maximum_fusion = f32[19,6,18,258]{3,2,1,0:T(8,128)S(1)} fusion(f32[20,1,18,256]{3,2,1,0:T(8,128)S(1)} %collective-permute-done.7, f32[20,1,18,256]{3,2,1,0:T(8,128)S(1)} %collective-permute-done.6, f32[20,4,1,256]{3,2,1,0:T(1,128)S(1)} %collective-permute-done.5, f32[20,4,16,256]{3,2,1,0:T(8,128)S(1)} %constant_dynamic-update-slice_fusion.20, ...), kind=kLoop, calls=%fused_computation.2 | loop fusion | flops 6352992 | bytes 4329504 | tf_op jit(solution)/shard_map/concatenate | solution.py:45
  292.6 1.0 copy-done.2
  293.6 0.7 constant_dynamic-update-slice_fusion.40
  (70 shorter events, 5.2 us)
Async XLA Ops:
  0.0 1.7 copy-start.1
  0.0 1.7 copy-start
  126.0 3.6 %collective-permute-start = (f32[20,4,1,256]{3,2,1,0:T(1,128)S(1)}, f32[20,4,1,256]{3,2,1,0:T(1,128)S(1)}, u32[]{:S(2)}, u32[]{:S(2)}) collective-permute-start(f32[20,4,1,256]{3,2,1,0:T(1,128)S(1)} %get-tuple-element.120), channel_id=1, source_target_pairs={{0,64},{64,128},{128,192},{192,256},{256,320},{320,384},{384,448},... | collective-permute-start | bytes 245768 | tf_op jit(solution)/shard_map/ppermute | solution.py:41
  128.1 5.2 %collective-permute-start.1 = (f32[20,4,1,256]{3,2,1,0:T(1,128)S(1)}, f32[20,4,1,256]{3,2,1,0:T(1,128)S(1)}, u32[]{:S(2)}, u32[]{:S(2)}) collective-permute-start(f32[20,4,1,256]{3,2,1,0:T(1,128)S(1)} %get-tuple-element.121), channel_id=1, source_target_pairs={{64,0},{128,64},{192,128},{256,192},{320,256},{384,320},{448,384},... | collective-permute-start | bytes 245768 | tf_op jit(solution)/shard_map/ppermute | solution.py:44
  133.5 7.9 %collective-permute-start.2 = (f32[20,1,18,256]{3,2,1,0:T(8,128)S(1)}, f32[20,1,18,256]{3,2,1,0:T(8,128)S(1)}, u32[]{:S(2)}, u32[]{:S(2)}) collective-permute-start(f32[20,1,18,256]{3,2,1,0:T(8,128)S(1)} %get-tuple-element.116), channel_id=1, source_target_pairs={{0,1},{1,2},{2,3},{3,4},{4,5},{5,6},{6,7},{7,8},{8,9},{9,10},{10,1... | collective-permute-start | bytes 1105928 | tf_op jit(solution)/shard_map/ppermute | solution.py:41
  135.7 10.1 %collective-permute-start.3 = (f32[20,1,18,256]{3,2,1,0:T(8,128)S(1)}, f32[20,1,18,256]{3,2,1,0:T(8,128)S(1)}, u32[]{:S(2)}, u32[]{:S(2)}) collective-permute-start(f32[20,1,18,256]{3,2,1,0:T(8,128)S(1)} %get-tuple-element.117), channel_id=1, source_target_pairs={{1,0},{2,1},{3,2},{4,3},{5,4},{6,5},{7,6},{8,7},{9,8},{10,9},{11,1... | collective-permute-start | bytes 1105928 | tf_op jit(solution)/shard_map/ppermute | solution.py:44
  266.1 4.3 %collective-permute-start.4 = (f32[20,4,1,256]{3,2,1,0:T(1,128)S(1)}, f32[20,4,1,256]{3,2,1,0:T(1,128)S(1)}, u32[]{:S(2)}, u32[]{:S(2)}) collective-permute-start(f32[20,4,1,256]{3,2,1,0:T(1,128)S(1)} %get-tuple-element.118), channel_id=1, source_target_pairs={{0,64},{64,128},{128,192},{192,256},{256,320},{320,384},{384,448},... | collective-permute-start | bytes 245768 | tf_op jit(solution)/shard_map/ppermute | solution.py:41
  268.9 5.2 %collective-permute-start.5 = (f32[20,4,1,256]{3,2,1,0:T(1,128)S(1)}, f32[20,4,1,256]{3,2,1,0:T(1,128)S(1)}, u32[]{:S(2)}, u32[]{:S(2)}) collective-permute-start(f32[20,4,1,256]{3,2,1,0:T(1,128)S(1)} %get-tuple-element.119), channel_id=1, source_target_pairs={{64,0},{128,64},{192,128},{256,192},{320,256},{384,320},{448,384},... | collective-permute-start | bytes 245768 | tf_op jit(solution)/shard_map/ppermute | solution.py:44
  274.2 7.9 %collective-permute-start.6 = (f32[20,1,18,256]{3,2,1,0:T(8,128)S(1)}, f32[20,1,18,256]{3,2,1,0:T(8,128)S(1)}, u32[]{:S(2)}, u32[]{:S(2)}) collective-permute-start(f32[20,1,18,256]{3,2,1,0:T(8,128)S(1)} %get-tuple-element.114), channel_id=1, source_target_pairs={{0,1},{1,2},{2,3},{3,4},{4,5},{5,6},{6,7},{7,8},{8,9},{9,10},{10,1... | collective-permute-start | bytes 1105928 | tf_op jit(solution)/shard_map/ppermute | solution.py:41
  276.4 10.1 %collective-permute-start.7 = (f32[20,1,18,256]{3,2,1,0:T(8,128)S(1)}, f32[20,1,18,256]{3,2,1,0:T(8,128)S(1)}, u32[]{:S(2)}, u32[]{:S(2)}) collective-permute-start(f32[20,1,18,256]{3,2,1,0:T(8,128)S(1)} %get-tuple-element.115), channel_id=1, source_target_pairs={{1,0},{2,1},{3,2},{4,3},{5,4},{6,5},{7,6},{8,7},{9,8},{10,9},{11,1... | collective-permute-start | bytes 1105928 | tf_op jit(solution)/shard_map/ppermute | solution.py:44
  292.6 1.0 copy-start.2
where the time goes:
time: 299 us; the launch traced here: 294 us
  blocking collectives  232 us (78%)
  waiting for transfers between devices  21.6 us (7%)
  starting transfers between devices  18.4 us (6%)
  other arithmetic  18.3 us (6%)
  between operations  3.16 us (1%)
    psum x2, blocking collectives, driving(): lax.psum((jnp.sum(fluid * flux_y), jnp.sum(fluid * density)), ('region',...  232 us
    ppermute x4, waiting for transfers between devices, with_halo(): lax.ppermute(lax.slice_in_dim(block, 0, width, axis=dim), axis, backward)  16.2 us
    concatenate x2, other arithmetic, with_halo(): block = jnp.concatenate([low, block, high], axis=dim)  9.53 us
    ppermute x4, starting transfers between devices, with_halo(): lax.ppermute(lax.slice_in_dim(block, block.shape[dim] - width, None, axis...  9.3 us
    ppermute x4, starting transfers between devices, with_halo(): lax.ppermute(lax.slice_in_dim(block, 0, width, axis=dim), axis, backward)  9.08 us
  transfers between devices with their start and end apart: 8, of which 8 were waited for; matrix products, arithmetic and copies ran while one was open for 0% of the time, Pallas kernels for 0%

commit v1 on v0

v1 whole, which is shorter than its diff:
```python
import jax
import jax.numpy as jnp
from jax import lax
from jax.experimental import pallas as pl
from jax.experimental.pallas import tpu as pltpu
from jax.sharding import Mesh
from jax.sharding import PartitionSpec as P

VELOCITIES = (
    (0, 0, 0),
    (1, 0, 0),
    (-1, 0, 0),
    (0, 1, 0),
    (0, -1, 0),
    (0, 0, 1),
    (0, 0, -1),
    (1, 1, 0),
    (-1, -1, 0),
    (1, -1, 0),
    (-1, 1, 0),
    (1, 0, 1),
    (-1, 0, -1),
    (1, 0, -1),
    (-1, 0, 1),
    (0, 1, 1),
    (0, -1, -1),
    (0, 1, -1),
    (0, -1, 1),
)
RELAX = 0.8
GAIN_RATE = 2.0
TARGET_SPEED = 0.05
KEEP = 1.0 / RELAX - 1.0

NX = 4
NY = 16
LANES = 128
ROWS = NY + 4
FRONT = 8
SOLID = 1e30
LIMIT = 1e29


def opposite_of(number):
    if number == 0:
        return 0
    return number + 1 if number % 2 == 1 else number - 1


def moments(f):
    total = [None] + [f[k] + f[k + 1] for k in range(1, 19, 2)]
    diff = [None] + [f[k] - f[k + 1] for k in range(1, 19, 2)]
    density = f[0]
    for value in total[1:]:
        density = density + value
    flux_x = diff[1] + diff[4] + diff[5] + diff[6] + diff[7]
    flux_y = diff[2] + (diff[4] - diff[5]) + (diff[8] + diff[9])
    flux_z = diff[3] + (diff[6] - diff[7]) + (diff[8] - diff[9])
    return density, flux_x, flux_y, flux_z, total, diff


def collide(f, fluid, shift):
    density, flux_x, flux_y, flux_z, total, diff = moments(f)
    inverse = 1.0 / (density + (1.0 - fluid))
    inverse = inverse * 1.5
    ux = flux_x * inverse
    uy = flux_y * inverse + 1.5 * shift
    uz = flux_z * inverse
    square = ux * ux + uy * uy + uz * uz
    base = 1.0 - square * (2.0 / 3.0)
    scaled = density * (1.0 / RELAX)
    open_site = fluid > 0.5
    weight = (scaled * (1.0 / 3.0), scaled * (1.0 / 18.0), scaled * (1.0 / 36.0))
    base_1 = weight[1] * base
    base_2 = weight[2] * base
    twice_1 = weight[1] * 2.0
    twice_2 = weight[2] * 2.0
    post = [jnp.where(open_site, weight[0] * base - KEEP * f[0], SOLID)]
    along = (None, ux, uy, uz, ux + uy, ux - uy, ux + uz, ux - uz, uy + uz, uy - uz)
    for pair in range(1, 10):
        speed = along[pair]
        odd = speed * (twice_1 if pair <= 3 else twice_2)
        even = (base_1 if pair <= 3 else base_2) + odd * speed
        even = even - (0.5 * KEEP) * total[pair]
        odd = odd - (0.5 * KEEP) * diff[pair]
        post.append(jnp.where(open_site, even + odd, SOLID))
        post.append(jnp.where(open_site, even - odd, SOLID))
    return post


def response(numbers, f, fluid):
    density, flux_x, flux_y, flux_z, _, _ = moments(f)
    inverse = 1.0 / (density + (1.0 - fluid))
    ux = flux_x * inverse
    uy = flux_y * inverse
    uz = flux_z * inverse
    base = 1.0 - 1.5 * (ux * ux + uy * uy + uz * uz)
    scaled = density * (fluid * (1.0 / RELAX))
    result = {}
    for number in numbers:
        move_x, move_y, move_z = VELOCITIES[number]
        weight = scaled * (1.0 / 18.0 if number < 7 else 1.0 / 36.0)
        speed = move_y * uy
        if move_x:
            speed = speed + move_x * ux
        if move_z:
            speed = speed + move_z * uz
        zero = weight * (base + speed * (3.0 + 4.5 * speed)) - (KEEP * fluid) * f[number]
        one = weight * (3.0 * move_y + 9.0 * move_y * speed - 3.0 * uy)
        two = weight * 3.0
        result[number] = (zero, one, two)
    return density, flux_y, result


def pack_kernel(pops, mask, to_low_y, to_high_y, to_low_x, to_high_x):
    for x in range(NX):
        for number in range(19):
            to_low_y[number, 2 * x : 2 * x + 2, :] = pops[number, x, 0:2, :]
            to_high_y[number, 2 * x : 2 * x + 2, :] = pops[number, x, NY - 2 : NY, :]
        to_low_y[19, 2 * x : 2 * x + 2, :] = mask[x, 0:2, :].astype(jnp.float32)
        to_high_y[19, 2 * x : 2 * x + 2, :] = mask[x, NY - 2 : NY, :].astype(jnp.float32)
    for out, x, up, down in ((to_low_x, 0, 10, 8), (to_high_x, NX - 1, 7, 9)):
        out[0:NY, :] = mask[x].astype(jnp.float32)
        out[NY : NY + 8, :] = jnp.zeros((8, 2 * LANES), jnp.float32)
        for place, y, number in ((0, NY - 1, up), (3, 0, down)):
            f = [pops[k, x, y : y + 1, :] for k in range(19)]
            fluid = mask[x, y : y + 1, :].astype(jnp.float32)
            _, _, coefs = response((number,), f, fluid)
            for i in range(3):
                row = NY + place + i
                out[row : row + 1, :] = coefs[number][i]


def sums_kernel(pops, mask, low_y, high_y, low_x, high_x, sums, to_low_x, to_high_x, flags):
    halves = (slice(0, LANES), slice(LANES, 2 * LANES))
    for out, first in ((to_low_x, 0), (to_high_x, NX - 2)):
        for layer in range(2):
            x = first + layer
            row = layer * ROWS
            for number in range(20):
                for half, lanes in enumerate(halves):
                    out[number, half, row : row + 2, :] = low_y[number, 2 * x : 2 * x + 2, lanes]
                    if number < 19:
                        out[number, half, row + 2 : row + 2 + NY, :] = pops[number, x, :, lanes]
                    else:
                        out[number, half, row + 2 : row + 2 + NY, :] = mask[x, :, lanes].astype(
                            jnp.float32
                        )
                    out[number, half, row + 2 + NY : row + ROWS, :] = high_y[
                        number, 2 * x : 2 * x + 2, lanes
                    ]
    flags[...] = jnp.zeros_like(flags)
    for half, lanes in enumerate(halves):
        for x in range(NX):
            row = FRONT + (x + 1) * ROWS
            flags[half, row + 1 : row + 2, :] = low_y[19, 2 * x + 1 : 2 * x + 2, lanes]
            flags[half, row + 2 : row + 2 + NY, :] = mask[x, :, lanes].astype(jnp.float32)
            flags[half, row + 2 + NY : row + 3 + NY, :] = high_y[19, 2 * x : 2 * x + 1, lanes]
        flags[half, FRONT + 2 : FRONT + 2 + NY, :] = low_x[0:NY, lanes]
        row = FRONT + (NX + 1) * ROWS
        flags[half, row + 2 : row + 2 + NY, :] = high_x[0:NY, lanes]
    lane = lax.broadcasted_iota(jnp.int32, (8, LANES), 1)
    numbers = [k for k in range(19) if VELOCITIES[k][1] != 0]
    acc = [jnp.zeros((8, LANES), jnp.float32) for _ in range(5)]
    for x in range(NX):
        for tile in range(NY // 8):
            row = FRONT + (x + 1) * ROWS + 2 + 8 * tile
            for half, lanes in enumerate(halves):
                f = [pops[k, x, 8 * tile : 8 * tile + 8, lanes] for k in range(19)]
                fluid = flags[half, row : row + 8, :]
                density, flux_y, coefs = response(numbers, f, fluid)
                acc[0] = acc[0] + fluid * flux_y
                acc[1] = acc[1] + fluid * density
                for number in numbers:
                    move_x, move_y, move_z = VELOCITIES[number]
                    start = row + move_x * ROWS + move_y
                    if move_z == 0:
                        ahead = flags[half, start : start + 8, :]
                    elif move_z == 1:
                        here = pltpu.roll(flags[half, start : start + 8, :], LANES - 1, 1)
                        if half == 0:
                            other = pltpu.roll(flags[1, start : start + 8, :], LANES - 1, 1)
                            ahead = jnp.where(lane == LANES - 1, other, here)
                        else:
                            ahead = jnp.where(lane == LANES - 1, 0.0, here)
                    else:
                        here = pltpu.roll(flags[half, start : start + 8, :], 1, 1)
                        if half == 1:
                            other = pltpu.roll(flags[0, start : start + 8, :], 1, 1)
                            ahead = jnp.where(lane == 0, other, here)
                        else:
                            ahead = jnp.where(lane == 0, 0.0, here)
                    sign = (2.0 * move_y) * ahead - move_y
                    for i in range(3):
                        acc[2 + i] = acc[2 + i] + sign * coefs[number][i]
    edge = [jnp.zeros((1, 2 * LANES), jnp.float32) for _ in range(3)]
    for beside, x in ((low_x, 0), (high_x, NX - 1)):
        for place, sign, flag in (
            (0, 2.0, high_y[19, 2 * x : 2 * x + 1, :]),
            (3, -2.0, low_y[19, 2 * x + 1 : 2 * x + 2, :]),
        ):
            for i in range(3):
                row = NY + place + i
                edge[i] = edge[i] + (sign * flag) * beside[row : row + 1, :]
    lane = lax.broadcasted_iota(jnp.int32, (1, LANES), 1)
    line = jnp.zeros((1, LANES), jnp.float32)
    for i in range(5):
        value = jnp.sum(acc[i], axis=0, keepdims=True)
        if i >= 2:
            value = value + (edge[i - 2][:, :LANES] + edge[i - 2][:, LANES:])
        value = jnp.sum(value, axis=1, keepdims=True)
        line = jnp.where(lane == i, value, line)
    sums[...] = jnp.broadcast_to(line[None], sums.shape)


def relay_kernel(arrived, sums):
    sums[...] = jnp.broadcast_to(jnp.sum(arrived[...], axis=0, keepdims=True), sums.shape)


def gather_row(post, number, half, row):
    return post[number, half, row : row + 8, :]


def streamed(post, row, lane):
    result = [[None] * 19, [None] * 19]
    for number in range(19):
        move_x, move_y, move_z = VELOCITIES[number]
        start = row - move_x * ROWS - move_y
        if number == 0:
            for half in range(2):
                result[half][0] = gather_row(post, 0, half, row)
            continue
        first = gather_row(post, number, 0, start)
        second = gather_row(post, number, 1, start)
        if move_z == 1:
            first = pltpu.roll(first, 1, 1)
            second = pltpu.roll(second, 1, 1)
            second = jnp.where(lane == 0, first, second)
            first = jnp.where(lane == 0, SOLID, first)
        elif move_z == -1:
            first = pltpu.roll(first, LANES - 1, 1)
            second = pltpu.roll(second, LANES - 1, 1)
            first = jnp.where(lane == LANES - 1, second, first)
            second = jnp.where(lane == LANES - 1, SOLID, second)
        for half, value in enumerate((first, second)):
            own = gather_row(post, opposite_of(number), half, row)
            result[half][number] = jnp.where(value < LIMIT, value, own)
    return result


def steps_kernel(arrived, pops, mask, low_y, high_y, low_x, high_x, out, post, later, flags):
    halves = (slice(0, LANES), slice(LANES, 2 * LANES))
    sums = jnp.sum(arrived[...], axis=0)

    def total(i):
        return jnp.broadcast_to(sums[:, i : i + 1], (8, LANES))

    mass = total(1)
    drive = GAIN_RATE * (TARGET_SPEED - total(0) / mass)
    shift_1 = RELAX * drive
    momentum = total(2) + shift_1 * (total(3) + shift_1 * total(4))
    drive = GAIN_RATE * (TARGET_SPEED - momentum / mass)
    shift_2 = RELAX * drive
    lane = lax.broadcasted_iota(jnp.int32, (8, LANES), 1)

    for x in range(NX):
        for tile in range(NY // 8):
            row = FRONT + (x + 2) * ROWS + 2 + 8 * tile
            for half, lanes in enumerate(halves):
                f = [pops[k, x, 8 * tile : 8 * tile + 8, lanes] for k in range(19)]
                fluid = mask[x, 8 * tile : 8 * tile + 8, lanes].astype(jnp.float32)
                flags[half, row : row + 8, :] = fluid
                for number, value in enumerate(collide(f, fluid, shift_1)):
                    post[number, half, row : row + 8, :] = value
    for beside, start in ((low_y, 0), (high_y, 2 + NY)):
        for half, lanes in enumerate(halves):
            f = [beside[k, :, lanes] for k in range(19)]
            fluid = beside[19, :, lanes]
            value = collide(f, fluid, shift_1)
            for x in range(NX):
                row = FRONT + (x + 2) * ROWS + start
                flags[half, row : row + 2, :] = fluid[2 * x : 2 * x + 2]
                for number in range(19):
                    post[number, half, row : row + 2, :] = value[number][2 * x : 2 * x + 2]
    for beside, start in ((low_x, 0), (high_x, (NX + 2) * ROWS)):
        for half in range(2):
            for tile in range(2 * ROWS // 8):
                at = slice(8 * tile, 8 * tile + 8)
                row = FRONT + start + 8 * tile
                f = [beside[k, half, at, :] for k in range(19)]
                fluid = beside[19, half, at, :]
                flags[half, row : row + 8, :] = fluid
                for number, value in enumerate(collide(f, fluid, shift_1)):
                    post[number, half, row : row + 8, :] = value
    for tile in range((NX + 2) * ROWS // 8):
        row = FRONT + ROWS + 8 * tile
        f = streamed(post, row, lane)
        for half in range(2):
            fluid = flags[half, row : row + 8, :]
            for number, value in enumerate(collide(f[half], fluid, shift_2)):
                later[number, half, row : row + 8, :] = value
    for x in range(NX):
        for tile in range(NY // 8):
            row = FRONT + (x + 2) * ROWS + 2 + 8 * tile
            f = streamed(later, row, lane)
            for half, lanes in enumerate(halves):
                open_site = flags[half, row : row + 8, :] > 0.5
                for number in range(19):
                    out[number, x, 8 * tile : 8 * tile + 8, lanes] = jnp.where(
                        open_site, f[half][number], 0.0
                    )


def f32(*shape):
    return jax.ShapeDtypeStruct(shape, jnp.float32)


def params():
    return pltpu.CompilerParams(vmem_limit_bytes=32 * 1024 * 1024)


def solution(mesh):
    regions, blocks = mesh.devices.shape
    cores = 2
    ring = 8 if blocks % 16 == 0 else 1
    grid = Mesh(
        mesh.devices.reshape(regions, blocks // (cores * ring), ring, cores),
        ("region", "x", "y", "core"),
    )
    local = ("x", "y", "core")
    first, second = regions * cores, blocks // cores

    def shifted(value, axis, count, step):
        pairs = [(i, i + step) for i in range(count) if 0 <= i + step < count]
        return lax.ppermute(value, axis, pairs)

    def on_device(pops, mask):
        to_low_y, to_high_y, to_low_x, to_high_x = pl.pallas_call(
            pack_kernel,
            out_shape=(f32(20, 8, 256), f32(20, 8, 256), f32(24, 256), f32(24, 256)),
            compiler_params=params(),
        )(pops, mask)
        low_y = shifted(to_high_y, "region", regions, 1)
        high_y = shifted(to_low_y, "region", regions, -1)
        low_x = shifted(to_high_x, local, blocks, 1)
        high_x = shifted(to_low_x, local, blocks, -1)
        sums, to_low_x, to_high_x = pl.pallas_call(
            sums_kernel,
            out_shape=(
                f32(first, 1, LANES),
                f32(20, 2, 2 * ROWS, LANES),
                f32(20, 2, 2 * ROWS, LANES),
            ),
            scratch_shapes=[pltpu.VMEM((2, FRONT + (NX + 2) * ROWS + 8, LANES), jnp.float32)],
            compiler_params=params(),
        )(pops, mask, low_y, high_y, low_x, high_x)
        low_x = shifted(to_high_x, local, blocks, 1)
        high_x = shifted(to_low_x, local, blocks, -1)
        sums = lax.all_to_all(sums, ("region", "core"), 0, 0, tiled=True)
        sums = pl.pallas_call(
            relay_kernel, out_shape=f32(second, 1, LANES), compiler_params=params()
        )(sums)
        sums = lax.all_to_all(sums, ("x", "y"), 0, 0, tiled=True)
        rows = FRONT + (NX + 4) * ROWS + 8
        return pl.pallas_call(
            steps_kernel,
            out_shape=f32(19, NX, NY, 2 * LANES),
            scratch_shapes=[
                pltpu.VMEM((19, 2, rows, LANES), jnp.float32),
                pltpu.VMEM((19, 2, rows, LANES), jnp.float32),
                pltpu.VMEM((2, rows, LANES), jnp.float32),
            ],
            compiler_params=params(),
        )(sums, pops, mask, low_y, high_y, low_x, high_x)

    return jax.shard_map(
        on_device,
        mesh=grid,
        in_specs=(P(None, local, "region", None), P(local, "region", None)),
        out_specs=P(None, local, "region", None),
        check_vma=False,
    )
```

time: 299 us -> 72.3 us (0.24); the launches traced: 294 us -> 71.9 us
  blocking collectives: 232 us -> 42.7 us
  waiting for transfers between devices: 21.6 us -> 0.83 us
  other arithmetic: 18.3 us -> 0 us
  Pallas kernels: 0 us -> 4.69 us
  starting transfers between devices: 18.4 us -> 21.5 us
  between operations: 3.16 us -> 0.08 us
    psum x2 -> x0, blocking collectives: 232 us -> none  [driving(): lax.psum((jnp.sum(fluid * flux_y), jnp.sum(fluid * density)), ('region',...]
    all_to_all x0 -> x2, blocking collectives: none -> 42.7 us  [the longest x1 22.2 us: on_device(): sums = lax.all_to_all(sums, ('region', 'core'), 0, 0, tiled=True)]
    ppermute x8 -> x6, waiting for transfers between devices: 21.6 us -> 0.83 us  [shifted(): return lax.ppermute(value, axis, pairs)]
    concatenate x4 -> x0, other arithmetic: 9.55 us -> none  [the longest x2 9.53 us: with_halo(): block = jnp.concatenate([low, block, high], axis=dim)]
    pallas_call x0 -> x4, Pallas kernels: none -> 4.69 us  [the longest x1 3.6 us: on_device(): pl.pallas_call(steps_kernel, out_shape=f32(19, NX, NY, 2 * LANES), scratc...]
    unnamed x56 -> x0, other arithmetic: 4.24 us -> none
    reduce_sum x3 -> x0, other arithmetic: 3.46 us -> none  [the longest x2 1.98 us: driving(): jnp.sum(fluid * density)]
    ppermute x8 -> x6, starting transfers between devices: 18.4 us -> 21.5 us  [shifted(): return lax.ppermute(value, axis, pairs)]
  transfers between devices with their start and end apart: 8 -> 6, of which waited for: 8 -> 1; matrix products, arithmetic and copies ran while one was open for 0% -> 0% of each run, Pallas kernels for 0% -> 0%
where the time goes in v1:
time: 72.3 us; the launch traced here: 71.9 us
  blocking collectives  42.7 us (59%)
  starting transfers between devices  21.5 us (30%)
  Pallas kernels  4.69 us (6%)
  local copies, waits for them, and re-layouts  2.14 us (3%)
  waiting for transfers between devices  0.83 us (1%)
    all_to_all x1, blocking collectives, on_device(): sums = lax.all_to_all(sums, ('region', 'core'), 0, 0, tiled=True)  22.2 us
    ppermute x6, starting transfers between devices, shifted(): return lax.ppermute(value, axis, pairs)  21.5 us
    all_to_all x1, blocking collectives, on_device(): sums = lax.all_to_all(sums, ('x', 'y'), 0, 0, tiled=True)  20.4 us
    pallas_call x1, Pallas kernels, on_device(): pl.pallas_call(steps_kernel, out_shape=f32(19, NX, NY, 2 * LANES), scratc...  3.6 us
    unnamed x6, local copies, waits for them, and re-layouts  2.14 us
  transfers between devices with their start and end apart: 6, of which 1 were waited for; matrix products, arithmetic and copies ran while one was open for 0% of the time, Pallas kernels for 0%

profile of v1, /device:TPU:1, one launch (start us, length us, event | category | flops | bytes accessed | tf_op | source)
XLA Modules:
  0.0 71.9 jit_solution(9226273365441648910)
XLA Ops:
  0.0 0.0 copy-start
  0.0 1.3 %copy-done = f32[19,4,16,256]{3,2,1,0:T(8,128)S(1)} copy-done((f32[19,4,16,256]{3,2,1,0:T(8,128)S(1)}, f32[19,4,16,256]{3,2,1,0:T(8,128)}, u32[]{:S(2)}) %copy-start) | copy-done | bytes 1245208
  1.3 0.0 copy-start.2
  1.3 0.8 %copy-done.2 = s32[4,16,256]{2,1,0:T(8,128)S(1)} copy-done((s32[4,16,256]{2,1,0:T(8,128)S(1)}, s32[4,16,256]{2,1,0:T(8,128)}, u32[]{:S(2)}) %copy-start.2) | copy-done | bytes 65560
  2.1 0.0 copy-start.1
  2.1 0.2 shard_map.28
  2.3 5.0 %collective-permute-start = (f32[20,8,256]{2,1,0:T(8,128)S(1)}, f32[20,8,256]{2,1,0:T(8,128)S(1)}, u32[]{:S(2)}, u32[]{:S(2)}) collective-permute-start(f32[20,8,256]{2,1,0:T(8,128)S(1)} %get-tuple-element.12), channel_id=1, source_target_pairs={{0,64},{64,128},{128,192},{192,256},{256,320},{320,384},{384,448},... | collective-permute-start | bytes 491528 | tf_op jit(solution)/shard_map/ppermute | solution.py:335
  7.3 1.3 %collective-permute-start.1 = (f32[20,8,256]{2,1,0:T(8,128)S(1)}, f32[20,8,256]{2,1,0:T(8,128)S(1)}, u32[]{:S(2)}, u32[]{:S(2)}) collective-permute-start(f32[20,8,256]{2,1,0:T(8,128)S(1)} %get-tuple-element.13), channel_id=1, source_target_pairs={{64,0},{128,64},{192,128},{256,192},{320,256},{384,320},{448,384},... | collective-permute-start | bytes 491528 | tf_op jit(solution)/shard_map/ppermute | solution.py:335
  8.6 4.0 %collective-permute-start.2 = (f32[24,256]{1,0:T(8,128)S(1)}, f32[24,256]{1,0:T(8,128)S(1)}, u32[]{:S(2)}, u32[]{:S(2)}) collective-permute-start(f32[24,256]{1,0:T(8,128)S(1)} %get-tuple-element.14), channel_id=1, source_target_pairs={{0,1},{1,2},{2,3},{3,4},{4,5},{5,6},{6,7},{7,8},{8,9},{9,10},{10,1... | collective-permute-start | bytes 73736 | tf_op jit(solution)/shard_map/ppermute | solution.py:335
  12.7 6.1 %collective-permute-start.3 = (f32[24,256]{1,0:T(8,128)S(1)}, f32[24,256]{1,0:T(8,128)S(1)}, u32[]{:S(2)}, u32[]{:S(2)}) collective-permute-start(f32[24,256]{1,0:T(8,128)S(1)} %get-tuple-element.15), channel_id=1, source_target_pairs={{1,0},{2,1},{3,2},{4,3},{5,4},{6,5},{7,6},{8,7},{9,8},{10,9},{11,1... | collective-permute-start | bytes 73736 | tf_op jit(solution)/shard_map/ppermute | solution.py:335
  18.8 0.0 collective-permute-done.2.low_x
  18.8 0.8 %collective-permute-done.3.high_x = f32[24,256]{1,0:T(8,128)S(1)} collective-permute-done((f32[24,256]{1,0:T(8,128)S(1)}, f32[24,256]{1,0:T(8,128)S(1)}, u32[]{:S(2)}, u32[]{:S(2)}) %collective-permute-start.3) | collective-permute-done | bytes 24608 | tf_op jit(solution)/shard_map/ppermute | solution.py:335
  19.6 0.0 collective-permute-done.low_y
  19.6 0.0 collective-permute-done.1.high_y
  19.6 0.9 %shard_map.29 = (f32[24,1,128]{2,1,0:T(1,128)S(1)}, f32[20,2,40,128]{3,2,1,0:T(8,128)S(1)}, f32[20,2,40,128]{3,2,1,0:T(8,128)S(1)}) custom-call(f32[19,4,16,256]{3,2,1,0:T(8,128)S(1)} %copy-done, s32[4,16,256]{2,1,0:T(8,128)S(1)} %copy-done.2, f32[20,8,256]{2,1,0:T(8,128)S(1)} %collective-permute-done.low_y, ...), custom_call_target="tpu_custom_call" | custom-call | tf_op jit(solution)/shard_map/pallas_call | solution.py:347
  20.5 1.9 %collective-permute-start.4 = (f32[20,2,40,128]{3,2,1,0:T(8,128)S(1)}, f32[20,2,40,128]{3,2,1,0:T(8,128)S(1)}, u32[]{:S(2)}, u32[]{:S(2)}) collective-permute-start(f32[20,2,40,128]{3,2,1,0:T(8,128)S(1)} %get-tuple-element.17), channel_id=1, source_target_pairs={{0,1},{1,2},{2,3},{3,4},{4,5},{5,6},{6,7},{7,8},{8,9},{9,10},{10,1... | collective-permute-start | bytes 2457608 | tf_op jit(solution)/shard_map/ppermute | solution.py:335
  22.4 3.2 %collective-permute-start.5 = (f32[20,2,40,128]{3,2,1,0:T(8,128)S(1)}, f32[20,2,40,128]{3,2,1,0:T(8,128)S(1)}, u32[]{:S(2)}, u32[]{:S(2)}) collective-permute-start(f32[20,2,40,128]{3,2,1,0:T(8,128)S(1)} %get-tuple-element.18), channel_id=1, source_target_pairs={{1,0},{2,1},{3,2},{4,3},{5,4},{6,5},{7,6},{8,7},{9,8},{10,9},{11,1... | collective-permute-start | bytes 2457608 | tf_op jit(solution)/shard_map/ppermute | solution.py:335
  25.6 22.2 %all_to_all.10.arrived = f32[24,1,128]{2,1,0:T(1,128)S(1)} all-to-all(f32[24,1,128]{2,1,0:T(1,128)S(1)} %get-tuple-element.16), channel_id=1, replica_groups=mesh['region'=12,'x'=4,'y'=8,'core'=2] {'region','core'}, dimensions={0} | all-to-all | bytes 24576 | tf_op jit(solution)/shard_map/all_to_all | solution.py:359
  47.9 20.4 %all_to_all.11.arrived = f32[32,1,128]{2,1,0:T(1,128)S(1)} all-to-all(f32[32,1,128]{2,1,0:T(1,128)S(1)} %shard_map.30), channel_id=1, replica_groups=mesh['region'=12,'x'=4,'y'=8,'core'=2] {'x','y'}, dimensions={0} | all-to-all | bytes 32768 | tf_op jit(solution)/shard_map/all_to_all | solution.py:363
  68.3 0.0 collective-permute-done.4.low_x
  68.3 0.0 collective-permute-done.5.high_x
  68.3 0.0 copy-done.1
  68.3 3.6 %shard_map.31 = f32[19,4,16,256]{3,2,1,0:T(8,128)} custom-call(f32[32,1,128]{2,1,0:T(1,128)S(1)} %all_to_all.11.arrived, f32[19,4,16,256]{3,2,1,0:T(8,128)S(1)} %copy-done.1, s32[4,16,256]{2,1,0:T(8,128)S(1)} %copy-done.2, f32[20,8,256]{2,1,0:T(8,128)S(1)} %collective-permute-done.low_y, f32[20,8,256]{2,1,0:T(8,128)S(1)} %collective-permute-done.1.high_y, ...), custom_call_target="tpu_custom_call" | custom-call | tf_op jit(solution)/shard_map/pallas_call | solution.py:365
  (1 shorter events, 0.0 us)
Async XLA Ops:
  0.0 1.3 %copy-start = (f32[19,4,16,256]{3,2,1,0:T(8,128)S(1)}, f32[19,4,16,256]{3,2,1,0:T(8,128)}, u32[]{:S(2)}) copy-start(f32[19,4,16,256]{3,2,1,0:T(8,128)} %pops.5) | copy-start | bytes 3735556
  1.3 0.8 %copy-start.2 = (s32[4,16,256]{2,1,0:T(8,128)S(1)}, s32[4,16,256]{2,1,0:T(8,128)}, u32[]{:S(2)}) copy-start(s32[4,16,256]{2,1,0:T(8,128)} %mask.5) | copy-start | bytes 196612
  2.1 66.2 %copy-start.1 = (f32[19,4,16,256]{3,2,1,0:T(8,128)S(1)}, f32[19,4,16,256]{3,2,1,0:T(8,128)}, u32[]{:S(2)}) copy-start(f32[19,4,16,256]{3,2,1,0:T(8,128)} %pops.5) | copy-start | bytes 3735556
  2.3 17.3 %collective-permute-start = (f32[20,8,256]{2,1,0:T(8,128)S(1)}, f32[20,8,256]{2,1,0:T(8,128)S(1)}, u32[]{:S(2)}, u32[]{:S(2)}) collective-permute-start(f32[20,8,256]{2,1,0:T(8,128)S(1)} %get-tuple-element.12), channel_id=1, source_target_pairs={{0,64},{64,128},{128,192},{192,256},{256,320},{320,384},{384,448},... | collective-permute-start | bytes 491528 | tf_op jit(solution)/shard_map/ppermute | solution.py:335
  7.3 12.3 %collective-permute-start.1 = (f32[20,8,256]{2,1,0:T(8,128)S(1)}, f32[20,8,256]{2,1,0:T(8,128)S(1)}, u32[]{:S(2)}, u32[]{:S(2)}) collective-permute-start(f32[20,8,256]{2,1,0:T(8,128)S(1)} %get-tuple-element.13), channel_id=1, source_target_pairs={{64,0},{128,64},{192,128},{256,192},{320,256},{384,320},{448,384},... | collective-permute-start | bytes 491528 | tf_op jit(solution)/shard_map/ppermute | solution.py:335
  8.6 10.2 %collective-permute-start.2 = (f32[24,256]{1,0:T(8,128)S(1)}, f32[24,256]{1,0:T(8,128)S(1)}, u32[]{:S(2)}, u32[]{:S(2)}) collective-permute-start(f32[24,256]{1,0:T(8,128)S(1)} %get-tuple-element.14), channel_id=1, source_target_pairs={{0,1},{1,2},{2,3},{3,4},{4,5},{5,6},{6,7},{7,8},{8,9},{9,10},{10,1... | collective-permute-start | bytes 73736 | tf_op jit(solution)/shard_map/ppermute | solution.py:335
  12.7 7.0 %collective-permute-start.3 = (f32[24,256]{1,0:T(8,128)S(1)}, f32[24,256]{1,0:T(8,128)S(1)}, u32[]{:S(2)}, u32[]{:S(2)}) collective-permute-start(f32[24,256]{1,0:T(8,128)S(1)} %get-tuple-element.15), channel_id=1, source_target_pairs={{1,0},{2,1},{3,2},{4,3},{5,4},{6,5},{7,6},{8,7},{9,8},{10,9},{11,1... | collective-permute-start | bytes 73736 | tf_op jit(solution)/shard_map/ppermute | solution.py:335
  20.5 47.8 %collective-permute-start.4 = (f32[20,2,40,128]{3,2,1,0:T(8,128)S(1)}, f32[20,2,40,128]{3,2,1,0:T(8,128)S(1)}, u32[]{:S(2)}, u32[]{:S(2)}) collective-permute-start(f32[20,2,40,128]{3,2,1,0:T(8,128)S(1)} %get-tuple-element.17), channel_id=1, source_target_pairs={{0,1},{1,2},{2,3},{3,4},{4,5},{5,6},{6,7},{7,8},{8,9},{9,10},{10,1... | collective-permute-start | bytes 2457608 | tf_op jit(solution)/shard_map/ppermute | solution.py:335
  22.4 45.9 %collective-permute-start.5 = (f32[20,2,40,128]{3,2,1,0:T(8,128)S(1)}, f32[20,2,40,128]{3,2,1,0:T(8,128)S(1)}, u32[]{:S(2)}, u32[]{:S(2)}) collective-permute-start(f32[20,2,40,128]{3,2,1,0:T(8,128)S(1)} %get-tuple-element.18), channel_id=1, source_target_pairs={{1,0},{2,1},{3,2},{4,3},{5,4},{6,5},{7,6},{8,7},{9,8},{10,9},{11,1... | collective-permute-start | bytes 2457608 | tf_op jit(solution)/shard_map/ppermute | solution.py:335

commit v2 on v1

--- a/solution.py
+++ b/solution.py
@@ -328,7 +328,7 @@
         ("region", "x", "y", "core"),
     )
     local = ("x", "y", "core")
-    first, second = regions * cores, blocks // cores
+    first, second = blocks // cores, regions * cores
 
     def shifted(value, axis, count, step):
         pairs = [(i, i + step) for i in range(count) if 0 <= i + step < count]
@@ -356,11 +356,11 @@
         )(pops, mask, low_y, high_y, low_x, high_x)
         low_x = shifted(to_high_x, local, blocks, 1)
         high_x = shifted(to_low_x, local, blocks, -1)
-        sums = lax.all_to_all(sums, ("region", "core"), 0, 0, tiled=True)
+        sums = lax.all_to_all(sums, ("x", "y"), 0, 0, tiled=True)
         sums = pl.pallas_call(
             relay_kernel, out_shape=f32(second, 1, LANES), compiler_params=params()
         )(sums)
-        sums = lax.all_to_all(sums, ("x", "y"), 0, 0, tiled=True)
+        sums = lax.all_to_all(sums, ("region", "core"), 0, 0, tiled=True)
         rows = FRONT + (NX + 4) * ROWS + 8
         return pl.pallas_call(
             steps_kernel,

time: 72.3 us -> 73.8 us (1.021)
  blocking collectives: 42.7 us -> 44.1 us
    all_to_all x1, blocking collectives: 22.2 us -> 28.4 us  [on_device(): sums = lax.all_to_all(sums, ('region', 'core'), 0, 0, tiled=True)]
    all_to_all x1, blocking collectives: 20.4 us -> 15.7 us  [on_device(): sums = lax.all_to_all(sums, ('x', 'y'), 0, 0, tiled=True)]
where the time goes in v2:
time: 73.8 us; the launch traced here: 73.4 us
  blocking collectives  44.1 us (60%)
  starting transfers between devices  21.5 us (29%)
  Pallas kernels  4.68 us (6%)
  local copies, waits for them, and re-layouts  2.14 us (3%)
  waiting for transfers between devices  0.83 us (1%)
    all_to_all x1, blocking collectives, on_device(): sums = lax.all_to_all(sums, ('region', 'core'), 0, 0, tiled=True)  28.4 us
    ppermute x6, starting transfers between devices, shifted(): return lax.ppermute(value, axis, pairs)  21.5 us
    all_to_all x1, blocking collectives, on_device(): sums = lax.all_to_all(sums, ('x', 'y'), 0, 0, tiled=True)  15.7 us
    pallas_call x1, Pallas kernels, on_device(): pl.pallas_call(steps_kernel, out_shape=f32(19, NX, NY, 2 * LANES), scratc...  3.58 us
    unnamed x6, local copies, waits for them, and re-layouts  2.14 us
  transfers between devices with their start and end apart: 6, of which 1 were waited for; matrix products, arithmetic and copies ran while one was open for 0% of the time, Pallas kernels for 0%

profile of v2, /device:TPU:1, one launch (start us, length us, event | category | flops | bytes accessed | tf_op | source)
XLA Modules:
  0.0 73.4 jit_solution(1074261427712769943)
XLA Ops:
  0.0 0.0 copy-start
  0.0 1.3 %copy-done = f32[19,4,16,256]{3,2,1,0:T(8,128)S(1)} copy-done((f32[19,4,16,256]{3,2,1,0:T(8,128)S(1)}, f32[19,4,16,256]{3,2,1,0:T(8,128)}, u32[]{:S(2)}) %copy-start) | copy-done | bytes 1245208
  1.3 0.0 copy-start.2
  1.3 0.8 %copy-done.2 = s32[4,16,256]{2,1,0:T(8,128)S(1)} copy-done((s32[4,16,256]{2,1,0:T(8,128)S(1)}, s32[4,16,256]{2,1,0:T(8,128)}, u32[]{:S(2)}) %copy-start.2) | copy-done | bytes 65560
  2.1 0.0 copy-start.1
  2.1 0.2 shard_map.28
  2.3 5.0 %collective-permute-start = (f32[20,8,256]{2,1,0:T(8,128)S(1)}, f32[20,8,256]{2,1,0:T(8,128)S(1)}, u32[]{:S(2)}, u32[]{:S(2)}) collective-permute-start(f32[20,8,256]{2,1,0:T(8,128)S(1)} %get-tuple-element.12), channel_id=1, source_target_pairs={{0,64},{64,128},{128,192},{192,256},{256,320},{320,384},{384,448},... | collective-permute-start | bytes 491528 | tf_op jit(solution)/shard_map/ppermute | solution.py:335
  7.3 1.3 %collective-permute-start.1 = (f32[20,8,256]{2,1,0:T(8,128)S(1)}, f32[20,8,256]{2,1,0:T(8,128)S(1)}, u32[]{:S(2)}, u32[]{:S(2)}) collective-permute-start(f32[20,8,256]{2,1,0:T(8,128)S(1)} %get-tuple-element.13), channel_id=1, source_target_pairs={{64,0},{128,64},{192,128},{256,192},{320,256},{384,320},{448,384},... | collective-permute-start | bytes 491528 | tf_op jit(solution)/shard_map/ppermute | solution.py:335
  8.6 4.0 %collective-permute-start.2 = (f32[24,256]{1,0:T(8,128)S(1)}, f32[24,256]{1,0:T(8,128)S(1)}, u32[]{:S(2)}, u32[]{:S(2)}) collective-permute-start(f32[24,256]{1,0:T(8,128)S(1)} %get-tuple-element.14), channel_id=1, source_target_pairs={{0,1},{1,2},{2,3},{3,4},{4,5},{5,6},{6,7},{7,8},{8,9},{9,10},{10,1... | collective-permute-start | bytes 73736 | tf_op jit(solution)/shard_map/ppermute | solution.py:335
  12.7 6.1 %collective-permute-start.3 = (f32[24,256]{1,0:T(8,128)S(1)}, f32[24,256]{1,0:T(8,128)S(1)}, u32[]{:S(2)}, u32[]{:S(2)}) collective-permute-start(f32[24,256]{1,0:T(8,128)S(1)} %get-tuple-element.15), channel_id=1, source_target_pairs={{1,0},{2,1},{3,2},{4,3},{5,4},{6,5},{7,6},{8,7},{9,8},{10,9},{11,1... | collective-permute-start | bytes 73736 | tf_op jit(solution)/shard_map/ppermute | solution.py:335
  18.8 0.0 collective-permute-done.2.low_x
  18.8 0.8 %collective-permute-done.3.high_x = f32[24,256]{1,0:T(8,128)S(1)} collective-permute-done((f32[24,256]{1,0:T(8,128)S(1)}, f32[24,256]{1,0:T(8,128)S(1)}, u32[]{:S(2)}, u32[]{:S(2)}) %collective-permute-start.3) | collective-permute-done | bytes 24608 | tf_op jit(solution)/shard_map/ppermute | solution.py:335
  19.6 0.0 collective-permute-done.low_y
  19.6 0.0 collective-permute-done.1.high_y
  19.6 0.9 %shard_map.29 = (f32[32,1,128]{2,1,0:T(1,128)S(1)}, f32[20,2,40,128]{3,2,1,0:T(8,128)S(1)}, f32[20,2,40,128]{3,2,1,0:T(8,128)S(1)}) custom-call(f32[19,4,16,256]{3,2,1,0:T(8,128)S(1)} %copy-done, s32[4,16,256]{2,1,0:T(8,128)S(1)} %copy-done.2, f32[20,8,256]{2,1,0:T(8,128)S(1)} %collective-permute-done.low_y, ...), custom_call_target="tpu_custom_call" | custom-call | tf_op jit(solution)/shard_map/pallas_call | solution.py:347
  20.5 1.9 %collective-permute-start.4 = (f32[20,2,40,128]{3,2,1,0:T(8,128)S(1)}, f32[20,2,40,128]{3,2,1,0:T(8,128)S(1)}, u32[]{:S(2)}, u32[]{:S(2)}) collective-permute-start(f32[20,2,40,128]{3,2,1,0:T(8,128)S(1)} %get-tuple-element.17), channel_id=1, source_target_pairs={{0,1},{1,2},{2,3},{3,4},{4,5},{5,6},{6,7},{7,8},{8,9},{9,10},{10,1... | collective-permute-start | bytes 2457608 | tf_op jit(solution)/shard_map/ppermute | solution.py:335
  22.4 3.2 %collective-permute-start.5 = (f32[20,2,40,128]{3,2,1,0:T(8,128)S(1)}, f32[20,2,40,128]{3,2,1,0:T(8,128)S(1)}, u32[]{:S(2)}, u32[]{:S(2)}) collective-permute-start(f32[20,2,40,128]{3,2,1,0:T(8,128)S(1)} %get-tuple-element.18), channel_id=1, source_target_pairs={{1,0},{2,1},{3,2},{4,3},{5,4},{6,5},{7,6},{8,7},{9,8},{10,9},{11,1... | collective-permute-start | bytes 2457608 | tf_op jit(solution)/shard_map/ppermute | solution.py:335
  25.6 15.7 %all_to_all.10.arrived = f32[32,1,128]{2,1,0:T(1,128)S(1)} all-to-all(f32[32,1,128]{2,1,0:T(1,128)S(1)} %get-tuple-element.16), channel_id=1, replica_groups=mesh['region'=12,'x'=4,'y'=8,'core'=2] {'x','y'}, dimensions={0} | all-to-all | bytes 32768 | tf_op jit(solution)/shard_map/all_to_all | solution.py:359
  41.4 28.4 %all_to_all.11.arrived = f32[24,1,128]{2,1,0:T(1,128)S(1)} all-to-all(f32[24,1,128]{2,1,0:T(1,128)S(1)} %shard_map.30), channel_id=1, replica_groups=mesh['region'=12,'x'=4,'y'=8,'core'=2] {'region','core'}, dimensions={0} | all-to-all | bytes 24576 | tf_op jit(solution)/shard_map/all_to_all | solution.py:363
  69.8 0.0 collective-permute-done.4.low_x
  69.8 0.0 collective-permute-done.5.high_x
  69.8 0.0 copy-done.1
  69.8 3.6 %shard_map.31 = f32[19,4,16,256]{3,2,1,0:T(8,128)} custom-call(f32[24,1,128]{2,1,0:T(1,128)S(1)} %all_to_all.11.arrived, f32[19,4,16,256]{3,2,1,0:T(8,128)S(1)} %copy-done.1, s32[4,16,256]{2,1,0:T(8,128)S(1)} %copy-done.2, f32[20,8,256]{2,1,0:T(8,128)S(1)} %collective-permute-done.low_y, f32[20,8,256]{2,1,0:T(8,128)S(1)} %collective-permute-done.1.high_y, ...), custom_call_target="tpu_custom_call" | custom-call | tf_op jit(solution)/shard_map/pallas_call | solution.py:365
  (1 shorter events, 0.0 us)
Async XLA Ops:
  0.0 1.3 %copy-start = (f32[19,4,16,256]{3,2,1,0:T(8,128)S(1)}, f32[19,4,16,256]{3,2,1,0:T(8,128)}, u32[]{:S(2)}) copy-start(f32[19,4,16,256]{3,2,1,0:T(8,128)} %pops.5) | copy-start | bytes 3735556
  1.3 0.8 %copy-start.2 = (s32[4,16,256]{2,1,0:T(8,128)S(1)}, s32[4,16,256]{2,1,0:T(8,128)}, u32[]{:S(2)}) copy-start(s32[4,16,256]{2,1,0:T(8,128)} %mask.5) | copy-start | bytes 196612
  2.1 67.6 %copy-start.1 = (f32[19,4,16,256]{3,2,1,0:T(8,128)S(1)}, f32[19,4,16,256]{3,2,1,0:T(8,128)}, u32[]{:S(2)}) copy-start(f32[19,4,16,256]{3,2,1,0:T(8,128)} %pops.5) | copy-start | bytes 3735556
  2.3 17.3 %collective-permute-start = (f32[20,8,256]{2,1,0:T(8,128)S(1)}, f32[20,8,256]{2,1,0:T(8,128)S(1)}, u32[]{:S(2)}, u32[]{:S(2)}) collective-permute-start(f32[20,8,256]{2,1,0:T(8,128)S(1)} %get-tuple-element.12), channel_id=1, source_target_pairs={{0,64},{64,128},{128,192},{192,256},{256,320},{320,384},{384,448},... | collective-permute-start | bytes 491528 | tf_op jit(solution)/shard_map/ppermute | solution.py:335
  7.3 12.3 %collective-permute-start.1 = (f32[20,8,256]{2,1,0:T(8,128)S(1)}, f32[20,8,256]{2,1,0:T(8,128)S(1)}, u32[]{:S(2)}, u32[]{:S(2)}) collective-permute-start(f32[20,8,256]{2,1,0:T(8,128)S(1)} %get-tuple-element.13), channel_id=1, source_target_pairs={{64,0},{128,64},{192,128},{256,192},{320,256},{384,320},{448,384},... | collective-permute-start | bytes 491528 | tf_op jit(solution)/shard_map/ppermute | solution.py:335
  8.6 10.2 %collective-permute-start.2 = (f32[24,256]{1,0:T(8,128)S(1)}, f32[24,256]{1,0:T(8,128)S(1)}, u32[]{:S(2)}, u32[]{:S(2)}) collective-permute-start(f32[24,256]{1,0:T(8,128)S(1)} %get-tuple-element.14), channel_id=1, source_target_pairs={{0,1},{1,2},{2,3},{3,4},{4,5},{5,6},{6,7},{7,8},{8,9},{9,10},{10,1... | collective-permute-start | bytes 73736 | tf_op jit(solution)/shard_map/ppermute | solution.py:335
  12.7 7.0 %collective-permute-start.3 = (f32[24,256]{1,0:T(8,128)S(1)}, f32[24,256]{1,0:T(8,128)S(1)}, u32[]{:S(2)}, u32[]{:S(2)}) collective-permute-start(f32[24,256]{1,0:T(8,128)S(1)} %get-tuple-element.15), channel_id=1, source_target_pairs={{1,0},{2,1},{3,2},{4,3},{5,4},{6,5},{7,6},{8,7},{9,8},{10,9},{11,1... | collective-permute-start | bytes 73736 | tf_op jit(solution)/shard_map/ppermute | solution.py:335
  20.5 49.3 %collective-permute-start.4 = (f32[20,2,40,128]{3,2,1,0:T(8,128)S(1)}, f32[20,2,40,128]{3,2,1,0:T(8,128)S(1)}, u32[]{:S(2)}, u32[]{:S(2)}) collective-permute-start(f32[20,2,40,128]{3,2,1,0:T(8,128)S(1)} %get-tuple-element.17), channel_id=1, source_target_pairs={{0,1},{1,2},{2,3},{3,4},{4,5},{5,6},{6,7},{7,8},{8,9},{9,10},{10,1... | collective-permute-start | bytes 2457608 | tf_op jit(solution)/shard_map/ppermute | solution.py:335
  22.4 47.3 %collective-permute-start.5 = (f32[20,2,40,128]{3,2,1,0:T(8,128)S(1)}, f32[20,2,40,128]{3,2,1,0:T(8,128)S(1)}, u32[]{:S(2)}, u32[]{:S(2)}) collective-permute-start(f32[20,2,40,128]{3,2,1,0:T(8,128)S(1)} %get-tuple-element.18), channel_id=1, source_target_pairs={{1,0},{2,1},{3,2},{4,3},{5,4},{6,5},{7,6},{8,7},{9,8},{10,9},{11,1... | collective-permute-start | bytes 2457608 | tf_op jit(solution)/shard_map/ppermute | solution.py:335

commit v3 on v2

--- a/solution.py
+++ b/solution.py
@@ -112,43 +112,47 @@
     return density, flux_y, result
 
 
-def pack_kernel(pops, mask, to_low_y, to_high_y, to_low_x, to_high_x):
+def pack_kernel(pops, mask, to_low_y, to_high_y):
     for x in range(NX):
+        rows = slice(2 * x, 2 * x + 2)
         for number in range(19):
-            to_low_y[number, 2 * x : 2 * x + 2, :] = pops[number, x, 0:2, :]
-            to_high_y[number, 2 * x : 2 * x + 2, :] = pops[number, x, NY - 2 : NY, :]
-        to_low_y[19, 2 * x : 2 * x + 2, :] = mask[x, 0:2, :].astype(jnp.float32)
-        to_high_y[19, 2 * x : 2 * x + 2, :] = mask[x, NY - 2 : NY, :].astype(jnp.float32)
-    for out, x, up, down in ((to_low_x, 0, 10, 8), (to_high_x, NX - 1, 7, 9)):
-        out[0:NY, :] = mask[x].astype(jnp.float32)
-        out[NY : NY + 8, :] = jnp.zeros((8, 2 * LANES), jnp.float32)
-        for place, y, number in ((0, NY - 1, up), (3, 0, down)):
-            f = [pops[k, x, y : y + 1, :] for k in range(19)]
-            fluid = mask[x, y : y + 1, :].astype(jnp.float32)
-            _, _, coefs = response((number,), f, fluid)
-            for i in range(3):
-                row = NY + place + i
-                out[row : row + 1, :] = coefs[number][i]
-
-
-def sums_kernel(pops, mask, low_y, high_y, low_x, high_x, sums, to_low_x, to_high_x, flags):
+            to_low_y[number, rows, :] = pops[number, x, 0:2, :]
+            to_high_y[number, rows, :] = pops[number, x, NY - 2 : NY, :]
+        to_low_y[19, rows, :] = mask[x, 0:2, :].astype(jnp.float32)
+        to_high_y[19, rows, :] = mask[x, NY - 2 : NY, :].astype(jnp.float32)
+
+
+def sums_kernel(pops, mask, low_y, high_y, mate_mask, far_mask, sums, to_mate, to_far, flags):
     halves = (slice(0, LANES), slice(LANES, 2 * LANES))
-    for out, first in ((to_low_x, 0), (to_high_x, NX - 2)):
+    core = lax.axis_index("core")
+    def pack(out, first):
         for layer in range(2):
             x = first + layer
             row = layer * ROWS
+            pair = slice(2 * x, 2 * x + 2)
             for number in range(20):
                 for half, lanes in enumerate(halves):
-                    out[number, half, row : row + 2, :] = low_y[number, 2 * x : 2 * x + 2, lanes]
+                    out[number, half, row : row + 2, :] = low_y[number, pair, lanes]
                     if number < 19:
-                        out[number, half, row + 2 : row + 2 + NY, :] = pops[number, x, :, lanes]
+                        block = pops[number, x, :, lanes]
                     else:
-                        out[number, half, row + 2 : row + 2 + NY, :] = mask[x, :, lanes].astype(
-                            jnp.float32
-                        )
-                    out[number, half, row + 2 + NY : row + ROWS, :] = high_y[
-                        number, 2 * x : 2 * x + 2, lanes
-                    ]
+                        block = mask[x, :, lanes].astype(jnp.float32)
+                    out[number, half, row + 2 : row + 2 + NY, :] = block
+                    out[number, half, row + 2 + NY : row + ROWS, :] = high_y[number, pair, lanes]
+
+    @pl.when(core == 0)
+    def _():
+        pack(to_mate, NX - 2)
+        pack(to_far, 0)
+
+    @pl.when(core == 1)
+    def _():
+        pack(to_mate, 0)
+        pack(to_far, NX - 2)
+
+    first_core = core == 0
+    low_x = jnp.where(first_core, far_mask[NX - 1], mate_mask[NX - 1]).astype(jnp.float32)
+    high_x = jnp.where(first_core, mate_mask[0], far_mask[0]).astype(jnp.float32)
     flags[...] = jnp.zeros_like(flags)
     for half, lanes in enumerate(halves):
         for x in range(NX):
@@ -156,9 +160,9 @@
             flags[half, row + 1 : row + 2, :] = low_y[19, 2 * x + 1 : 2 * x + 2, lanes]
             flags[half, row + 2 : row + 2 + NY, :] = mask[x, :, lanes].astype(jnp.float32)
             flags[half, row + 2 + NY : row + 3 + NY, :] = high_y[19, 2 * x : 2 * x + 1, lanes]
-        flags[half, FRONT + 2 : FRONT + 2 + NY, :] = low_x[0:NY, lanes]
+        flags[half, FRONT + 2 : FRONT + 2 + NY, :] = low_x[:, lanes]
         row = FRONT + (NX + 1) * ROWS
-        flags[half, row + 2 : row + 2 + NY, :] = high_x[0:NY, lanes]
+        flags[half, row + 2 : row + 2 + NY, :] = high_x[:, lanes]
     lane = lax.broadcasted_iota(jnp.int32, (8, LANES), 1)
     numbers = [k for k in range(19) if VELOCITIES[k][1] != 0]
     acc = [jnp.zeros((8, LANES), jnp.float32) for _ in range(5)]
@@ -193,21 +197,22 @@
                     sign = (2.0 * move_y) * ahead - move_y
                     for i in range(3):
                         acc[2 + i] = acc[2 + i] + sign * coefs[number][i]
-    edge = [jnp.zeros((1, 2 * LANES), jnp.float32) for _ in range(3)]
-    for beside, x in ((low_x, 0), (high_x, NX - 1)):
-        for place, sign, flag in (
-            (0, 2.0, high_y[19, 2 * x : 2 * x + 1, :]),
-            (3, -2.0, low_y[19, 2 * x + 1 : 2 * x + 2, :]),
-        ):
-            for i in range(3):
-                row = NY + place + i
-                edge[i] = edge[i] + (sign * flag) * beside[row : row + 1, :]
+    place = lax.broadcasted_iota(jnp.int32, (8, LANES), 0)
+    for beside, y, sign, links in (
+        (low_y, 0, 2.0, ((10, 1, low_x), (7, 2 * NX - 1, high_x))),
+        (high_y, NY - 1, -2.0, ((8, 0, low_x), (9, 2 * NX - 2, high_x))),
+    ):
+        for lanes in halves:
+            f = [beside[k, :, lanes] for k in range(19)]
+            _, _, coefs = response([link[0] for link in links], f, beside[19, :, lanes])
+            for number, row, layer in links:
+                ahead = jnp.where(place == row, sign * layer[y : y + 1, lanes], 0.0)
+                for i in range(3):
+                    acc[2 + i] = acc[2 + i] + ahead * coefs[number][i]
     lane = lax.broadcasted_iota(jnp.int32, (1, LANES), 1)
     line = jnp.zeros((1, LANES), jnp.float32)
     for i in range(5):
         value = jnp.sum(acc[i], axis=0, keepdims=True)
-        if i >= 2:
-            value = value + (edge[i - 2][:, :LANES] + edge[i - 2][:, LANES:])
         value = jnp.sum(value, axis=1, keepdims=True)
         line = jnp.where(lane == i, value, line)
     sums[...] = jnp.broadcast_to(line[None], sums.shape)
@@ -248,7 +253,7 @@
     return result
 
 
-def steps_kernel(arrived, pops, mask, low_y, high_y, low_x, high_x, out, post, later, flags):
+def steps_kernel(arrived, pops, mask, low_y, high_y, mate, far, out, post, later, flags):
     halves = (slice(0, LANES), slice(LANES, 2 * LANES))
     sums = jnp.sum(arrived[...], axis=0)
 
@@ -282,16 +287,18 @@
                 flags[half, row : row + 2, :] = fluid[2 * x : 2 * x + 2]
                 for number in range(19):
                     post[number, half, row : row + 2, :] = value[number][2 * x : 2 * x + 2]
-    for beside, start in ((low_x, 0), (high_x, (NX + 2) * ROWS)):
+    core = lax.axis_index("core")
+    for beside, side in ((mate, 1 - core), (far, core)):
+        start = pl.multiple_of(FRONT + side * ((NX + 2) * ROWS), 8)
         for half in range(2):
             for tile in range(2 * ROWS // 8):
                 at = slice(8 * tile, 8 * tile + 8)
-                row = FRONT + start + 8 * tile
+                rows = pl.ds(start + 8 * tile, 8)
                 f = [beside[k, half, at, :] for k in range(19)]
                 fluid = beside[19, half, at, :]
-                flags[half, row : row + 8, :] = fluid
+                flags[half, rows, :] = fluid
                 for number, value in enumerate(collide(f, fluid, shift_1)):
-                    post[number, half, row : row + 8, :] = value
+                    post[number, half, rows, :] = value
     for tile in range((NX + 2) * ROWS // 8):
         row = FRONT + ROWS + 8 * tile
         f = streamed(post, row, lane)
@@ -330,21 +337,28 @@
     local = ("x", "y", "core")
     first, second = blocks // cores, regions * cores
 
-    def shifted(value, axis, count, step):
-        pairs = [(i, i + step) for i in range(count) if 0 <= i + step < count]
-        return lax.ppermute(value, axis, pairs)
+    def shifted(value, step):
+        pairs = [(i, i + step) for i in range(regions) if 0 <= i + step < regions]
+        return lax.ppermute(value, "region", pairs)
+
+    def from_mate(value):
+        return lax.ppermute(value, "core", [(0, 1), (1, 0)])
+
+    def from_far(value):
+        ends = [(i, i + 1) for i in range(1, blocks - 1, 2)]
+        return lax.ppermute(value, local, ends + [(j, i) for i, j in ends])
 
     def on_device(pops, mask):
-        to_low_y, to_high_y, to_low_x, to_high_x = pl.pallas_call(
+        mate_mask = from_mate(mask)
+        to_low_y, to_high_y = pl.pallas_call(
             pack_kernel,
-            out_shape=(f32(20, 8, 256), f32(20, 8, 256), f32(24, 256), f32(24, 256)),
+            out_shape=(f32(20, 8, 256), f32(20, 8, 256)),
             compiler_params=params(),
         )(pops, mask)
-        low_y = shifted(to_high_y, "region", regions, 1)
-        high_y = shifted(to_low_y, "region", regions, -1)
-        low_x = shifted(to_high_x, local, blocks, 1)
-        high_x = shifted(to_low_x, local, blocks, -1)
-        sums, to_low_x, to_high_x = pl.pallas_call(
+        low_y = shifted(to_high_y, 1)
+        high_y = shifted(to_low_y, -1)
+        far_mask = from_far(mask)
+        sums, to_mate, to_far = pl.pallas_call(
             sums_kernel,
             out_shape=(
                 f32(first, 1, LANES),
@@ -353,9 +367,9 @@
             ),
             scratch_shapes=[pltpu.VMEM((2, FRONT + (NX + 2) * ROWS + 8, LANES), jnp.float32)],
             compiler_params=params(),
-        )(pops, mask, low_y, high_y, low_x, high_x)
-        low_x = shifted(to_high_x, local, blocks, 1)
-        high_x = shifted(to_low_x, local, blocks, -1)
+        )(pops, mask, low_y, high_y, mate_mask, far_mask)
+        mate = from_mate(to_mate)
+        far = from_far(to_far)
         sums = lax.all_to_all(sums, ("x", "y"), 0, 0, tiled=True)
         sums = pl.pallas_call(
             relay_kernel, out_shape=f32(second, 1, LANES), compiler_params=params()
@@ -371,7 +385,7 @@
                 pltpu.VMEM((2, rows, LANES), jnp.float32),
             ],
             compiler_params=params(),
-        )(sums, pops, mask, low_y, high_y, low_x, high_x)
+        )(sums, pops, mask, low_y, high_y, mate, far)
 
     return jax.shard_map(
         on_device,

time: 73.8 us -> 70.8 us (0.959)
  blocking collectives: 44.1 us -> 40.5 us
    all_to_all x1, blocking collectives: 15.7 us -> 13.3 us  [on_device(): sums = lax.all_to_all(sums, ('x', 'y'), 0, 0, tiled=True)]
    all_to_all x1, blocking collectives: 28.4 us -> 27.1 us  [on_device(): sums = lax.all_to_all(sums, ('region', 'core'), 0, 0, tiled=True)]
where the time goes in v3:
time: 70.8 us; the launch traced here: 70.4 us
  blocking collectives  40.5 us (57%)
  starting transfers between devices  22.1 us (31%)
  Pallas kernels  4.77 us (7%)
  local copies, waits for them, and re-layouts  2.14 us (3%)
  waiting for transfers between devices  0.88 us (1%)
    all_to_all x1, blocking collectives, on_device(): sums = lax.all_to_all(sums, ('region', 'core'), 0, 0, tiled=True)  27.1 us
    all_to_all x1, blocking collectives, on_device(): sums = lax.all_to_all(sums, ('x', 'y'), 0, 0, tiled=True)  13.3 us
    ppermute x2, starting transfers between devices, from_mate(): return lax.ppermute(value, 'core', [(0, 1), (1, 0)])  9.85 us
    ppermute x2, starting transfers between devices, shifted(): return lax.ppermute(value, 'region', pairs)  6.26 us
    ppermute x2, starting transfers between devices, from_far(): return lax.ppermute(value, local, ends + [(j, i) for i, j in ends])  5.97 us
    pallas_call x1, Pallas kernels, on_device(): pl.pallas_call(steps_kernel, out_shape=f32(19, NX, NY, 2 * LANES), scratc...  3.6 us
    unnamed x6, local copies, waits for them, and re-layouts  2.14 us
  transfers between devices with their start and end apart: 6, of which 1 were waited for; matrix products, arithmetic and copies ran while one was open for 0% of the time, Pallas kernels for 0%

profile of v3, /device:TPU:1, one launch (start us, length us, event | category | flops | bytes accessed | tf_op | source)
XLA Modules:
  0.0 70.4 jit_solution(15710945845538290657)
XLA Ops:
  0.0 0.0 copy-start
  0.0 1.3 %copy-done = f32[19,4,16,256]{3,2,1,0:T(8,128)S(1)} copy-done((f32[19,4,16,256]{3,2,1,0:T(8,128)S(1)}, f32[19,4,16,256]{3,2,1,0:T(8,128)}, u32[]{:S(2)}) %copy-start) | copy-done | bytes 1245208
  1.3 0.0 copy-start.2
  1.3 0.8 %copy-done.2 = s32[4,16,256]{2,1,0:T(8,128)S(1)} copy-done((s32[4,16,256]{2,1,0:T(8,128)S(1)}, s32[4,16,256]{2,1,0:T(8,128)}, u32[]{:S(2)}) %copy-start.2) | copy-done | bytes 65560
  2.1 0.1 shard_map.28
  2.3 0.0 copy-start.1
  2.3 5.0 %collective-permute-start = (f32[20,8,256]{2,1,0:T(8,128)S(1)}, f32[20,8,256]{2,1,0:T(8,128)S(1)}, u32[]{:S(2)}, u32[]{:S(2)}) collective-permute-start(f32[20,8,256]{2,1,0:T(8,128)S(1)} %get-tuple-element.10), channel_id=1, source_target_pairs={{0,64},{64,128},{128,192},{192,256},{256,320},{320,384},{384,448},... | collective-permute-start | bytes 491528 | tf_op jit(solution)/shard_map/ppermute | solution.py:342
  7.3 1.3 %collective-permute-start.1 = (f32[20,8,256]{2,1,0:T(8,128)S(1)}, f32[20,8,256]{2,1,0:T(8,128)S(1)}, u32[]{:S(2)}, u32[]{:S(2)}) collective-permute-start(f32[20,8,256]{2,1,0:T(8,128)S(1)} %get-tuple-element.11), channel_id=1, source_target_pairs={{64,0},{128,64},{192,128},{256,192},{320,256},{384,320},{448,384},... | collective-permute-start | bytes 491528 | tf_op jit(solution)/shard_map/ppermute | solution.py:342
  8.6 4.0 %collective-permute-start.3 = (s32[4,16,256]{2,1,0:T(8,128)S(1)}, s32[4,16,256]{2,1,0:T(8,128)S(1)}, u32[]{:S(2)}, u32[]{:S(2)}) collective-permute-start(s32[4,16,256]{2,1,0:T(8,128)S(1)} %copy-done.2), channel_id=1, source_target_pairs={{1,2},{3,4},{5,6},{7,8},{9,10},{11,12},{13,14},{15,16},{17,18},{19... | collective-permute-start | bytes 196616 | tf_op jit(solution)/shard_map/ppermute | solution.py:349
  12.6 5.5 %collective-permute-start.2 = (s32[4,16,256]{2,1,0:T(8,128)S(1)}, s32[4,16,256]{2,1,0:T(8,128)S(1)}, u32[]{:S(2)}, u32[]{:S(2)}) collective-permute-start(s32[4,16,256]{2,1,0:T(8,128)S(1)} %copy-done.2), channel_id=1, source_target_pairs={{0,1},{1,0},{2,3},{3,2},{4,5},{5,4},{6,7},{7,6},{8,9},{9,8},{10,11... | collective-permute-start | bytes 196616 | tf_op jit(solution)/shard_map/ppermute | solution.py:345
  18.1 0.0 collective-permute-done.3.far_mask
  18.1 0.9 %collective-permute-done.2.mate_mask = s32[4,16,256]{2,1,0:T(8,128)S(1)} collective-permute-done((s32[4,16,256]{2,1,0:T(8,128)S(1)}, s32[4,16,256]{2,1,0:T(8,128)S(1)}, u32[]{:S(2)}, u32[]{:S(2)}) %collective-permute-start.2) | collective-permute-done | bytes 65568 | tf_op jit(solution)/shard_map/ppermute | solution.py:345
  19.0 0.0 collective-permute-done.low_y
  19.0 0.0 collective-permute-done.1.high_y
  19.0 1.0 %shard_map.29 = (f32[32,1,128]{2,1,0:T(1,128)S(1)}, f32[20,2,40,128]{3,2,1,0:T(8,128)S(1)}, f32[20,2,40,128]{3,2,1,0:T(8,128)S(1)}) custom-call(f32[19,4,16,256]{3,2,1,0:T(8,128)S(1)} %copy-done, s32[4,16,256]{2,1,0:T(8,128)S(1)} %copy-done.2, f32[20,8,256]{2,1,0:T(8,128)S(1)} %collective-permute-done.low_y, ...), custom_call_target="tpu_custom_call" | custom-call | tf_op jit(solution)/shard_map/pallas_call | solution.py:361
  20.0 4.3 %collective-permute-start.4 = (f32[20,2,40,128]{3,2,1,0:T(8,128)S(1)}, f32[20,2,40,128]{3,2,1,0:T(8,128)S(1)}, u32[]{:S(2)}, u32[]{:S(2)}) collective-permute-start(f32[20,2,40,128]{3,2,1,0:T(8,128)S(1)} %get-tuple-element.13), channel_id=1, source_target_pairs={{0,1},{1,0},{2,3},{3,2},{4,5},{5,4},{6,7},{7,6},{8,9},{9,8},{10,11... | collective-permute-start | bytes 2457608 | tf_op jit(solution)/shard_map/ppermute | solution.py:345
  24.4 1.9 %collective-permute-start.5 = (f32[20,2,40,128]{3,2,1,0:T(8,128)S(1)}, f32[20,2,40,128]{3,2,1,0:T(8,128)S(1)}, u32[]{:S(2)}, u32[]{:S(2)}) collective-permute-start(f32[20,2,40,128]{3,2,1,0:T(8,128)S(1)} %get-tuple-element.14), channel_id=1, source_target_pairs={{1,2},{3,4},{5,6},{7,8},{9,10},{11,12},{13,14},{15,16},{17,18},{19... | collective-permute-start | bytes 2457608 | tf_op jit(solution)/shard_map/ppermute | solution.py:349
  26.3 13.3 %all_to_all.10.arrived = f32[32,1,128]{2,1,0:T(1,128)S(1)} all-to-all(f32[32,1,128]{2,1,0:T(1,128)S(1)} %get-tuple-element.12), channel_id=1, replica_groups=mesh['region'=12,'x'=4,'y'=8,'core'=2] {'x','y'}, dimensions={0} | all-to-all | bytes 32768 | tf_op jit(solution)/shard_map/all_to_all | solution.py:373
  39.7 27.1 %all_to_all.11.arrived = f32[24,1,128]{2,1,0:T(1,128)S(1)} all-to-all(f32[24,1,128]{2,1,0:T(1,128)S(1)} %shard_map.30), channel_id=1, replica_groups=mesh['region'=12,'x'=4,'y'=8,'core'=2] {'region','core'}, dimensions={0} | all-to-all | bytes 24576 | tf_op jit(solution)/shard_map/all_to_all | solution.py:377
  66.8 0.0 collective-permute-done.4.mate
  66.8 0.0 collective-permute-done.5.far
  66.8 0.0 copy-done.1
  66.8 3.6 %shard_map.31 = f32[19,4,16,256]{3,2,1,0:T(8,128)} custom-call(f32[24,1,128]{2,1,0:T(1,128)S(1)} %all_to_all.11.arrived, f32[19,4,16,256]{3,2,1,0:T(8,128)S(1)} %copy-done.1, s32[4,16,256]{2,1,0:T(8,128)S(1)} %copy-done.2, f32[20,8,256]{2,1,0:T(8,128)S(1)} %collective-permute-done.low_y, f32[20,8,256]{2,1,0:T(8,128)S(1)} %collective-permute-done.1.high_y, ...), custom_call_target="tpu_custom_call" | custom-call | tf_op jit(solution)/shard_map/pallas_call | solution.py:379
  (1 shorter events, 0.0 us)
Async XLA Ops:
  0.0 1.3 %copy-start = (f32[19,4,16,256]{3,2,1,0:T(8,128)S(1)}, f32[19,4,16,256]{3,2,1,0:T(8,128)}, u32[]{:S(2)}) copy-start(f32[19,4,16,256]{3,2,1,0:T(8,128)} %pops.5) | copy-start | bytes 3735556
  1.3 0.8 %copy-start.2 = (s32[4,16,256]{2,1,0:T(8,128)S(1)}, s32[4,16,256]{2,1,0:T(8,128)}, u32[]{:S(2)}) copy-start(s32[4,16,256]{2,1,0:T(8,128)} %mask.5) | copy-start | bytes 196612
  2.3 64.5 %copy-start.1 = (f32[19,4,16,256]{3,2,1,0:T(8,128)S(1)}, f32[19,4,16,256]{3,2,1,0:T(8,128)}, u32[]{:S(2)}) copy-start(f32[19,4,16,256]{3,2,1,0:T(8,128)} %pops.5) | copy-start | bytes 3735556
  2.3 16.7 %collective-permute-start = (f32[20,8,256]{2,1,0:T(8,128)S(1)}, f32[20,8,256]{2,1,0:T(8,128)S(1)}, u32[]{:S(2)}, u32[]{:S(2)}) collective-permute-start(f32[20,8,256]{2,1,0:T(8,128)S(1)} %get-tuple-element.10), channel_id=1, source_target_pairs={{0,64},{64,128},{128,192},{192,256},{256,320},{320,384},{384,448},... | collective-permute-start | bytes 491528 | tf_op jit(solution)/shard_map/ppermute | solution.py:342
  7.3 11.8 %collective-permute-start.1 = (f32[20,8,256]{2,1,0:T(8,128)S(1)}, f32[20,8,256]{2,1,0:T(8,128)S(1)}, u32[]{:S(2)}, u32[]{:S(2)}) collective-permute-start(f32[20,8,256]{2,1,0:T(8,128)S(1)} %get-tuple-element.11), channel_id=1, source_target_pairs={{64,0},{128,64},{192,128},{256,192},{320,256},{384,320},{448,384},... | collective-permute-start | bytes 491528 | tf_op jit(solution)/shard_map/ppermute | solution.py:342
  8.6 9.6 %collective-permute-start.3 = (s32[4,16,256]{2,1,0:T(8,128)S(1)}, s32[4,16,256]{2,1,0:T(8,128)S(1)}, u32[]{:S(2)}, u32[]{:S(2)}) collective-permute-start(s32[4,16,256]{2,1,0:T(8,128)S(1)} %copy-done.2), channel_id=1, source_target_pairs={{1,2},{3,4},{5,6},{7,8},{9,10},{11,12},{13,14},{15,16},{17,18},{19... | collective-permute-start | bytes 196616 | tf_op jit(solution)/shard_map/ppermute | solution.py:349
  12.6 6.4 %collective-permute-start.2 = (s32[4,16,256]{2,1,0:T(8,128)S(1)}, s32[4,16,256]{2,1,0:T(8,128)S(1)}, u32[]{:S(2)}, u32[]{:S(2)}) collective-permute-start(s32[4,16,256]{2,1,0:T(8,128)S(1)} %copy-done.2), channel_id=1, source_target_pairs={{0,1},{1,0},{2,3},{3,2},{4,5},{5,4},{6,7},{7,6},{8,9},{9,8},{10,11... | collective-permute-start | bytes 196616 | tf_op jit(solution)/shard_map/ppermute | solution.py:345
  20.0 46.8 %collective-permute-start.4 = (f32[20,2,40,128]{3,2,1,0:T(8,128)S(1)}, f32[20,2,40,128]{3,2,1,0:T(8,128)S(1)}, u32[]{:S(2)}, u32[]{:S(2)}) collective-permute-start(f32[20,2,40,128]{3,2,1,0:T(8,128)S(1)} %get-tuple-element.13), channel_id=1, source_target_pairs={{0,1},{1,0},{2,3},{3,2},{4,5},{5,4},{6,7},{7,6},{8,9},{9,8},{10,11... | collective-permute-start | bytes 2457608 | tf_op jit(solution)/shard_map/ppermute | solution.py:345
  24.4 42.4 %collective-permute-start.5 = (f32[20,2,40,128]{3,2,1,0:T(8,128)S(1)}, f32[20,2,40,128]{3,2,1,0:T(8,128)S(1)}, u32[]{:S(2)}, u32[]{:S(2)}) collective-permute-start(f32[20,2,40,128]{3,2,1,0:T(8,128)S(1)} %get-tuple-element.14), channel_id=1, source_target_pairs={{1,2},{3,4},{5,6},{7,8},{9,10},{11,12},{13,14},{15,16},{17,18},{19... | collective-permute-start | bytes 2457608 | tf_op jit(solution)/shard_map/ppermute | solution.py:349

commit v4 on v3

--- a/solution.py
+++ b/solution.py
@@ -39,6 +39,10 @@
 FRONT = 8
 SOLID = 1e30
 LIMIT = 1e29
+HALVES = (slice(0, LANES), slice(LANES, 2 * LANES))
+TOWARD_HIGH = (1, 7, 9, 11, 13)
+TOWARD_LOW = (2, 10, 8, 14, 12)
+SLOTS = 15
 
 
 def opposite_of(number):
@@ -112,47 +116,75 @@
     return density, flux_y, result
 
 
-def pack_kernel(pops, mask, to_low_y, to_high_y):
+def pack_kernel(
+    pops_in, mask_in, pops, mask, to_low_y, to_high_y, to_far, to_mate, pops_sem, mask_sem
+):
+    pops_copy = pltpu.make_async_copy(pops_in, pops, pops_sem)
+    mask_copy = pltpu.make_async_copy(mask_in, mask, mask_sem)
+    pops_copy.start()
+    mask_copy.start()
+    mask_copy.wait()
+    core = lax.axis_index("core")
+    for x in range(NX):
+        rows = slice(2 * x, 2 * x + 2)
+        to_low_y[19, rows, :] = mask[x, 0:2, :].astype(jnp.float32)
+        to_high_y[19, rows, :] = mask[x, NY - 2 : NY, :].astype(jnp.float32)
+
+    to_mate[...] = mask[(1 - core) * (NX - 1)].astype(jnp.float32)
+    to_far[...] = mask[core * (NX - 1)].astype(jnp.float32)
+    pops_copy.wait()
     for x in range(NX):
         rows = slice(2 * x, 2 * x + 2)
         for number in range(19):
             to_low_y[number, rows, :] = pops[number, x, 0:2, :]
             to_high_y[number, rows, :] = pops[number, x, NY - 2 : NY, :]
-        to_low_y[19, rows, :] = mask[x, 0:2, :].astype(jnp.float32)
-        to_high_y[19, rows, :] = mask[x, NY - 2 : NY, :].astype(jnp.float32)
-
-
-def sums_kernel(pops, mask, low_y, high_y, mate_mask, far_mask, sums, to_mate, to_far, flags):
-    halves = (slice(0, LANES), slice(LANES, 2 * LANES))
+
+
+def pack_layers(pops, mask, low_y, high_y, out, up):
+    pieces = ((low_y, 0, 2), (None, 2, 8), (None, 10, 8), (high_y, 2 + NY, 2))
+
+    def piece(part, number, x, half):
+        beside, start, size = part
+        lanes = HALVES[half]
+        if beside is not None:
+            return beside[number, 2 * x : 2 * x + 2, lanes]
+        if number < 19:
+            return pops[number, x, start - 2 : start - 2 + size, lanes]
+        return mask[x, start - 2 : start - 2 + size, lanes].astype(jnp.float32)
+
+    def put(plane, part, half, value):
+        row = (plane % 2) * ROWS + part[1]
+        out[plane // 2, half, row : row + part[2], :] = value
+
+    border, behind = (NX - 1, NX - 2) if up else (0, 1)
+    for half in range(2):
+        for part in pieces:
+            for number in range(20):
+                put(number, part, half, piece(part, number, border, half))
+            f = [piece(part, number, behind, half) for number in range(19)]
+            for i, number in enumerate(TOWARD_HIGH if up else TOWARD_LOW):
+                put(20 + i, part, half, f[number])
+            for i, value in enumerate(moments(f)[:4]):
+                put(25 + i, part, half, value)
+            put(29, part, half, piece(part, 19, behind, half))
+
+
+def layers_kernel(pops, mask, low_y, high_y, sums, to_far, to_mate):
     core = lax.axis_index("core")
-    def pack(out, first):
-        for layer in range(2):
-            x = first + layer
-            row = layer * ROWS
-            pair = slice(2 * x, 2 * x + 2)
-            for number in range(20):
-                for half, lanes in enumerate(halves):
-                    out[number, half, row : row + 2, :] = low_y[number, pair, lanes]
-                    if number < 19:
-                        block = pops[number, x, :, lanes]
-                    else:
-                        block = mask[x, :, lanes].astype(jnp.float32)
-                    out[number, half, row + 2 : row + 2 + NY, :] = block
-                    out[number, half, row + 2 + NY : row + ROWS, :] = high_y[number, pair, lanes]
-
-    @pl.when(core == 0)
-    def _():
-        pack(to_mate, NX - 2)
-        pack(to_far, 0)
-
-    @pl.when(core == 1)
-    def _():
-        pack(to_mate, 0)
-        pack(to_far, NX - 2)
-
+    for which in range(2):
+
+        @pl.when(core == which)
+        def _():
+            pack_layers(pops, mask, low_y, high_y, to_mate, which == 0)
+            pack_layers(pops, mask, low_y, high_y, to_far, which == 1)
+
+
+def sums_kernel(pops, mask, low_y, high_y, far_mask, mate_mask, sums, flags):
+    halves = HALVES
+    core = lax.axis_index("core")
     first_core = core == 0
-    low_x = jnp.where(first_core, far_mask[NX - 1], mate_mask[NX - 1]).astype(jnp.float32)
-    high_x = jnp.where(first_core, mate_mask[0], far_mask[0]).astype(jnp.float32)
+    low_x = jnp.where(first_core, far_mask[...], mate_mask[...])
+    high_x = jnp.where(first_core, mate_mask[...], far_mask[...])
     flags[...] = jnp.zeros_like(flags)
     for half, lanes in enumerate(halves):
         for x in range(NX):
@@ -253,8 +285,34 @@
     return result
 
 
-def steps_kernel(arrived, pops, mask, low_y, high_y, mate, far, out, post, later, flags):
-    halves = (slice(0, LANES), slice(LANES, 2 * LANES))
+def outer_layer(beside, at, side, half, shift, post):
+    core_rows = ((0, 8), (8, 8), (16, 4))
+    for start, size in core_rows:
+
+        def plane(number):
+            row = (number % 2) * ROWS + start
+            return beside[number // 2, half, row : row + size, :]
+
+        density, flux_x, flux_y, flux_z = [plane(25 + i) for i in range(4)]
+        fluid = plane(29)
+        toward = 1.0 - 2.0 * side.astype(jnp.float32)
+        inverse = 1.5 / (density + (1.0 - fluid))
+        ux = flux_x * inverse * toward
+        uy = flux_y * inverse + 1.5 * shift[:size]
+        uz = flux_z * inverse
+        base = 1.0 - (ux * ux + uy * uy + uz * uz) * (2.0 / 3.0)
+        scaled = density * (1.0 / RELAX)
+        for i, speed in enumerate((ux, ux + uy, ux - uy, ux + uz, ux - uz)):
+            weight = scaled * (1.0 / 18.0 if i == 0 else 1.0 / 36.0)
+            value = weight * (base + speed * (2.0 + 2.0 * speed)) - KEEP * plane(20 + i)
+            number = TOWARD_HIGH[i] + side * (TOWARD_LOW[i] - TOWARD_HIGH[i])
+            post[number, half, pl.ds(at + start, size), :] = jnp.where(fluid > 0.5, value, SOLID)
+
+
+def steps_kernel(
+    arrived, pops, mask, low_y, high_y, far, mate, out, post, later, flags, block, sems
+):
+    halves = HALVES
     sums = jnp.sum(arrived[...], axis=0)
 
     def total(i):
@@ -289,16 +347,22 @@
                     post[number, half, row : row + 2, :] = value[number][2 * x : 2 * x + 2]
     core = lax.axis_index("core")
     for beside, side in ((mate, 1 - core), (far, core)):
-        start = pl.multiple_of(FRONT + side * ((NX + 2) * ROWS), 8)
+        inner = FRONT + ROWS + side * ((NX + 1) * ROWS)
+        outer = FRONT + side * ((NX + 3) * ROWS)
         for half in range(2):
-            for tile in range(2 * ROWS // 8):
-                at = slice(8 * tile, 8 * tile + 8)
-                rows = pl.ds(start + 8 * tile, 8)
-                f = [beside[k, half, at, :] for k in range(19)]
-                fluid = beside[19, half, at, :]
+            for start, size in ((0, 8), (8, 8), (16, 4)):
+                rows = pl.ds(inner + start, size)
+
+                def plane(number):
+                    row = (number % 2) * ROWS + start
+                    return beside[number // 2, half, row : row + size, :]
+
+                f = [plane(number) for number in range(19)]
+                fluid = plane(19)
                 flags[half, rows, :] = fluid
-                for number, value in enumerate(collide(f, fluid, shift_1)):
+                for number, value in enumerate(collide(f, fluid, shift_1[:size])):
                     post[number, half, rows, :] = value
+            outer_layer(beside, outer, side, half, shift_1, post)
     for tile in range((NX + 2) * ROWS // 8):
         row = FRONT + ROWS + 8 * tile
         f = streamed(post, row, lane)
@@ -313,9 +377,12 @@
             for half, lanes in enumerate(halves):
                 open_site = flags[half, row : row + 8, :] > 0.5
                 for number in range(19):
-                    out[number, x, 8 * tile : 8 * tile + 8, lanes] = jnp.where(
+                    block[x, number, 8 * tile : 8 * tile + 8, lanes] = jnp.where(
                         open_site, f[half][number], 0.0
                     )
+        pltpu.make_async_copy(block.at[x], out.at[:, x], sems.at[x]).start()
+    for x in range(NX):
+        pltpu.make_async_copy(block.at[x], out.at[:, x], sems.at[x]).wait()
 
 
 def f32(*shape):
@@ -341,35 +408,52 @@
         pairs = [(i, i + step) for i in range(regions) if 0 <= i + step < regions]
         return lax.ppermute(value, "region", pairs)
 
+    def swapped(value, pairs):
+        return lax.ppermute(value, local, pairs + [(j, i) for i, j in pairs])
+
     def from_mate(value):
-        return lax.ppermute(value, "core", [(0, 1), (1, 0)])
+        return swapped(value, [(i, i + 1) for i in range(0, blocks - 1, 2)])
 
     def from_far(value):
-        ends = [(i, i + 1) for i in range(1, blocks - 1, 2)]
-        return lax.ppermute(value, local, ends + [(j, i) for i, j in ends])
+        return swapped(value, [(i, i + 1) for i in range(1, blocks - 1, 2)])
 
     def on_device(pops, mask):
-        mate_mask = from_mate(mask)
-        to_low_y, to_high_y = pl.pallas_call(
+        hbm = pl.BlockSpec(memory_space=pltpu.HBM)
+        pops, mask, to_low_y, to_high_y, to_far, to_mate = pl.pallas_call(
             pack_kernel,
-            out_shape=(f32(20, 8, 256), f32(20, 8, 256)),
+            out_shape=(
+                f32(19, NX, NY, 2 * LANES),
+                jax.ShapeDtypeStruct((NX, NY, 2 * LANES), jnp.int32),
+                f32(20, 8, 256),
+                f32(20, 8, 256),
+                f32(NY, 2 * LANES),
+                f32(NY, 2 * LANES),
+            ),
+            in_specs=[hbm, hbm],
+            scratch_shapes=[pltpu.SemaphoreType.DMA, pltpu.SemaphoreType.DMA],
             compiler_params=params(),
-        )(pops, mask)
+        )(
+            pltpu.with_memory_space_constraint(pops, pltpu.HBM),
+            pltpu.with_memory_space_constraint(mask, pltpu.HBM),
+        )
         low_y = shifted(to_high_y, 1)
         high_y = shifted(to_low_y, -1)
-        far_mask = from_far(mask)
-        sums, to_mate, to_far = pl.pallas_call(
+        far_mask = from_far(to_far)
+        mate_mask = from_mate(to_mate)
+        sums = pl.pallas_call(
             sums_kernel,
-            out_shape=(
-                f32(first, 1, LANES),
-                f32(20, 2, 2 * ROWS, LANES),
-                f32(20, 2, 2 * ROWS, LANES),
-            ),
+            out_shape=f32(first, 1, LANES),
             scratch_shapes=[pltpu.VMEM((2, FRONT + (NX + 2) * ROWS + 8, LANES), jnp.float32)],
             compiler_params=params(),
-        )(pops, mask, low_y, high_y, mate_mask, far_mask)
+        )(pops, mask, low_y, high_y, far_mask, mate_mask)
+        to_far, to_mate = pl.pallas_call(
+            layers_kernel,
+            out_shape=(f32(SLOTS, 2, 2 * ROWS, LANES), f32(SLOTS, 2, 2 * ROWS, LANES)),
+            in_specs=[pl.BlockSpec(memory_space=pltpu.VMEM)] * 4 + [pl.BlockSpec(memory_space=pl.ANY)],
+            compiler_params=params(),
+        )(pops, mask, low_y, high_y, sums)
+        far = from_far(to_far)
         mate = from_mate(to_mate)
-        far = from_far(to_far)
         sums = lax.all_to_all(sums, ("x", "y"), 0, 0, tiled=True)
         sums = pl.pallas_call(
             relay_kernel, out_shape=f32(second, 1, LANES), compiler_params=params()
@@ -378,14 +462,17 @@
         rows = FRONT + (NX + 4) * ROWS + 8
         return pl.pallas_call(
             steps_kernel,
-            out_shape=f32(19, NX, NY, 2 * LANES),
+            out_shape=pltpu.HBM((19, NX, NY, 2 * LANES), jnp.float32),
+            out_specs=hbm,
             scratch_shapes=[
                 pltpu.VMEM((19, 2, rows, LANES), jnp.float32),
                 pltpu.VMEM((19, 2, rows, LANES), jnp.float32),
                 pltpu.VMEM((2, rows, LANES), jnp.float32),
+                pltpu.VMEM((NX, 19, NY, 2 * LANES), jnp.float32),
+                pltpu.SemaphoreType.DMA((NX,)),
             ],
             compiler_params=params(),
-        )(sums, pops, mask, low_y, high_y, mate, far)
+        )(sums, pops, mask, low_y, high_y, far, mate)
 
     return jax.shard_map(
         on_device,

time: 70.8 us -> 69.3 us (0.979)
  local copies, waits for them, and re-layouts: 2.14 us -> 0 us
  starting transfers between devices: 22.1 us -> 20.8 us
  Pallas kernels: 4.77 us -> 5.79 us
  blocking collectives: 40.5 us -> 41.5 us
    unnamed x6 -> x0, local copies, waits for them, and re-layouts: 2.14 us -> none
    all_to_all x1, blocking collectives: 13.3 us -> 15.3 us  [on_device(): sums = lax.all_to_all(sums, ('x', 'y'), 0, 0, tiled=True)]
    ppermute x4, starting transfers between devices: 15.8 us -> 14.7 us  [swapped(): return lax.ppermute(value, local, pairs + [(j, i) for i, j in pairs])]
    pallas_call x3 -> x4, Pallas kernels: 4.73 us -> 5.75 us  [the longest x1 3.26 us: on_device(): pl.pallas_call(steps_kernel, out_shape=pltpu.HBM((19, NX, NY, 2 * LANES),...]
    all_to_all x1, blocking collectives: 27.1 us -> 26.1 us  [on_device(): sums = lax.all_to_all(sums, ('region', 'core'), 0, 0, tiled=True)]
where the time goes in v4:
time: 69.3 us; the launch traced here: 68.9 us
  blocking collectives  41.5 us (60%)
  starting transfers between devices  20.8 us (30%)
  Pallas kernels  5.79 us (8%)
  waiting for transfers between devices  0.82 us (1%)
    all_to_all x1, blocking collectives, on_device(): sums = lax.all_to_all(sums, ('region', 'core'), 0, 0, tiled=True)  26.1 us
    all_to_all x1, blocking collectives, on_device(): sums = lax.all_to_all(sums, ('x', 'y'), 0, 0, tiled=True)  15.3 us
    ppermute x4, starting transfers between devices, swapped(): return lax.ppermute(value, local, pairs + [(j, i) for i, j in pairs])  14.7 us
    ppermute x2, starting transfers between devices, shifted(): return lax.ppermute(value, 'region', pairs)  6.13 us
    pallas_call x1, Pallas kernels, on_device(): pl.pallas_call(steps_kernel, out_shape=pltpu.HBM((19, NX, NY, 2 * LANES),...  3.26 us
    pallas_call x1, Pallas kernels, on_device(): pl.pallas_call(pack_kernel, out_shape=(f32(19, NX, NY, 2 * LANES), jax.Sh...  1.44 us
  transfers between devices with their start and end apart: 6, of which 1 were waited for; matrix products, arithmetic and copies ran while one was open for 0% of the time, Pallas kernels for 0%

profile of v4, /device:TPU:1, one launch (start us, length us, event | category | flops | bytes accessed | tf_op | source)
XLA Modules:
  0.0 68.9 jit_solution(15511634534342176008)
XLA Ops:
  0.0 1.4 %shard_map.28 = (f32[19,4,16,256]{3,2,1,0:T(8,128)S(1)}, s32[4,16,256]{2,1,0:T(8,128)S(1)}, f32[20,8,256]{2,1,0:T(8,128)S(1)}, f32[20,8,256]{2,1,0:T(8,128)S(1)}...) custom-call(f32[19,4,16,256]{3,2,1,0:T(8,128)} %pops_in.1, s32[4,16,256]{2,1,0:T(8,128)} %mask_in.1), custom_call_target="tpu_custom_call" | custom-call | tf_op jit(solution)/shard_map/pallas_call | solution.py:422
  1.5 4.8 %collective-permute-start = (f32[20,8,256]{2,1,0:T(8,128)S(1)}, f32[20,8,256]{2,1,0:T(8,128)S(1)}, u32[]{:S(2)}, u32[]{:S(2)}) collective-permute-start(f32[20,8,256]{2,1,0:T(8,128)S(1)} %get-tuple-element.15), channel_id=1, source_target_pairs={{0,64},{64,128},{128,192},{192,256},{256,320},{320,384},{384,448},... | collective-permute-start | bytes 491528 | tf_op jit(solution)/shard_map/ppermute | solution.py:409
  6.3 1.3 %collective-permute-start.1 = (f32[20,8,256]{2,1,0:T(8,128)S(1)}, f32[20,8,256]{2,1,0:T(8,128)S(1)}, u32[]{:S(2)}, u32[]{:S(2)}) collective-permute-start(f32[20,8,256]{2,1,0:T(8,128)S(1)} %get-tuple-element.16), channel_id=1, source_target_pairs={{64,0},{128,64},{192,128},{256,192},{320,256},{384,320},{448,384},... | collective-permute-start | bytes 491528 | tf_op jit(solution)/shard_map/ppermute | solution.py:409
  7.6 4.0 %collective-permute-start.2 = (f32[16,256]{1,0:T(8,128)S(1)}, f32[16,256]{1,0:T(8,128)S(1)}, u32[]{:S(2)}, u32[]{:S(2)}) collective-permute-start(f32[16,256]{1,0:T(8,128)S(1)} %get-tuple-element.17), channel_id=1, source_target_pairs={{1,2},{3,4},{5,6},{7,8},{9,10},{11,12},{13,14},{15,16},{17,18},{19... | collective-permute-start | bytes 49160 | tf_op jit(solution)/shard_map/ppermute | solution.py:412
  11.6 5.5 %collective-permute-start.3 = (f32[16,256]{1,0:T(8,128)S(1)}, f32[16,256]{1,0:T(8,128)S(1)}, u32[]{:S(2)}, u32[]{:S(2)}) collective-permute-start(f32[16,256]{1,0:T(8,128)S(1)} %get-tuple-element.18), channel_id=1, source_target_pairs={{0,1},{2,3},{4,5},{6,7},{8,9},{10,11},{12,13},{14,15},{16,17},{18,... | collective-permute-start | bytes 49160 | tf_op jit(solution)/shard_map/ppermute | solution.py:412
  17.2 0.0 collective-permute-done.2.far_mask
  17.2 0.8 %collective-permute-done.3.mate_mask = f32[16,256]{1,0:T(8,128)S(1)} collective-permute-done((f32[16,256]{1,0:T(8,128)S(1)}, f32[16,256]{1,0:T(8,128)S(1)}, u32[]{:S(2)}, u32[]{:S(2)}) %collective-permute-start.3) | collective-permute-done | bytes 16416 | tf_op jit(solution)/shard_map/ppermute | solution.py:412
  18.0 0.0 collective-permute-done.low_y
  18.0 0.0 collective-permute-done.1.high_y
  18.0 0.8 %shard_map.29.sums = f32[32,1,128]{2,1,0:T(1,128)S(1)} custom-call(f32[19,4,16,256]{3,2,1,0:T(8,128)S(1)} %get-tuple-element.13.pops, s32[4,16,256]{2,1,0:T(8,128)S(1)} %get-tuple-element.14.mask, f32[20,8,256]{2,1,0:T(8,128)S(1)} %collective-permute-done.low_y, f32[20,8,256]{2,1,0:T(8,128)S(1)} %collective-permute-done.1.high_y, ...), custom_call_target="tpu_custom_call" | custom-call | tf_op jit(solution)/shard_map/pallas_call | solution.py:443
  18.8 0.2 shard_map.31
  19.0 1.9 %collective-permute-start.4 = (f32[15,2,40,128]{3,2,1,0:T(8,128)S(1)}, f32[15,2,40,128]{3,2,1,0:T(8,128)S(1)}, u32[]{:S(2)}, u32[]{:S(2)}) collective-permute-start(f32[15,2,40,128]{3,2,1,0:T(8,128)S(1)} %get-tuple-element.19), channel_id=1, source_target_pairs={{1,2},{3,4},{5,6},{7,8},{9,10},{11,12},{13,14},{15,16},{17,18},{19... | collective-permute-start | bytes 1843208 | tf_op jit(solution)/shard_map/ppermute | solution.py:412
  21.0 3.2 %collective-permute-start.5 = (f32[15,2,40,128]{3,2,1,0:T(8,128)S(1)}, f32[15,2,40,128]{3,2,1,0:T(8,128)S(1)}, u32[]{:S(2)}, u32[]{:S(2)}) collective-permute-start(f32[15,2,40,128]{3,2,1,0:T(8,128)S(1)} %get-tuple-element.20), channel_id=1, source_target_pairs={{0,1},{2,3},{4,5},{6,7},{8,9},{10,11},{12,13},{14,15},{16,17},{18,... | collective-permute-start | bytes 1843208 | tf_op jit(solution)/shard_map/ppermute | solution.py:412
  24.2 15.3 %all_to_all.10.arrived = f32[32,1,128]{2,1,0:T(1,128)S(1)} all-to-all(f32[32,1,128]{2,1,0:T(1,128)S(1)} %shard_map.29.sums), channel_id=1, replica_groups=mesh['region'=12,'x'=4,'y'=8,'core'=2] {'x','y'}, dimensions={0} | all-to-all | bytes 32768 | tf_op jit(solution)/shard_map/all_to_all | solution.py:457
  39.6 26.1 %all_to_all.11.arrived = f32[24,1,128]{2,1,0:T(1,128)S(1)} all-to-all(f32[24,1,128]{2,1,0:T(1,128)S(1)} %shard_map.30), channel_id=1, replica_groups=mesh['region'=12,'x'=4,'y'=8,'core'=2] {'region','core'}, dimensions={0} | all-to-all | bytes 24576 | tf_op jit(solution)/shard_map/all_to_all | solution.py:461
  65.7 0.0 collective-permute-done.4.far
  65.7 0.0 collective-permute-done.5.mate
  65.7 3.3 %shard_map.32 = f32[19,4,16,256]{3,2,1,0:T(8,128)} custom-call(f32[24,1,128]{2,1,0:T(1,128)S(1)} %all_to_all.11.arrived, f32[19,4,16,256]{3,2,1,0:T(8,128)S(1)} %get-tuple-element.13.pops, s32[4,16,256]{2,1,0:T(8,128)S(1)} %get-tuple-element.14.mask, f32[20,8,256]{2,1,0:T(8,128)S(1)} %collective-permute-done.low_y, ...), custom_call_target="tpu_custom_call" | custom-call | tf_op jit(solution)/shard_map/pallas_call | solution.py:463
  (1 shorter events, 0.0 us)
Async XLA Ops:
  1.5 16.5 %collective-permute-start = (f32[20,8,256]{2,1,0:T(8,128)S(1)}, f32[20,8,256]{2,1,0:T(8,128)S(1)}, u32[]{:S(2)}, u32[]{:S(2)}) collective-permute-start(f32[20,8,256]{2,1,0:T(8,128)S(1)} %get-tuple-element.15), channel_id=1, source_target_pairs={{0,64},{64,128},{128,192},{192,256},{256,320},{320,384},{384,448},... | collective-permute-start | bytes 491528 | tf_op jit(solution)/shard_map/ppermute | solution.py:409
  6.3 11.7 %collective-permute-start.1 = (f32[20,8,256]{2,1,0:T(8,128)S(1)}, f32[20,8,256]{2,1,0:T(8,128)S(1)}, u32[]{:S(2)}, u32[]{:S(2)}) collective-permute-start(f32[20,8,256]{2,1,0:T(8,128)S(1)} %get-tuple-element.16), channel_id=1, source_target_pairs={{64,0},{128,64},{192,128},{256,192},{320,256},{384,320},{448,384},... | collective-permute-start | bytes 491528 | tf_op jit(solution)/shard_map/ppermute | solution.py:409
  7.6 9.6 %collective-permute-start.2 = (f32[16,256]{1,0:T(8,128)S(1)}, f32[16,256]{1,0:T(8,128)S(1)}, u32[]{:S(2)}, u32[]{:S(2)}) collective-permute-start(f32[16,256]{1,0:T(8,128)S(1)} %get-tuple-element.17), channel_id=1, source_target_pairs={{1,2},{3,4},{5,6},{7,8},{9,10},{11,12},{13,14},{15,16},{17,18},{19... | collective-permute-start | bytes 49160 | tf_op jit(solution)/shard_map/ppermute | solution.py:412
  11.6 6.3 %collective-permute-start.3 = (f32[16,256]{1,0:T(8,128)S(1)}, f32[16,256]{1,0:T(8,128)S(1)}, u32[]{:S(2)}, u32[]{:S(2)}) collective-permute-start(f32[16,256]{1,0:T(8,128)S(1)} %get-tuple-element.18), channel_id=1, source_target_pairs={{0,1},{2,3},{4,5},{6,7},{8,9},{10,11},{12,13},{14,15},{16,17},{18,... | collective-permute-start | bytes 49160 | tf_op jit(solution)/shard_map/ppermute | solution.py:412
  19.0 46.6 %collective-permute-start.4 = (f32[15,2,40,128]{3,2,1,0:T(8,128)S(1)}, f32[15,2,40,128]{3,2,1,0:T(8,128)S(1)}, u32[]{:S(2)}, u32[]{:S(2)}) collective-permute-start(f32[15,2,40,128]{3,2,1,0:T(8,128)S(1)} %get-tuple-element.19), channel_id=1, source_target_pairs={{1,2},{3,4},{5,6},{7,8},{9,10},{11,12},{13,14},{15,16},{17,18},{19... | collective-permute-start | bytes 1843208 | tf_op jit(solution)/shard_map/ppermute | solution.py:412
  21.0 44.7 %collective-permute-start.5 = (f32[15,2,40,128]{3,2,1,0:T(8,128)S(1)}, f32[15,2,40,128]{3,2,1,0:T(8,128)S(1)}, u32[]{:S(2)}, u32[]{:S(2)}) collective-permute-start(f32[15,2,40,128]{3,2,1,0:T(8,128)S(1)} %get-tuple-element.20), channel_id=1, source_target_pairs={{0,1},{2,3},{4,5},{6,7},{8,9},{10,11},{12,13},{14,15},{16,17},{18,... | collective-permute-start | bytes 1843208 | tf_op jit(solution)/shard_map/ppermute | solution.py:412

commit v5 on v4

--- a/solution.py
+++ b/solution.py
@@ -309,6 +309,18 @@
             post[number, half, pl.ds(at + start, size), :] = jnp.where(fluid > 0.5, value, SOLID)
 
 
+def last_streaming(later, flags, block, x, lane):
+    for tile in range(NY // 8):
+        row = FRONT + (x + 2) * ROWS + 2 + 8 * tile
+        f = streamed(later, row, lane)
+        for half, lanes in enumerate(HALVES):
+            open_site = flags[half, row : row + 8, :] > 0.5
+            for number in range(19):
+                block[x, number, 8 * tile : 8 * tile + 8, lanes] = jnp.where(
+                    open_site, f[half][number], 0.0
+                )
+
+
 def steps_kernel(
     arrived, pops, mask, low_y, high_y, far, mate, out, post, later, flags, block, sems
 ):
@@ -363,6 +375,7 @@
                 for number, value in enumerate(collide(f, fluid, shift_1[:size])):
                     post[number, half, rows, :] = value
             outer_layer(beside, outer, side, half, shift_1, post)
+    done = 0
     for tile in range((NX + 2) * ROWS // 8):
         row = FRONT + ROWS + 8 * tile
         f = streamed(post, row, lane)
@@ -370,17 +383,10 @@
             fluid = flags[half, row : row + 8, :]
             for number, value in enumerate(collide(f[half], fluid, shift_2)):
                 later[number, half, row : row + 8, :] = value
-    for x in range(NX):
-        for tile in range(NY // 8):
-            row = FRONT + (x + 2) * ROWS + 2 + 8 * tile
-            f = streamed(later, row, lane)
-            for half, lanes in enumerate(halves):
-                open_site = flags[half, row : row + 8, :] > 0.5
-                for number in range(19):
-                    block[x, number, 8 * tile : 8 * tile + 8, lanes] = jnp.where(
-                        open_site, f[half][number], 0.0
-                    )
-        pltpu.make_async_copy(block.at[x], out.at[:, x], sems.at[x]).start()
+        while done < NX and row + 8 >= FRONT + (done + 4) * ROWS:
+            last_streaming(later, flags, block, done, lane)
+            pltpu.make_async_copy(block.at[done], out.at[:, done], sems.at[done]).start()
+            done += 1
     for x in range(NX):
         pltpu.make_async_copy(block.at[x], out.at[:, x], sems.at[x]).wait()
 
@@ -456,7 +462,10 @@
         mate = from_mate(to_mate)
         sums = lax.all_to_all(sums, ("x", "y"), 0, 0, tiled=True)
         sums = pl.pallas_call(
-            relay_kernel, out_shape=f32(second, 1, LANES), compiler_params=params()
+            relay_kernel,
+            out_shape=f32(second, 1, LANES),
+            compiler_params=params(),
+            cost_estimate=pl.CostEstimate(flops=3 * 10**10, bytes_accessed=0, transcendentals=0),
         )(sums)
         sums = lax.all_to_all(sums, ("region", "core"), 0, 0, tiled=True)
         rows = FRONT + (NX + 4) * ROWS + 8

time: 69.3 us -> 64.3 us (0.928)
  blocking collectives: 41.5 us -> 27.1 us
  starting transfers between devices: 20.8 us -> 28.3 us
  Pallas kernels: 5.79 us -> 7.19 us
    all_to_all x1 -> x0, blocking collectives: 15.3 us -> none  [on_device(): sums = lax.all_to_all(sums, ('x', 'y'), 0, 0, tiled=True)]
    all_to_all x0 -> x1, starting transfers between devices: none -> 5.58 us  [on_device(): sums = lax.all_to_all(sums, ('x', 'y'), 0, 0, tiled=True)]
    ppermute x4, starting transfers between devices: 14.7 us -> 16.6 us  [swapped(): return lax.ppermute(value, local, pairs + [(j, i) for i, j in pairs])]
    all_to_all x1, blocking collectives: 26.1 us -> 27.1 us  [on_device(): sums = lax.all_to_all(sums, ('region', 'core'), 0, 0, tiled=True)]
    pallas_call x1, Pallas kernels: 0.21 us -> 1.04 us  [on_device(): pl.pallas_call(layers_kernel, out_shape=(f32(SLOTS, 2, 2 * ROWS, LANES),...]
  transfers between devices with their start and end apart: 6 -> 7, of which waited for: 1 -> 2; matrix products, arithmetic and copies ran while one was open for 0% -> 0% of each run, Pallas kernels for 0% -> 2%
where the time goes in v5:
time: 64.3 us; the launch traced here: 64 us
  starting transfers between devices  28.3 us (44%)
  blocking collectives  27.1 us (42%)
  Pallas kernels  7.19 us (11%)
  waiting for transfers between devices  1.35 us (2%)
    all_to_all x1, blocking collectives, on_device(): sums = lax.all_to_all(sums, ('region', 'core'), 0, 0, tiled=True)  27.1 us
    ppermute x4, starting transfers between devices, swapped(): return lax.ppermute(value, local, pairs + [(j, i) for i, j in pairs])  16.6 us
    ppermute x2, starting transfers between devices, shifted(): return lax.ppermute(value, 'region', pairs)  6.13 us
    all_to_all x1, starting transfers between devices, on_device(): sums = lax.all_to_all(sums, ('x', 'y'), 0, 0, tiled=True)  5.58 us
    pallas_call x1, Pallas kernels, on_device(): pl.pallas_call(steps_kernel, out_shape=pltpu.HBM((19, NX, NY, 2 * LANES),...  3.25 us
    pallas_call x1, Pallas kernels, on_device(): pl.pallas_call(pack_kernel, out_shape=(f32(19, NX, NY, 2 * LANES), jax.Sh...  1.44 us
    pallas_call x1, Pallas kernels, on_device(): pl.pallas_call(sums_kernel, out_shape=f32(first, 1, LANES), scratch_shape...  1.42 us
  transfers between devices with their start and end apart: 7, of which 2 were waited for; matrix products, arithmetic and copies ran while one was open for 0% of the time, Pallas kernels for 2%

profile of v5, /device:TPU:1, one launch (start us, length us, event | category | flops | bytes accessed | tf_op | source)
XLA Modules:
  0.0 64.0 jit_solution(10465613657263984452)
XLA Ops:
  0.0 1.4 %shard_map.28 = (f32[19,4,16,256]{3,2,1,0:T(8,128)S(1)}, s32[4,16,256]{2,1,0:T(8,128)S(1)}, f32[20,8,256]{2,1,0:T(8,128)S(1)}, f32[20,8,256]{2,1,0:T(8,128)S(1)}...) custom-call(f32[19,4,16,256]{3,2,1,0:T(8,128)} %pops_in.1, s32[4,16,256]{2,1,0:T(8,128)} %mask_in.1), custom_call_target="tpu_custom_call" | custom-call | tf_op jit(solution)/shard_map/pallas_call | solution.py:428
  1.5 4.8 %collective-permute-start = (f32[20,8,256]{2,1,0:T(8,128)S(1)}, f32[20,8,256]{2,1,0:T(8,128)S(1)}, u32[]{:S(2)}, u32[]{:S(2)}) collective-permute-start(f32[20,8,256]{2,1,0:T(8,128)S(1)} %get-tuple-element.15), channel_id=1, source_target_pairs={{0,64},{64,128},{128,192},{192,256},{256,320},{320,384},{384,448},... | collective-permute-start | bytes 491528 | tf_op jit(solution)/shard_map/ppermute | solution.py:415
  6.3 1.3 %collective-permute-start.1 = (f32[20,8,256]{2,1,0:T(8,128)S(1)}, f32[20,8,256]{2,1,0:T(8,128)S(1)}, u32[]{:S(2)}, u32[]{:S(2)}) collective-permute-start(f32[20,8,256]{2,1,0:T(8,128)S(1)} %get-tuple-element.16), channel_id=1, source_target_pairs={{64,0},{128,64},{192,128},{256,192},{320,256},{384,320},{448,384},... | collective-permute-start | bytes 491528 | tf_op jit(solution)/shard_map/ppermute | solution.py:415
  7.6 4.0 %collective-permute-start.2 = (f32[16,256]{1,0:T(8,128)S(1)}, f32[16,256]{1,0:T(8,128)S(1)}, u32[]{:S(2)}, u32[]{:S(2)}) collective-permute-start(f32[16,256]{1,0:T(8,128)S(1)} %get-tuple-element.17), channel_id=1, source_target_pairs={{1,2},{3,4},{5,6},{7,8},{9,10},{11,12},{13,14},{15,16},{17,18},{19... | collective-permute-start | bytes 49160 | tf_op jit(solution)/shard_map/ppermute | solution.py:418
  11.6 5.5 %collective-permute-start.3 = (f32[16,256]{1,0:T(8,128)S(1)}, f32[16,256]{1,0:T(8,128)S(1)}, u32[]{:S(2)}, u32[]{:S(2)}) collective-permute-start(f32[16,256]{1,0:T(8,128)S(1)} %get-tuple-element.18), channel_id=1, source_target_pairs={{0,1},{2,3},{4,5},{6,7},{8,9},{10,11},{12,13},{14,15},{16,17},{18,... | collective-permute-start | bytes 49160 | tf_op jit(solution)/shard_map/ppermute | solution.py:418
  17.2 0.0 collective-permute-done.2.far_mask
  17.2 0.8 %collective-permute-done.3.mate_mask = f32[16,256]{1,0:T(8,128)S(1)} collective-permute-done((f32[16,256]{1,0:T(8,128)S(1)}, f32[16,256]{1,0:T(8,128)S(1)}, u32[]{:S(2)}, u32[]{:S(2)}) %collective-permute-start.3) | collective-permute-done | bytes 16416 | tf_op jit(solution)/shard_map/ppermute | solution.py:418
  18.0 0.0 collective-permute-done.low_y
  18.0 0.0 collective-permute-done.1.high_y
  18.0 1.4 %shard_map.29.sums = f32[32,1,128]{2,1,0:T(1,128)} custom-call(f32[19,4,16,256]{3,2,1,0:T(8,128)S(1)} %get-tuple-element.13.pops, s32[4,16,256]{2,1,0:T(8,128)S(1)} %get-tuple-element.14.mask, f32[20,8,256]{2,1,0:T(8,128)S(1)} %collective-permute-done.low_y, f32[20,8,256]{2,1,0:T(8,128)S(1)} %collective-permute-done.1.high_y, ...), custom_call_target="tpu_custom_call" | custom-call | tf_op jit(solution)/shard_map/pallas_call | solution.py:449
  19.4 5.6 %all-to-all-start = ((f32[32,1,128]{2,1,0:T(1,128)}), f32[32,1,128]{2,1,0:T(1,128)S(1)}, u32[]{:S(2)}, u32[]{:S(2)}) async-start(f32[32,1,128]{2,1,0:T(1,128)} %shard_map.29.sums), calls=%async_computation | async-start | bytes 32768 | tf_op jit(solution)/shard_map/all_to_all | solution.py:463
  25.0 1.0 %shard_map.31 = (f32[15,2,40,128]{3,2,1,0:T(8,128)}, f32[15,2,40,128]{3,2,1,0:T(8,128)S(1)}) custom-call(f32[19,4,16,256]{3,2,1,0:T(8,128)S(1)} %get-tuple-element.13.pops, s32[4,16,256]{2,1,0:T(8,128)S(1)} %get-tuple-element.14.mask, f32[20,8,256]{2,1,0:T(8,128)S(1)} %collective-permute-done.low_y, f32[20,8,256]{2,1,0:T(8,128)S(1)} %collective-permute-done.1.high_y, ...), custom_call_target="tpu_custom_call" | custom-call | tf_op jit(solution)/shard_map/pallas_call | solution.py:455
  26.0 5.1 %collective-permute-start.4 = (f32[15,2,40,128]{3,2,1,0:T(8,128)}, f32[15,2,40,128]{3,2,1,0:T(8,128)S(1)}, u32[]{:S(2)}, u32[]{:S(2)}) collective-permute-start(f32[15,2,40,128]{3,2,1,0:T(8,128)} %get-tuple-element.19), channel_id=1, source_target_pairs={{1,2},{3,4},{5,6},{7,8},{9,10},{11,12},{13,14},{15,16},{17,18},{19... | collective-permute-start | bytes 1843208 | tf_op jit(solution)/shard_map/ppermute | solution.py:418
  31.1 1.9 %collective-permute-start.5 = (f32[15,2,40,128]{3,2,1,0:T(8,128)S(1)}, f32[15,2,40,128]{3,2,1,0:T(8,128)S(1)}, u32[]{:S(2)}, u32[]{:S(2)}) collective-permute-start(f32[15,2,40,128]{3,2,1,0:T(8,128)S(1)} %get-tuple-element.20), channel_id=1, source_target_pairs={{0,1},{2,3},{4,5},{6,7},{8,9},{10,11},{12,13},{14,15},{16,17},{18,... | collective-permute-start | bytes 1843208 | tf_op jit(solution)/shard_map/ppermute | solution.py:418
  33.1 0.5 all-to-all-done.arrived
  33.7 27.1 %all_to_all.10.arrived = f32[24,1,128]{2,1,0:T(1,128)S(1)} all-to-all(f32[24,1,128]{2,1,0:T(1,128)S(1)} %shard_map.30), channel_id=1, replica_groups=mesh['region'=12,'x'=4,'y'=8,'core'=2] {'region','core'}, dimensions={0} | all-to-all | bytes 24576 | tf_op jit(solution)/shard_map/all_to_all | solution.py:470
  60.7 0.0 collective-permute-done.4.far
  60.7 0.0 collective-permute-done.5.mate
  60.7 3.2 %shard_map.32 = f32[19,4,16,256]{3,2,1,0:T(8,128)} custom-call(f32[24,1,128]{2,1,0:T(1,128)S(1)} %all_to_all.10.arrived, f32[19,4,16,256]{3,2,1,0:T(8,128)S(1)} %get-tuple-element.13.pops, s32[4,16,256]{2,1,0:T(8,128)S(1)} %get-tuple-element.14.mask, f32[20,8,256]{2,1,0:T(8,128)S(1)} %collective-permute-done.low_y, ...), custom_call_target="tpu_custom_call" | custom-call | tf_op jit(solution)/shard_map/pallas_call | solution.py:472
  (1 shorter events, 0.0 us)
Async XLA Ops:
  1.5 16.5 %collective-permute-start = (f32[20,8,256]{2,1,0:T(8,128)S(1)}, f32[20,8,256]{2,1,0:T(8,128)S(1)}, u32[]{:S(2)}, u32[]{:S(2)}) collective-permute-start(f32[20,8,256]{2,1,0:T(8,128)S(1)} %get-tuple-element.15), channel_id=1, source_target_pairs={{0,64},{64,128},{128,192},{192,256},{256,320},{320,384},{384,448},... | collective-permute-start | bytes 491528 | tf_op jit(solution)/shard_map/ppermute | solution.py:415
  6.3 11.7 %collective-permute-start.1 = (f32[20,8,256]{2,1,0:T(8,128)S(1)}, f32[20,8,256]{2,1,0:T(8,128)S(1)}, u32[]{:S(2)}, u32[]{:S(2)}) collective-permute-start(f32[20,8,256]{2,1,0:T(8,128)S(1)} %get-tuple-element.16), channel_id=1, source_target_pairs={{64,0},{128,64},{192,128},{256,192},{320,256},{384,320},{448,384},... | collective-permute-start | bytes 491528 | tf_op jit(solution)/shard_map/ppermute | solution.py:415
  7.6 9.6 %collective-permute-start.2 = (f32[16,256]{1,0:T(8,128)S(1)}, f32[16,256]{1,0:T(8,128)S(1)}, u32[]{:S(2)}, u32[]{:S(2)}) collective-permute-start(f32[16,256]{1,0:T(8,128)S(1)} %get-tuple-element.17), channel_id=1, source_target_pairs={{1,2},{3,4},{5,6},{7,8},{9,10},{11,12},{13,14},{15,16},{17,18},{19... | collective-permute-start | bytes 49160 | tf_op jit(solution)/shard_map/ppermute | solution.py:418
  11.6 6.3 %collective-permute-start.3 = (f32[16,256]{1,0:T(8,128)S(1)}, f32[16,256]{1,0:T(8,128)S(1)}, u32[]{:S(2)}, u32[]{:S(2)}) collective-permute-start(f32[16,256]{1,0:T(8,128)S(1)} %get-tuple-element.18), channel_id=1, source_target_pairs={{0,1},{2,3},{4,5},{6,7},{8,9},{10,11},{12,13},{14,15},{16,17},{18,... | collective-permute-start | bytes 49160 | tf_op jit(solution)/shard_map/ppermute | solution.py:418
  19.4 14.2 %all-to-all-start = ((f32[32,1,128]{2,1,0:T(1,128)}), f32[32,1,128]{2,1,0:T(1,128)S(1)}, u32[]{:S(2)}, u32[]{:S(2)}) async-start(f32[32,1,128]{2,1,0:T(1,128)} %shard_map.29.sums), calls=%async_computation | async-start | bytes 32768 | tf_op jit(solution)/shard_map/all_to_all | solution.py:463
  26.0 34.7 %collective-permute-start.4 = (f32[15,2,40,128]{3,2,1,0:T(8,128)}, f32[15,2,40,128]{3,2,1,0:T(8,128)S(1)}, u32[]{:S(2)}, u32[]{:S(2)}) collective-permute-start(f32[15,2,40,128]{3,2,1,0:T(8,128)} %get-tuple-element.19), channel_id=1, source_target_pairs={{1,2},{3,4},{5,6},{7,8},{9,10},{11,12},{13,14},{15,16},{17,18},{19... | collective-permute-start | bytes 1843208 | tf_op jit(solution)/shard_map/ppermute | solution.py:418
  31.1 29.6 %collective-permute-start.5 = (f32[15,2,40,128]{3,2,1,0:T(8,128)S(1)}, f32[15,2,40,128]{3,2,1,0:T(8,128)S(1)}, u32[]{:S(2)}, u32[]{:S(2)}) collective-permute-start(f32[15,2,40,128]{3,2,1,0:T(8,128)S(1)} %get-tuple-element.20), channel_id=1, source_target_pairs={{0,1},{2,3},{4,5},{6,7},{8,9},{10,11},{12,13},{14,15},{16,17},{18,... | collective-permute-start | bytes 1843208 | tf_op jit(solution)/shard_map/ppermute | solution.py:418

commit v6 on v5

--- a/solution.py
+++ b/solution.py
@@ -42,6 +42,9 @@
 HALVES = (slice(0, LANES), slice(LANES, 2 * LANES))
 TOWARD_HIGH = (1, 7, 9, 11, 13)
 TOWARD_LOW = (2, 10, 8, 14, 12)
+UPWARD = (3, 7, 10, 15, 17)
+DOWNWARD = (4, 9, 8, 18, 16)
+SPARE = (0, 1, 2, 5)
 SLOTS = 15
 
 
@@ -72,14 +75,13 @@
     uz = flux_z * inverse
     square = ux * ux + uy * uy + uz * uz
     base = 1.0 - square * (2.0 / 3.0)
-    scaled = density * (1.0 / RELAX)
     open_site = fluid > 0.5
+    scaled = jnp.where(open_site, density * (1.0 / RELAX), 0.0)
     weight = (scaled * (1.0 / 3.0), scaled * (1.0 / 18.0), scaled * (1.0 / 36.0))
-    base_1 = weight[1] * base
-    base_2 = weight[2] * base
+    base_0, base_1, base_2 = (jnp.where(open_site, w * base, SOLID) for w in weight)
     twice_1 = weight[1] * 2.0
     twice_2 = weight[2] * 2.0
-    post = [jnp.where(open_site, weight[0] * base - KEEP * f[0], SOLID)]
+    post = [base_0 - KEEP * f[0]]
     along = (None, ux, uy, uz, ux + uy, ux - uy, ux + uz, ux - uz, uy + uz, uy - uz)
     for pair in range(1, 10):
         speed = along[pair]
@@ -87,8 +89,8 @@
         even = (base_1 if pair <= 3 else base_2) + odd * speed
         even = even - (0.5 * KEEP) * total[pair]
         odd = odd - (0.5 * KEEP) * diff[pair]
-        post.append(jnp.where(open_site, even + odd, SOLID))
-        post.append(jnp.where(open_site, even - odd, SOLID))
+        post.append(even + odd)
+        post.append(even - odd)
     return post
 
 
@@ -125,48 +127,74 @@
     mask_copy.start()
     mask_copy.wait()
     core = lax.axis_index("core")
-    for x in range(NX):
-        rows = slice(2 * x, 2 * x + 2)
-        to_low_y[19, rows, :] = mask[x, 0:2, :].astype(jnp.float32)
-        to_high_y[19, rows, :] = mask[x, NY - 2 : NY, :].astype(jnp.float32)
-
     to_mate[...] = mask[(1 - core) * (NX - 1)].astype(jnp.float32)
     to_far[...] = mask[core * (NX - 1)].astype(jnp.float32)
     pops_copy.wait()
-    for x in range(NX):
-        rows = slice(2 * x, 2 * x + 2)
-        for number in range(19):
-            to_low_y[number, rows, :] = pops[number, x, 0:2, :]
-            to_high_y[number, rows, :] = pops[number, x, NY - 2 : NY, :]
+    for out, border, behind, numbers in (
+        (to_low_y, 0, 1, DOWNWARD),
+        (to_high_y, NY - 1, NY - 2, UPWARD),
+    ):
+        for x in range(NX):
+            f = [pops[number, x, behind : behind + 1, :] for number in range(19)]
+            planes = [pops[number, x, border : border + 1, :] for number in range(19)]
+            planes.append(mask[x, border : border + 1, :].astype(jnp.float32))
+            planes += [f[number] for number in numbers]
+            planes += list(moments(f)[:4])
+            planes.append(mask[x, behind : behind + 1, :].astype(jnp.float32))
+            for i, value in enumerate(planes):
+                row = NX * (i % 2) + x
+                out[i // 2, row : row + 1, :] = value
+
+
+def y_plane(beside, plane, lanes, x=None):
+    first = NX * (plane % 2)
+    if x is None:
+        return beside[plane // 2, first : first + NX, lanes]
+    return beside[plane // 2, first + x : first + x + 1, lanes]
 
 
 def pack_layers(pops, mask, low_y, high_y, out, up):
-    pieces = ((low_y, 0, 2), (None, 2, 8), (None, 10, 8), (high_y, 2 + NY, 2))
-
-    def piece(part, number, x, half):
-        beside, start, size = part
-        lanes = HALVES[half]
-        if beside is not None:
-            return beside[number, 2 * x : 2 * x + 2, lanes]
-        if number < 19:
-            return pops[number, x, start - 2 : start - 2 + size, lanes]
-        return mask[x, start - 2 : start - 2 + size, lanes].astype(jnp.float32)
-
-    def put(plane, part, half, value):
-        row = (plane % 2) * ROWS + part[1]
-        out[plane // 2, half, row : row + part[2], :] = value
-
     border, behind = (NX - 1, NX - 2) if up else (0, 1)
-    for half in range(2):
-        for part in pieces:
+    toward = TOWARD_HIGH if up else TOWARD_LOW
+
+    def put(plane, start, half, value):
+        row = (plane % 2) * ROWS + start
+        out[plane // 2, half, row : row + value.shape[0], :] = value
+
+    for half, lanes in enumerate(HALVES):
+        for tile in range(NY // 8):
+            rows = slice(8 * tile, 8 * tile + 8)
+            start = 2 + 8 * tile
+            for number in range(19):
+                put(number, start, half, pops[number, border, rows, lanes])
+            put(19, start, half, mask[border, rows, lanes].astype(jnp.float32))
+            f = [pops[number, behind, rows, lanes] for number in range(19)]
+            for i, number in enumerate(toward):
+                put(20 + i, start, half, f[number])
+            for i, value in enumerate(moments(f)[:4]):
+                put(25 + i, start, half, value)
+            put(29, start, half, mask[behind, rows, lanes].astype(jnp.float32))
+        for beside, inner, outer, numbers in (
+            (low_y, 1, 0, UPWARD),
+            (high_y, 2 + NY, 3 + NY, DOWNWARD),
+        ):
             for number in range(20):
-                put(number, part, half, piece(part, number, border, half))
-            f = [piece(part, number, behind, half) for number in range(19)]
-            for i, number in enumerate(TOWARD_HIGH if up else TOWARD_LOW):
-                put(20 + i, part, half, f[number])
+                put(number, inner, half, y_plane(beside, number, lanes, border))
+            for i, number in enumerate(numbers):
+                put(number, outer, half, y_plane(beside, 20 + i, lanes, border))
+            for i, number in enumerate(SPARE):
+                put(number, outer, half, y_plane(beside, 25 + i, lanes, border))
+            put(19, outer, half, y_plane(beside, 29, lanes, border))
+            f = [y_plane(beside, number, lanes, behind) for number in range(19)]
+            for i, number in enumerate(toward):
+                put(20 + i, inner, half, f[number])
+                place = numbers.index(number) if number in numbers else 0
+                put(20 + i, outer, half, y_plane(beside, 20 + place, lanes, behind))
             for i, value in enumerate(moments(f)[:4]):
-                put(25 + i, part, half, value)
-            put(29, part, half, piece(part, 19, behind, half))
+                put(25 + i, inner, half, value)
+                put(25 + i, outer, half, y_plane(beside, 25 + i, lanes, behind))
+            put(29, inner, half, y_plane(beside, 19, lanes, behind))
+            put(29, outer, half, y_plane(beside, 29, lanes, behind))
 
 
 def layers_kernel(pops, mask, low_y, high_y, sums, to_far, to_mate):
@@ -179,19 +207,20 @@
             pack_layers(pops, mask, low_y, high_y, to_far, which == 1)
 
 
-def sums_kernel(pops, mask, low_y, high_y, far_mask, mate_mask, sums, flags):
+def sums_kernel(pops, mask, low_y, high_y, far_mask, chip_masks, sums, flags):
     halves = HALVES
     core = lax.axis_index("core")
     first_core = core == 0
-    low_x = jnp.where(first_core, far_mask[...], mate_mask[...])
-    high_x = jnp.where(first_core, mate_mask[...], far_mask[...])
+    mate_mask = chip_masks[1 - core]
+    low_x = jnp.where(first_core, far_mask[...], mate_mask)
+    high_x = jnp.where(first_core, mate_mask, far_mask[...])
     flags[...] = jnp.zeros_like(flags)
     for half, lanes in enumerate(halves):
         for x in range(NX):
             row = FRONT + (x + 1) * ROWS
-            flags[half, row + 1 : row + 2, :] = low_y[19, 2 * x + 1 : 2 * x + 2, lanes]
+            flags[half, row + 1 : row + 2, :] = y_plane(low_y, 19, lanes, x)
             flags[half, row + 2 : row + 2 + NY, :] = mask[x, :, lanes].astype(jnp.float32)
-            flags[half, row + 2 + NY : row + 3 + NY, :] = high_y[19, 2 * x : 2 * x + 1, lanes]
+            flags[half, row + 2 + NY : row + 3 + NY, :] = y_plane(high_y, 19, lanes, x)
         flags[half, FRONT + 2 : FRONT + 2 + NY, :] = low_x[:, lanes]
         row = FRONT + (NX + 1) * ROWS
         flags[half, row + 2 : row + 2 + NY, :] = high_x[:, lanes]
@@ -229,22 +258,24 @@
                     sign = (2.0 * move_y) * ahead - move_y
                     for i in range(3):
                         acc[2 + i] = acc[2 + i] + sign * coefs[number][i]
-    place = lax.broadcasted_iota(jnp.int32, (8, LANES), 0)
+    extra = [jnp.zeros((1, LANES), jnp.float32) for _ in range(3)]
     for beside, y, sign, links in (
-        (low_y, 0, 2.0, ((10, 1, low_x), (7, 2 * NX - 1, high_x))),
-        (high_y, NY - 1, -2.0, ((8, 0, low_x), (9, 2 * NX - 2, high_x))),
+        (low_y, 0, 2.0, ((10, 0, low_x), (7, NX - 1, high_x))),
+        (high_y, NY - 1, -2.0, ((8, 0, low_x), (9, NX - 1, high_x))),
     ):
         for lanes in halves:
-            f = [beside[k, :, lanes] for k in range(19)]
-            _, _, coefs = response([link[0] for link in links], f, beside[19, :, lanes])
-            for number, row, layer in links:
-                ahead = jnp.where(place == row, sign * layer[y : y + 1, lanes], 0.0)
+            for number, x, layer in links:
+                f = [y_plane(beside, k, lanes, x) for k in range(19)]
+                _, _, coefs = response((number,), f, y_plane(beside, 19, lanes, x))
+                ahead = sign * layer[y : y + 1, lanes]
                 for i in range(3):
-                    acc[2 + i] = acc[2 + i] + ahead * coefs[number][i]
+                    extra[i] = extra[i] + ahead * coefs[number][i]
     lane = lax.broadcasted_iota(jnp.int32, (1, LANES), 1)
     line = jnp.zeros((1, LANES), jnp.float32)
     for i in range(5):
         value = jnp.sum(acc[i], axis=0, keepdims=True)
+        if i >= 2:
+            value = value + extra[i - 2]
         value = jnp.sum(value, axis=1, keepdims=True)
         line = jnp.where(lane == i, value, line)
     sums[...] = jnp.broadcast_to(line[None], sums.shape)
@@ -285,28 +316,45 @@
     return result
 
 
-def outer_layer(beside, at, side, half, shift, post):
-    core_rows = ((0, 8), (8, 8), (16, 4))
-    for start, size in core_rows:
-
-        def plane(number):
-            row = (number % 2) * ROWS + start
-            return beside[number // 2, half, row : row + size, :]
-
-        density, flux_x, flux_y, flux_z = [plane(25 + i) for i in range(4)]
-        fluid = plane(29)
-        toward = 1.0 - 2.0 * side.astype(jnp.float32)
-        inverse = 1.5 / (density + (1.0 - fluid))
-        ux = flux_x * inverse * toward
-        uy = flux_y * inverse + 1.5 * shift[:size]
-        uz = flux_z * inverse
-        base = 1.0 - (ux * ux + uy * uy + uz * uz) * (2.0 / 3.0)
-        scaled = density * (1.0 / RELAX)
-        for i, speed in enumerate((ux, ux + uy, ux - uy, ux + uz, ux - uz)):
-            weight = scaled * (1.0 / 18.0 if i == 0 else 1.0 / 36.0)
-            value = weight * (base + speed * (2.0 + 2.0 * speed)) - KEEP * plane(20 + i)
-            number = TOWARD_HIGH[i] + side * (TOWARD_LOW[i] - TOWARD_HIGH[i])
-            post[number, half, pl.ds(at + start, size), :] = jnp.where(fluid > 0.5, value, SOLID)
+def arriving(f, fluid, flow, speeds, shift):
+    density, flux_x, flux_y, flux_z = flow
+    inverse = 1.5 / (density + (1.0 - fluid))
+    ux = flux_x * inverse
+    uy = flux_y * inverse + 1.5 * shift
+    uz = flux_z * inverse
+    base = 1.0 - (ux * ux + uy * uy + uz * uz) * (2.0 / 3.0)
+    scaled = density * (1.0 / RELAX)
+    result = []
+    for i, speed in enumerate(speeds(ux, uy, uz)):
+        weight = scaled * (1.0 / 18.0 if i == 0 else 1.0 / 36.0)
+        value = weight * (base + speed * (2.0 + 2.0 * speed)) - KEEP * f[i]
+        result.append(jnp.where(fluid > 0.5, value, SOLID))
+    return result
+
+
+def along_x(sign):
+    return lambda ux, uy, uz: (
+        sign * ux,
+        sign * ux + uy,
+        sign * ux - uy,
+        sign * ux + uz,
+        sign * ux - uz,
+    )
+
+
+def along_y(sign):
+    return lambda ux, uy, uz: (
+        sign * uy,
+        sign * uy + ux,
+        sign * uy - ux,
+        sign * uy + uz,
+        sign * uy - uz,
+    )
+
+
+def x_plane(beside, plane, half, start, size):
+    row = (plane % 2) * ROWS + start
+    return beside[plane // 2, half, row : row + size, :]
 
 
 def last_streaming(later, flags, block, x, lane):
@@ -347,34 +395,55 @@
                 flags[half, row : row + 8, :] = fluid
                 for number, value in enumerate(collide(f, fluid, shift_1)):
                     post[number, half, row : row + 8, :] = value
-    for beside, start in ((low_y, 0), (high_y, 2 + NY)):
+    first_row = FRONT + 2 * ROWS
+    for beside, inner, outer, numbers, sign in (
+        (low_y, 1, 0, UPWARD, 1.0),
+        (high_y, 2 + NY, 3 + NY, DOWNWARD, -1.0),
+    ):
         for half, lanes in enumerate(halves):
-            f = [beside[k, :, lanes] for k in range(19)]
-            fluid = beside[19, :, lanes]
-            value = collide(f, fluid, shift_1)
+            planes = [y_plane(beside, i, lanes) for i in range(30)]
+            value = collide(planes[:19], planes[19], shift_1[:NX])
+            moved = arriving(
+                planes[20:25], planes[29], planes[25:29], along_y(sign), shift_1[:NX]
+            )
             for x in range(NX):
-                row = FRONT + (x + 2) * ROWS + start
-                flags[half, row : row + 2, :] = fluid[2 * x : 2 * x + 2]
+                row = first_row + x * ROWS + inner
+                flags[half, row : row + 1, :] = planes[19][x : x + 1]
                 for number in range(19):
-                    post[number, half, row : row + 2, :] = value[number][2 * x : 2 * x + 2]
+                    post[number, half, row : row + 1, :] = value[number][x : x + 1]
+                row = first_row + x * ROWS + outer
+                flags[half, row : row + 1, :] = planes[29][x : x + 1]
+                for i, number in enumerate(numbers):
+                    post[number, half, row : row + 1, :] = moved[i][x : x + 1]
     core = lax.axis_index("core")
     for beside, side in ((mate, 1 - core), (far, core)):
         inner = FRONT + ROWS + side * ((NX + 1) * ROWS)
         outer = FRONT + side * ((NX + 3) * ROWS)
+        sign = 1.0 - 2.0 * side.astype(jnp.float32)
         for half in range(2):
+            for start, size in ((1, 8), (9, 8), (17, 2)):
+                rows = pl.ds(inner + start, size)
+                planes = [x_plane(beside, i, half, start, size) for i in range(20)]
+                flags[half, rows, :] = planes[19]
+                for number, value in enumerate(collide(planes[:19], planes[19], shift_1[:size])):
+                    post[number, half, rows, :] = value
+            for start, numbers, upward in ((0, UPWARD, 1.0), (ROWS - 1, DOWNWARD, -1.0)):
+                row = pl.ds(inner + start, 1)
+                f = [x_plane(beside, number, half, start, 1) for number in numbers]
+                flow = [x_plane(beside, number, half, start, 1) for number in SPARE]
+                fluid = x_plane(beside, 19, half, start, 1)
+                flags[half, row, :] = fluid
+                moved = arriving(f, fluid, flow, along_y(upward), shift_1[:1])
+                for i, number in enumerate(numbers):
+                    post[number, half, row, :] = moved[i]
             for start, size in ((0, 8), (8, 8), (16, 4)):
-                rows = pl.ds(inner + start, size)
-
-                def plane(number):
-                    row = (number % 2) * ROWS + start
-                    return beside[number // 2, half, row : row + size, :]
-
-                f = [plane(number) for number in range(19)]
-                fluid = plane(19)
-                flags[half, rows, :] = fluid
-                for number, value in enumerate(collide(f, fluid, shift_1[:size])):
-                    post[number, half, rows, :] = value
-            outer_layer(beside, outer, side, half, shift_1, post)
+                planes = [x_plane(beside, i, half, start, size) for i in range(20, 30)]
+                moved = arriving(
+                    planes[:5], planes[9], planes[5:9], along_x(sign), shift_1[:size]
+                )
+                for i in range(5):
+                    number = TOWARD_HIGH[i] + side * (TOWARD_LOW[i] - TOWARD_HIGH[i])
+                    post[number, half, pl.ds(outer + start, size), :] = moved[i]
     done = 0
     for tile in range((NX + 2) * ROWS // 8):
         row = FRONT + ROWS + 8 * tile
@@ -430,8 +499,8 @@
             out_shape=(
                 f32(19, NX, NY, 2 * LANES),
                 jax.ShapeDtypeStruct((NX, NY, 2 * LANES), jnp.int32),
-                f32(20, 8, 256),
-                f32(20, 8, 256),
+                f32(SLOTS, 2 * NX, 256),
+                f32(SLOTS, 2 * NX, 256),
                 f32(NY, 2 * LANES),
                 f32(NY, 2 * LANES),
             ),
@@ -445,13 +514,13 @@
         low_y = shifted(to_high_y, 1)
         high_y = shifted(to_low_y, -1)
         far_mask = from_far(to_far)
-        mate_mask = from_mate(to_mate)
+        chip_masks = lax.all_gather(to_mate, "core")
         sums = pl.pallas_call(
             sums_kernel,
             out_shape=f32(first, 1, LANES),
             scratch_shapes=[pltpu.VMEM((2, FRONT + (NX + 2) * ROWS + 8, LANES), jnp.float32)],
             compiler_params=params(),
-        )(pops, mask, low_y, high_y, far_mask, mate_mask)
+        )(pops, mask, low_y, high_y, far_mask, chip_masks)
         to_far, to_mate = pl.pallas_call(
             layers_kernel,
             out_shape=(f32(SLOTS, 2, 2 * ROWS, LANES), f32(SLOTS, 2, 2 * ROWS, LANES)),

time: 64.3 us -> 64.2 us (level)
  blocking collectives: 27.1 us -> 33 us
  starting transfers between devices: 28.3 us -> 23.4 us
  waiting for transfers between devices: 1.35 us -> 0.23 us
    ppermute x4 -> x3, starting transfers between devices: 16.6 us -> 11.3 us  [swapped(): return lax.ppermute(value, local, pairs + [(j, i) for i, j in pairs])]
    all_gather x0 -> x1, blocking collectives: none -> 5.09 us  [on_device(): chip_masks = lax.all_gather(to_mate, 'core')]
    all_to_all x1, blocking collectives: 27.1 us -> 27.9 us  [on_device(): sums = lax.all_to_all(sums, ('region', 'core'), 0, 0, tiled=True)]
    ppermute x4 -> x3, waiting for transfers between devices: 0.81 us -> 0.01 us  [swapped(): return lax.ppermute(value, local, pairs + [(j, i) for i, j in pairs])]
  transfers between devices with their start and end apart: 7 -> 6, of which waited for: 2 -> 1; matrix products, arithmetic and copies ran while one was open for 0% -> 0% of each run, Pallas kernels for 2% -> 2%
where the time goes in v6:
time: 64.2 us; the launch traced here: 63.9 us
  blocking collectives  33 us (51%)
  starting transfers between devices  23.4 us (36%)
  Pallas kernels  7.2 us (11%)
    all_to_all x1, blocking collectives, on_device(): sums = lax.all_to_all(sums, ('region', 'core'), 0, 0, tiled=True)  27.9 us
    ppermute x3, starting transfers between devices, swapped(): return lax.ppermute(value, local, pairs + [(j, i) for i, j in pairs])  11.3 us
    ppermute x2, starting transfers between devices, shifted(): return lax.ppermute(value, 'region', pairs)  6.12 us
    all_to_all x1, starting transfers between devices, on_device(): sums = lax.all_to_all(sums, ('x', 'y'), 0, 0, tiled=True)  5.93 us
    all_gather x1, blocking collectives, on_device(): chip_masks = lax.all_gather(to_mate, 'core')  5.09 us
    pallas_call x1, Pallas kernels, on_device(): pl.pallas_call(steps_kernel, out_shape=pltpu.HBM((19, NX, NY, 2 * LANES),...  3.16 us
    pallas_call x1, Pallas kernels, on_device(): pl.pallas_call(pack_kernel, out_shape=(f32(19, NX, NY, 2 * LANES), jax.Sh...  1.46 us
    pallas_call x1, Pallas kernels, on_device(): pl.pallas_call(sums_kernel, out_shape=f32(first, 1, LANES), scratch_shape...  1.46 us
  transfers between devices with their start and end apart: 6, of which 1 were waited for; matrix products, arithmetic and copies ran while one was open for 0% of the time, Pallas kernels for 2%

profile of v6, /device:TPU:1, one launch (start us, length us, event | category | flops | bytes accessed | tf_op | source)
XLA Modules:
  0.0 63.9 jit_solution(16719360288181184000)
XLA Ops:
  0.0 1.5 %shard_map.28 = (f32[19,4,16,256]{3,2,1,0:T(8,128)S(1)}, s32[4,16,256]{2,1,0:T(8,128)S(1)}, f32[15,8,256]{2,1,0:T(8,128)S(1)}, f32[15,8,256]{2,1,0:T(8,128)S(1)}...) custom-call(f32[19,4,16,256]{3,2,1,0:T(8,128)} %pops_in.1, s32[4,16,256]{2,1,0:T(8,128)} %mask_in.1), custom_call_target="tpu_custom_call" | custom-call | tf_op jit(solution)/shard_map/pallas_call | solution.py:497
  1.5 4.8 %collective-permute-start = (f32[15,8,256]{2,1,0:T(8,128)S(1)}, f32[15,8,256]{2,1,0:T(8,128)S(1)}, u32[]{:S(2)}, u32[]{:S(2)}) collective-permute-start(f32[15,8,256]{2,1,0:T(8,128)S(1)} %get-tuple-element.15), channel_id=1, source_target_pairs={{0,64},{64,128},{128,192},{192,256},{256,320},{320,384},{384,448},... | collective-permute-start | bytes 368648 | tf_op jit(solution)/shard_map/ppermute | solution.py:484
  6.3 1.3 %collective-permute-start.1 = (f32[15,8,256]{2,1,0:T(8,128)S(1)}, f32[15,8,256]{2,1,0:T(8,128)S(1)}, u32[]{:S(2)}, u32[]{:S(2)}) collective-permute-start(f32[15,8,256]{2,1,0:T(8,128)S(1)} %get-tuple-element.16), channel_id=1, source_target_pairs={{64,0},{128,64},{192,128},{256,192},{320,256},{384,320},{448,384},... | collective-permute-start | bytes 368648 | tf_op jit(solution)/shard_map/ppermute | solution.py:484
  7.6 4.0 %collective-permute-start.2 = (f32[16,256]{1,0:T(8,128)S(1)}, f32[16,256]{1,0:T(8,128)S(1)}, u32[]{:S(2)}, u32[]{:S(2)}) collective-permute-start(f32[16,256]{1,0:T(8,128)S(1)} %get-tuple-element.17), channel_id=1, source_target_pairs={{1,2},{3,4},{5,6},{7,8},{9,10},{11,12},{13,14},{15,16},{17,18},{19... | collective-permute-start | bytes 49160 | tf_op jit(solution)/shard_map/ppermute | solution.py:487
  11.7 5.1 %all-gather = f32[32,256]{1,0:T(8,128)S(1)} all-gather(f32[16,256]{1,0:T(8,128)S(1)} %get-tuple-element.18), channel_id=2, replica_groups=mesh['region'=12,'x'=4,'y'=8,'core'=2] {'core'}, dimensions={0}, use_global_device_ids=true | all-gather | bytes 49152 | tf_op jit(solution)/shard_map/all_gather | solution.py:517
  16.8 0.0 collective-permute-done.2.far_mask
  16.8 0.0 collective-permute-done.low_y
  16.8 0.0 collective-permute-done.1.high_y
  16.8 1.5 %shard_map.29.sums = f32[32,1,128]{2,1,0:T(1,128)} custom-call(f32[19,4,16,256]{3,2,1,0:T(8,128)S(1)} %get-tuple-element.13.pops, s32[4,16,256]{2,1,0:T(8,128)S(1)} %get-tuple-element.14.mask, f32[15,8,256]{2,1,0:T(8,128)S(1)} %collective-permute-done.low_y, f32[15,8,256]{2,1,0:T(8,128)S(1)} %collective-permute-done.1.high_y, ...), custom_call_target="tpu_custom_call" | custom-call | tf_op jit(solution)/shard_map/pallas_call | solution.py:518
  18.2 5.9 %all-to-all-start = ((f32[32,1,128]{2,1,0:T(1,128)}), f32[32,1,128]{2,1,0:T(1,128)S(1)}, u32[]{:S(2)}, u32[]{:S(2)}) async-start(f32[32,1,128]{2,1,0:T(1,128)} %shard_map.29.sums), calls=%async_computation | async-start | bytes 32768 | tf_op jit(solution)/shard_map/all_to_all | solution.py:532
  24.2 1.1 %shard_map.31 = (f32[15,2,40,128]{3,2,1,0:T(8,128)}, f32[15,2,40,128]{3,2,1,0:T(8,128)S(1)}) custom-call(f32[19,4,16,256]{3,2,1,0:T(8,128)S(1)} %get-tuple-element.13.pops, s32[4,16,256]{2,1,0:T(8,128)S(1)} %get-tuple-element.14.mask, f32[15,8,256]{2,1,0:T(8,128)S(1)} %collective-permute-done.low_y, f32[15,8,256]{2,1,0:T(8,128)S(1)} %collective-permute-done.1.high_y, ...), custom_call_target="tpu_custom_call" | custom-call | tf_op jit(solution)/shard_map/pallas_call | solution.py:524
  25.2 5.4 %collective-permute-start.3 = (f32[15,2,40,128]{3,2,1,0:T(8,128)}, f32[15,2,40,128]{3,2,1,0:T(8,128)S(1)}, u32[]{:S(2)}, u32[]{:S(2)}) collective-permute-start(f32[15,2,40,128]{3,2,1,0:T(8,128)} %get-tuple-element.19), channel_id=1, source_target_pairs={{1,2},{3,4},{5,6},{7,8},{9,10},{11,12},{13,14},{15,16},{17,18},{19... | collective-permute-start | bytes 1843208 | tf_op jit(solution)/shard_map/ppermute | solution.py:487
  30.6 1.9 %collective-permute-start.4 = (f32[15,2,40,128]{3,2,1,0:T(8,128)S(1)}, f32[15,2,40,128]{3,2,1,0:T(8,128)S(1)}, u32[]{:S(2)}, u32[]{:S(2)}) collective-permute-start(f32[15,2,40,128]{3,2,1,0:T(8,128)S(1)} %get-tuple-element.20), channel_id=1, source_target_pairs={{0,1},{2,3},{4,5},{6,7},{8,9},{10,11},{12,13},{14,15},{16,17},{18,... | collective-permute-start | bytes 1843208 | tf_op jit(solution)/shard_map/ppermute | solution.py:487
  32.6 0.2 all-to-all-done.arrived
  32.8 27.9 %all_to_all.10.arrived = f32[24,1,128]{2,1,0:T(1,128)S(1)} all-to-all(f32[24,1,128]{2,1,0:T(1,128)S(1)} %shard_map.30), channel_id=1, replica_groups=mesh['region'=12,'x'=4,'y'=8,'core'=2] {'region','core'}, dimensions={0} | all-to-all | bytes 24576 | tf_op jit(solution)/shard_map/all_to_all | solution.py:539
  60.8 0.0 collective-permute-done.3.far
  60.8 0.0 collective-permute-done.4.mate
  60.8 3.2 %shard_map.32 = f32[19,4,16,256]{3,2,1,0:T(8,128)} custom-call(f32[24,1,128]{2,1,0:T(1,128)S(1)} %all_to_all.10.arrived, f32[19,4,16,256]{3,2,1,0:T(8,128)S(1)} %get-tuple-element.13.pops, s32[4,16,256]{2,1,0:T(8,128)S(1)} %get-tuple-element.14.mask, f32[15,8,256]{2,1,0:T(8,128)S(1)} %collective-permute-done.low_y, ...), custom_call_target="tpu_custom_call" | custom-call | tf_op jit(solution)/shard_map/pallas_call | solution.py:541
  (1 shorter events, 0.0 us)
Async XLA Ops:
  1.5 15.3 %collective-permute-start = (f32[15,8,256]{2,1,0:T(8,128)S(1)}, f32[15,8,256]{2,1,0:T(8,128)S(1)}, u32[]{:S(2)}, u32[]{:S(2)}) collective-permute-start(f32[15,8,256]{2,1,0:T(8,128)S(1)} %get-tuple-element.15), channel_id=1, source_target_pairs={{0,64},{64,128},{128,192},{192,256},{256,320},{320,384},{384,448},... | collective-permute-start | bytes 368648 | tf_op jit(solution)/shard_map/ppermute | solution.py:484
  6.3 10.5 %collective-permute-start.1 = (f32[15,8,256]{2,1,0:T(8,128)S(1)}, f32[15,8,256]{2,1,0:T(8,128)S(1)}, u32[]{:S(2)}, u32[]{:S(2)}) collective-permute-start(f32[15,8,256]{2,1,0:T(8,128)S(1)} %get-tuple-element.16), channel_id=1, source_target_pairs={{64,0},{128,64},{192,128},{256,192},{320,256},{384,320},{448,384},... | collective-permute-start | bytes 368648 | tf_op jit(solution)/shard_map/ppermute | solution.py:484
  7.6 9.1 %collective-permute-start.2 = (f32[16,256]{1,0:T(8,128)S(1)}, f32[16,256]{1,0:T(8,128)S(1)}, u32[]{:S(2)}, u32[]{:S(2)}) collective-permute-start(f32[16,256]{1,0:T(8,128)S(1)} %get-tuple-element.17), channel_id=1, source_target_pairs={{1,2},{3,4},{5,6},{7,8},{9,10},{11,12},{13,14},{15,16},{17,18},{19... | collective-permute-start | bytes 49160 | tf_op jit(solution)/shard_map/ppermute | solution.py:487
  18.2 14.6 %all-to-all-start = ((f32[32,1,128]{2,1,0:T(1,128)}), f32[32,1,128]{2,1,0:T(1,128)S(1)}, u32[]{:S(2)}, u32[]{:S(2)}) async-start(f32[32,1,128]{2,1,0:T(1,128)} %shard_map.29.sums), calls=%async_computation | async-start | bytes 32768 | tf_op jit(solution)/shard_map/all_to_all | solution.py:532
  25.2 35.5 %collective-permute-start.3 = (f32[15,2,40,128]{3,2,1,0:T(8,128)}, f32[15,2,40,128]{3,2,1,0:T(8,128)S(1)}, u32[]{:S(2)}, u32[]{:S(2)}) collective-permute-start(f32[15,2,40,128]{3,2,1,0:T(8,128)} %get-tuple-element.19), channel_id=1, source_target_pairs={{1,2},{3,4},{5,6},{7,8},{9,10},{11,12},{13,14},{15,16},{17,18},{19... | collective-permute-start | bytes 1843208 | tf_op jit(solution)/shard_map/ppermute | solution.py:487
  30.6 30.1 %collective-permute-start.4 = (f32[15,2,40,128]{3,2,1,0:T(8,128)S(1)}, f32[15,2,40,128]{3,2,1,0:T(8,128)S(1)}, u32[]{:S(2)}, u32[]{:S(2)}) collective-permute-start(f32[15,2,40,128]{3,2,1,0:T(8,128)S(1)} %get-tuple-element.20), channel_id=1, source_target_pairs={{0,1},{2,3},{4,5},{6,7},{8,9},{10,11},{12,13},{14,15},{16,17},{18,... | collective-permute-start | bytes 1843208 | tf_op jit(solution)/shard_map/ppermute | solution.py:487

commit v7 on v6

--- a/solution.py
+++ b/solution.py
@@ -477,7 +477,7 @@
         ("region", "x", "y", "core"),
     )
     local = ("x", "y", "core")
-    first, second = blocks // cores, regions * cores
+    first, second = regions * cores, blocks // cores
 
     def shifted(value, step):
         pairs = [(i, i + step) for i in range(regions) if 0 <= i + step < regions]
@@ -529,14 +529,14 @@
         )(pops, mask, low_y, high_y, sums)
         far = from_far(to_far)
         mate = from_mate(to_mate)
-        sums = lax.all_to_all(sums, ("x", "y"), 0, 0, tiled=True)
+        sums = lax.all_to_all(sums, ("region", "core"), 0, 0, tiled=True)
         sums = pl.pallas_call(
             relay_kernel,
             out_shape=f32(second, 1, LANES),
             compiler_params=params(),
             cost_estimate=pl.CostEstimate(flops=3 * 10**10, bytes_accessed=0, transcendentals=0),
         )(sums)
-        sums = lax.all_to_all(sums, ("region", "core"), 0, 0, tiled=True)
+        sums = lax.all_to_all(sums, ("x", "y"), 0, 0, tiled=True)
         rows = FRONT + (NX + 4) * ROWS + 8
         return pl.pallas_call(
             steps_kernel,

time: 64.2 us -> 62.8 us (0.978)
  blocking collectives: 33 us -> 24 us
  starting transfers between devices: 23.4 us -> 28.1 us
  waiting for transfers between devices: 0.23 us -> 3.14 us
    all_to_all x1, blocking collectives: 27.9 us -> 18.9 us  [on_device(): sums = lax.all_to_all(sums, ('x', 'y'), 0, 0, tiled=True)]
    all_to_all x1, starting transfers between devices: 5.93 us -> 12.8 us  [on_device(): sums = lax.all_to_all(sums, ('region', 'core'), 0, 0, tiled=True)]
    all_to_all x1, waiting for transfers between devices: 0.22 us -> 3.12 us  [on_device(): sums = lax.all_to_all(sums, ('region', 'core'), 0, 0, tiled=True)]
    ppermute x3, starting transfers between devices: 11.3 us -> 9.22 us  [swapped(): return lax.ppermute(value, local, pairs + [(j, i) for i, j in pairs])]
where the time goes in v7:
time: 62.8 us; the launch traced here: 62.5 us
  starting transfers between devices  28.1 us (45%)
  blocking collectives  24 us (38%)
  Pallas kernels  7.2 us (11%)
  waiting for transfers between devices  3.14 us (5%)
    all_to_all x1, blocking collectives, on_device(): sums = lax.all_to_all(sums, ('x', 'y'), 0, 0, tiled=True)  18.9 us
    all_to_all x1, starting transfers between devices, on_device(): sums = lax.all_to_all(sums, ('region', 'core'), 0, 0, tiled=True)  12.8 us
    ppermute x3, starting transfers between devices, swapped(): return lax.ppermute(value, local, pairs + [(j, i) for i, j in pairs])  9.22 us
    ppermute x2, starting transfers between devices, shifted(): return lax.ppermute(value, 'region', pairs)  6.12 us
    all_gather x1, blocking collectives, on_device(): chip_masks = lax.all_gather(to_mate, 'core')  5.09 us
    pallas_call x1, Pallas kernels, on_device(): pl.pallas_call(steps_kernel, out_shape=pltpu.HBM((19, NX, NY, 2 * LANES),...  3.17 us
    all_to_all x1, waiting for transfers between devices, on_device(): sums = lax.all_to_all(sums, ('region', 'core'), 0, 0, tiled=True)  3.12 us
    pallas_call x1, Pallas kernels, on_device(): pl.pallas_call(pack_kernel, out_shape=(f32(19, NX, NY, 2 * LANES), jax.Sh...  1.46 us
  transfers between devices with their start and end apart: 6, of which 1 were waited for; matrix products, arithmetic and copies ran while one was open for 0% of the time, Pallas kernels for 2%

profile of v7, /device:TPU:1, one launch (start us, length us, event | category | flops | bytes accessed | tf_op | source)
XLA Modules:
  0.0 62.5 jit_solution(12002448182969458206)
XLA Ops:
  0.0 1.5 %shard_map.28 = (f32[19,4,16,256]{3,2,1,0:T(8,128)S(1)}, s32[4,16,256]{2,1,0:T(8,128)S(1)}, f32[15,8,256]{2,1,0:T(8,128)S(1)}, f32[15,8,256]{2,1,0:T(8,128)S(1)}...) custom-call(f32[19,4,16,256]{3,2,1,0:T(8,128)} %pops_in.1, s32[4,16,256]{2,1,0:T(8,128)} %mask_in.1), custom_call_target="tpu_custom_call" | custom-call | tf_op jit(solution)/shard_map/pallas_call | solution.py:497
  1.5 4.8 %collective-permute-start = (f32[15,8,256]{2,1,0:T(8,128)S(1)}, f32[15,8,256]{2,1,0:T(8,128)S(1)}, u32[]{:S(2)}, u32[]{:S(2)}) collective-permute-start(f32[15,8,256]{2,1,0:T(8,128)S(1)} %get-tuple-element.15), channel_id=1, source_target_pairs={{0,64},{64,128},{128,192},{192,256},{256,320},{320,384},{384,448},... | collective-permute-start | bytes 368648 | tf_op jit(solution)/shard_map/ppermute | solution.py:484
  6.3 1.3 %collective-permute-start.1 = (f32[15,8,256]{2,1,0:T(8,128)S(1)}, f32[15,8,256]{2,1,0:T(8,128)S(1)}, u32[]{:S(2)}, u32[]{:S(2)}) collective-permute-start(f32[15,8,256]{2,1,0:T(8,128)S(1)} %get-tuple-element.16), channel_id=1, source_target_pairs={{64,0},{128,64},{192,128},{256,192},{320,256},{384,320},{448,384},... | collective-permute-start | bytes 368648 | tf_op jit(solution)/shard_map/ppermute | solution.py:484
  7.6 4.0 %collective-permute-start.2 = (f32[16,256]{1,0:T(8,128)S(1)}, f32[16,256]{1,0:T(8,128)S(1)}, u32[]{:S(2)}, u32[]{:S(2)}) collective-permute-start(f32[16,256]{1,0:T(8,128)S(1)} %get-tuple-element.17), channel_id=1, source_target_pairs={{1,2},{3,4},{5,6},{7,8},{9,10},{11,12},{13,14},{15,16},{17,18},{19... | collective-permute-start | bytes 49160 | tf_op jit(solution)/shard_map/ppermute | solution.py:487
  11.7 5.1 %all-gather = f32[32,256]{1,0:T(8,128)S(1)} all-gather(f32[16,256]{1,0:T(8,128)S(1)} %get-tuple-element.18), channel_id=2, replica_groups=mesh['region'=12,'x'=4,'y'=8,'core'=2] {'core'}, dimensions={0}, use_global_device_ids=true | all-gather | bytes 49152 | tf_op jit(solution)/shard_map/all_gather | solution.py:517
  16.8 0.0 collective-permute-done.2.far_mask
  16.8 0.0 collective-permute-done.low_y
  16.8 0.0 collective-permute-done.1.high_y
  16.8 1.4 %shard_map.29.sums = f32[24,1,128]{2,1,0:T(1,128)} custom-call(f32[19,4,16,256]{3,2,1,0:T(8,128)S(1)} %get-tuple-element.13.pops, s32[4,16,256]{2,1,0:T(8,128)S(1)} %get-tuple-element.14.mask, f32[15,8,256]{2,1,0:T(8,128)S(1)} %collective-permute-done.low_y, f32[15,8,256]{2,1,0:T(8,128)S(1)} %collective-permute-done.1.high_y, ...), custom_call_target="tpu_custom_call" | custom-call | tf_op jit(solution)/shard_map/pallas_call | solution.py:518
  18.2 12.8 %all-to-all-start = ((f32[24,1,128]{2,1,0:T(1,128)}), f32[24,1,128]{2,1,0:T(1,128)S(1)}, u32[]{:S(2)}, u32[]{:S(2)}) async-start(f32[24,1,128]{2,1,0:T(1,128)} %shard_map.29.sums), calls=%async_computation | async-start | bytes 24576 | tf_op jit(solution)/shard_map/all_to_all | solution.py:532
  31.0 1.1 %shard_map.31 = (f32[15,2,40,128]{3,2,1,0:T(8,128)}, f32[15,2,40,128]{3,2,1,0:T(8,128)S(1)}) custom-call(f32[19,4,16,256]{3,2,1,0:T(8,128)S(1)} %get-tuple-element.13.pops, s32[4,16,256]{2,1,0:T(8,128)S(1)} %get-tuple-element.14.mask, f32[15,8,256]{2,1,0:T(8,128)S(1)} %collective-permute-done.low_y, f32[15,8,256]{2,1,0:T(8,128)S(1)} %collective-permute-done.1.high_y, ...), custom_call_target="tpu_custom_call" | custom-call | tf_op jit(solution)/shard_map/pallas_call | solution.py:524
  32.1 3.3 %collective-permute-start.3 = (f32[15,2,40,128]{3,2,1,0:T(8,128)}, f32[15,2,40,128]{3,2,1,0:T(8,128)S(1)}, u32[]{:S(2)}, u32[]{:S(2)}) collective-permute-start(f32[15,2,40,128]{3,2,1,0:T(8,128)} %get-tuple-element.19), channel_id=1, source_target_pairs={{1,2},{3,4},{5,6},{7,8},{9,10},{11,12},{13,14},{15,16},{17,18},{19... | collective-permute-start | bytes 1843208 | tf_op jit(solution)/shard_map/ppermute | solution.py:487
  35.3 1.9 %collective-permute-start.4 = (f32[15,2,40,128]{3,2,1,0:T(8,128)S(1)}, f32[15,2,40,128]{3,2,1,0:T(8,128)S(1)}, u32[]{:S(2)}, u32[]{:S(2)}) collective-permute-start(f32[15,2,40,128]{3,2,1,0:T(8,128)S(1)} %get-tuple-element.20), channel_id=1, source_target_pairs={{0,1},{2,3},{4,5},{6,7},{8,9},{10,11},{12,13},{14,15},{16,17},{18,... | collective-permute-start | bytes 1843208 | tf_op jit(solution)/shard_map/ppermute | solution.py:487
  37.3 3.1 %all-to-all-done.arrived = f32[24,1,128]{2,1,0:T(1,128)S(1)} async-done(((f32[24,1,128]{2,1,0:T(1,128)}), f32[24,1,128]{2,1,0:T(1,128)S(1)}, u32[]{:S(2)}, u32[]{:S(2)}) %all-to-all-start) | async-done | bytes 12320 | tf_op jit(solution)/shard_map/all_to_all | solution.py:532
  40.4 18.9 %all_to_all.10.arrived = f32[32,1,128]{2,1,0:T(1,128)S(1)} all-to-all(f32[32,1,128]{2,1,0:T(1,128)S(1)} %shard_map.30), channel_id=1, replica_groups=mesh['region'=12,'x'=4,'y'=8,'core'=2] {'x','y'}, dimensions={0} | all-to-all | bytes 32768 | tf_op jit(solution)/shard_map/all_to_all | solution.py:539
  59.3 0.0 collective-permute-done.3.far
  59.3 0.0 collective-permute-done.4.mate
  59.3 3.2 %shard_map.32 = f32[19,4,16,256]{3,2,1,0:T(8,128)} custom-call(f32[32,1,128]{2,1,0:T(1,128)S(1)} %all_to_all.10.arrived, f32[19,4,16,256]{3,2,1,0:T(8,128)S(1)} %get-tuple-element.13.pops, s32[4,16,256]{2,1,0:T(8,128)S(1)} %get-tuple-element.14.mask, f32[15,8,256]{2,1,0:T(8,128)S(1)} %collective-permute-done.low_y, ...), custom_call_target="tpu_custom_call" | custom-call | tf_op jit(solution)/shard_map/pallas_call | solution.py:541
  (1 shorter events, 0.0 us)
Async XLA Ops:
  1.5 15.3 %collective-permute-start = (f32[15,8,256]{2,1,0:T(8,128)S(1)}, f32[15,8,256]{2,1,0:T(8,128)S(1)}, u32[]{:S(2)}, u32[]{:S(2)}) collective-permute-start(f32[15,8,256]{2,1,0:T(8,128)S(1)} %get-tuple-element.15), channel_id=1, source_target_pairs={{0,64},{64,128},{128,192},{192,256},{256,320},{320,384},{384,448},... | collective-permute-start | bytes 368648 | tf_op jit(solution)/shard_map/ppermute | solution.py:484
  6.3 10.5 %collective-permute-start.1 = (f32[15,8,256]{2,1,0:T(8,128)S(1)}, f32[15,8,256]{2,1,0:T(8,128)S(1)}, u32[]{:S(2)}, u32[]{:S(2)}) collective-permute-start(f32[15,8,256]{2,1,0:T(8,128)S(1)} %get-tuple-element.16), channel_id=1, source_target_pairs={{64,0},{128,64},{192,128},{256,192},{320,256},{384,320},{448,384},... | collective-permute-start | bytes 368648 | tf_op jit(solution)/shard_map/ppermute | solution.py:484
  7.6 9.1 %collective-permute-start.2 = (f32[16,256]{1,0:T(8,128)S(1)}, f32[16,256]{1,0:T(8,128)S(1)}, u32[]{:S(2)}, u32[]{:S(2)}) collective-permute-start(f32[16,256]{1,0:T(8,128)S(1)} %get-tuple-element.17), channel_id=1, source_target_pairs={{1,2},{3,4},{5,6},{7,8},{9,10},{11,12},{13,14},{15,16},{17,18},{19... | collective-permute-start | bytes 49160 | tf_op jit(solution)/shard_map/ppermute | solution.py:487
  18.2 22.2 %all-to-all-start = ((f32[24,1,128]{2,1,0:T(1,128)}), f32[24,1,128]{2,1,0:T(1,128)S(1)}, u32[]{:S(2)}, u32[]{:S(2)}) async-start(f32[24,1,128]{2,1,0:T(1,128)} %shard_map.29.sums), calls=%async_computation | async-start | bytes 24576 | tf_op jit(solution)/shard_map/all_to_all | solution.py:532
  32.1 27.2 %collective-permute-start.3 = (f32[15,2,40,128]{3,2,1,0:T(8,128)}, f32[15,2,40,128]{3,2,1,0:T(8,128)S(1)}, u32[]{:S(2)}, u32[]{:S(2)}) collective-permute-start(f32[15,2,40,128]{3,2,1,0:T(8,128)} %get-tuple-element.19), channel_id=1, source_target_pairs={{1,2},{3,4},{5,6},{7,8},{9,10},{11,12},{13,14},{15,16},{17,18},{19... | collective-permute-start | bytes 1843208 | tf_op jit(solution)/shard_map/ppermute | solution.py:487
  35.3 24.0 %collective-permute-start.4 = (f32[15,2,40,128]{3,2,1,0:T(8,128)S(1)}, f32[15,2,40,128]{3,2,1,0:T(8,128)S(1)}, u32[]{:S(2)}, u32[]{:S(2)}) collective-permute-start(f32[15,2,40,128]{3,2,1,0:T(8,128)S(1)} %get-tuple-element.20), channel_id=1, source_target_pairs={{0,1},{2,3},{4,5},{6,7},{8,9},{10,11},{12,13},{14,15},{16,17},{18,... | collective-permute-start | bytes 1843208 | tf_op jit(solution)/shard_map/ppermute | solution.py:487

commit v8 on v7

--- a/solution.py
+++ b/solution.py
@@ -121,20 +121,23 @@
 def pack_kernel(
     pops_in, mask_in, pops, mask, to_low_y, to_high_y, to_far, to_mate, pops_sem, mask_sem
 ):
-    pops_copy = pltpu.make_async_copy(pops_in, pops, pops_sem)
+    pops_copies = [
+        pltpu.make_async_copy(pops_in.at[:, x], pops.at[:, x], pops_sem.at[x]) for x in range(NX)
+    ]
     mask_copy = pltpu.make_async_copy(mask_in, mask, mask_sem)
-    pops_copy.start()
     mask_copy.start()
+    for pops_copy in pops_copies:
+        pops_copy.start()
     mask_copy.wait()
     core = lax.axis_index("core")
     to_mate[...] = mask[(1 - core) * (NX - 1)].astype(jnp.float32)
     to_far[...] = mask[core * (NX - 1)].astype(jnp.float32)
-    pops_copy.wait()
-    for out, border, behind, numbers in (
-        (to_low_y, 0, 1, DOWNWARD),
-        (to_high_y, NY - 1, NY - 2, UPWARD),
-    ):
-        for x in range(NX):
+    for x in range(NX):
+        pops_copies[x].wait()
+        for out, border, behind, numbers in (
+            (to_low_y, 0, 1, DOWNWARD),
+            (to_high_y, NY - 1, NY - 2, UPWARD),
+        ):
             f = [pops[number, x, behind : behind + 1, :] for number in range(19)]
             planes = [pops[number, x, border : border + 1, :] for number in range(19)]
             planes.append(mask[x, border : border + 1, :].astype(jnp.float32))
@@ -233,7 +236,15 @@
             for half, lanes in enumerate(halves):
                 f = [pops[k, x, 8 * tile : 8 * tile + 8, lanes] for k in range(19)]
                 fluid = flags[half, row : row + 8, :]
-                density, flux_y, coefs = response(numbers, f, fluid)
+                density, flux_x, flux_y, flux_z, _, _ = moments(f)
+                inverse = 1.0 / (density + (1.0 - fluid))
+                ux = flux_x * inverse
+                uy = flux_y * inverse
+                uz = flux_z * inverse
+                base = 1.0 - 1.5 * (ux * ux + uy * uy + uz * uz)
+                scaled = density * (fluid * (1.0 / RELAX))
+                parts = [[0.0] * 3, [0.0] * 3]
+                kept = 0.0
                 acc[0] = acc[0] + fluid * flux_y
                 acc[1] = acc[1] + fluid * density
                 for number in numbers:
@@ -256,8 +267,22 @@
                         else:
                             ahead = jnp.where(lane == 0, 0.0, here)
                     sign = (2.0 * move_y) * ahead - move_y
-                    for i in range(3):
-                        acc[2 + i] = acc[2 + i] + sign * coefs[number][i]
+                    speed = move_y * uy
+                    if move_x:
+                        speed = speed + move_x * ux
+                    if move_z:
+                        speed = speed + move_z * uz
+                    part = parts[0 if number < 7 else 1]
+                    part[0] = part[0] + sign * (base + speed * (3.0 + 4.5 * speed))
+                    part[1] = part[1] + sign * (move_y * (1.0 + 3.0 * speed) - uy)
+                    part[2] = part[2] + sign
+                    kept = kept + sign * f[number]
+                acc[2] = acc[2] - (KEEP * fluid) * kept
+                for part, weight in zip(parts, (1.0 / 18.0, 1.0 / 36.0)):
+                    weight = scaled * weight
+                    acc[2] = acc[2] + weight * part[0]
+                    acc[3] = acc[3] + (3.0 * weight) * part[1]
+                    acc[4] = acc[4] + (3.0 * weight) * part[2]
     extra = [jnp.zeros((1, LANES), jnp.float32) for _ in range(3)]
     for beside, y, sign, links in (
         (low_y, 0, 2.0, ((10, 0, low_x), (7, NX - 1, high_x))),
@@ -505,7 +530,7 @@
                 f32(NY, 2 * LANES),
             ),
             in_specs=[hbm, hbm],
-            scratch_shapes=[pltpu.SemaphoreType.DMA, pltpu.SemaphoreType.DMA],
+            scratch_shapes=[pltpu.SemaphoreType.DMA((NX,)), pltpu.SemaphoreType.DMA],
             compiler_params=params(),
         )(
             pltpu.with_memory_space_constraint(pops, pltpu.HBM),

time: 62.8 us -> 62.6 us (level)
  no operation moved by 1% of the time
where the time goes in v8:
time: 62.6 us; the launch traced here: 62.3 us
  starting transfers between devices  28.1 us (45%)
  blocking collectives  24 us (38%)
  Pallas kernels  7 us (11%)
  waiting for transfers between devices  3.14 us (5%)
    all_to_all x1, blocking collectives, on_device(): sums = lax.all_to_all(sums, ('x', 'y'), 0, 0, tiled=True)  18.9 us
    all_to_all x1, starting transfers between devices, on_device(): sums = lax.all_to_all(sums, ('region', 'core'), 0, 0, tiled=True)  12.8 us
    ppermute x3, starting transfers between devices, swapped(): return lax.ppermute(value, local, pairs + [(j, i) for i, j in pairs])  9.22 us
    ppermute x2, starting transfers between devices, shifted(): return lax.ppermute(value, 'region', pairs)  6.12 us
    all_gather x1, blocking collectives, on_device(): chip_masks = lax.all_gather(to_mate, 'core')  5.09 us
    pallas_call x1, Pallas kernels, on_device(): pl.pallas_call(steps_kernel, out_shape=pltpu.HBM((19, NX, NY, 2 * LANES),...  3.17 us
    all_to_all x1, waiting for transfers between devices, on_device(): sums = lax.all_to_all(sums, ('region', 'core'), 0, 0, tiled=True)  3.12 us
    pallas_call x1, Pallas kernels, on_device(): pl.pallas_call(sums_kernel, out_shape=f32(first, 1, LANES), scratch_shape...  1.36 us
  transfers between devices with their start and end apart: 6, of which 1 were waited for; matrix products, arithmetic and copies ran while one was open for 0% of the time, Pallas kernels for 2%

profile of v8, /device:TPU:1, one launch (start us, length us, event | category | flops | bytes accessed | tf_op | source)
XLA Modules:
  0.0 62.3 jit_solution(4706646040757830198)
XLA Ops:
  0.0 1.4 %shard_map.28 = (f32[19,4,16,256]{3,2,1,0:T(8,128)S(1)}, s32[4,16,256]{2,1,0:T(8,128)S(1)}, f32[15,8,256]{2,1,0:T(8,128)S(1)}, f32[15,8,256]{2,1,0:T(8,128)S(1)}...) custom-call(f32[19,4,16,256]{3,2,1,0:T(8,128)} %pops_in.1, s32[4,16,256]{2,1,0:T(8,128)} %mask_in.1), custom_call_target="tpu_custom_call" | custom-call | tf_op jit(solution)/shard_map/pallas_call | solution.py:522
  1.4 4.8 %collective-permute-start = (f32[15,8,256]{2,1,0:T(8,128)S(1)}, f32[15,8,256]{2,1,0:T(8,128)S(1)}, u32[]{:S(2)}, u32[]{:S(2)}) collective-permute-start(f32[15,8,256]{2,1,0:T(8,128)S(1)} %get-tuple-element.15), channel_id=1, source_target_pairs={{0,64},{64,128},{128,192},{192,256},{256,320},{320,384},{384,448},... | collective-permute-start | bytes 368648 | tf_op jit(solution)/shard_map/ppermute | solution.py:509
  6.2 1.3 %collective-permute-start.1 = (f32[15,8,256]{2,1,0:T(8,128)S(1)}, f32[15,8,256]{2,1,0:T(8,128)S(1)}, u32[]{:S(2)}, u32[]{:S(2)}) collective-permute-start(f32[15,8,256]{2,1,0:T(8,128)S(1)} %get-tuple-element.16), channel_id=1, source_target_pairs={{64,0},{128,64},{192,128},{256,192},{320,256},{384,320},{448,384},... | collective-permute-start | bytes 368648 | tf_op jit(solution)/shard_map/ppermute | solution.py:509
  7.5 4.0 %collective-permute-start.2 = (f32[16,256]{1,0:T(8,128)S(1)}, f32[16,256]{1,0:T(8,128)S(1)}, u32[]{:S(2)}, u32[]{:S(2)}) collective-permute-start(f32[16,256]{1,0:T(8,128)S(1)} %get-tuple-element.17), channel_id=1, source_target_pairs={{1,2},{3,4},{5,6},{7,8},{9,10},{11,12},{13,14},{15,16},{17,18},{19... | collective-permute-start | bytes 49160 | tf_op jit(solution)/shard_map/ppermute | solution.py:512
  11.6 5.1 %all-gather = f32[32,256]{1,0:T(8,128)S(1)} all-gather(f32[16,256]{1,0:T(8,128)S(1)} %get-tuple-element.18), channel_id=2, replica_groups=mesh['region'=12,'x'=4,'y'=8,'core'=2] {'core'}, dimensions={0}, use_global_device_ids=true | all-gather | bytes 49152 | tf_op jit(solution)/shard_map/all_gather | solution.py:542
  16.7 0.0 collective-permute-done.2.far_mask
  16.7 0.0 collective-permute-done.low_y
  16.7 0.0 collective-permute-done.1.high_y
  16.7 1.4 %shard_map.29.sums = f32[24,1,128]{2,1,0:T(1,128)} custom-call(f32[19,4,16,256]{3,2,1,0:T(8,128)S(1)} %get-tuple-element.13.pops, s32[4,16,256]{2,1,0:T(8,128)S(1)} %get-tuple-element.14.mask, f32[15,8,256]{2,1,0:T(8,128)S(1)} %collective-permute-done.low_y, f32[15,8,256]{2,1,0:T(8,128)S(1)} %collective-permute-done.1.high_y, ...), custom_call_target="tpu_custom_call" | custom-call | tf_op jit(solution)/shard_map/pallas_call | solution.py:543
  18.0 12.8 %all-to-all-start = ((f32[24,1,128]{2,1,0:T(1,128)}), f32[24,1,128]{2,1,0:T(1,128)S(1)}, u32[]{:S(2)}, u32[]{:S(2)}) async-start(f32[24,1,128]{2,1,0:T(1,128)} %shard_map.29.sums), calls=%async_computation | async-start | bytes 24576 | tf_op jit(solution)/shard_map/all_to_all | solution.py:557
  30.8 1.1 %shard_map.31 = (f32[15,2,40,128]{3,2,1,0:T(8,128)}, f32[15,2,40,128]{3,2,1,0:T(8,128)S(1)}) custom-call(f32[19,4,16,256]{3,2,1,0:T(8,128)S(1)} %get-tuple-element.13.pops, s32[4,16,256]{2,1,0:T(8,128)S(1)} %get-tuple-element.14.mask, f32[15,8,256]{2,1,0:T(8,128)S(1)} %collective-permute-done.low_y, f32[15,8,256]{2,1,0:T(8,128)S(1)} %collective-permute-done.1.high_y, ...), custom_call_target="tpu_custom_call" | custom-call | tf_op jit(solution)/shard_map/pallas_call | solution.py:549
  31.9 3.3 %collective-permute-start.3 = (f32[15,2,40,128]{3,2,1,0:T(8,128)}, f32[15,2,40,128]{3,2,1,0:T(8,128)S(1)}, u32[]{:S(2)}, u32[]{:S(2)}) collective-permute-start(f32[15,2,40,128]{3,2,1,0:T(8,128)} %get-tuple-element.19), channel_id=1, source_target_pairs={{1,2},{3,4},{5,6},{7,8},{9,10},{11,12},{13,14},{15,16},{17,18},{19... | collective-permute-start | bytes 1843208 | tf_op jit(solution)/shard_map/ppermute | solution.py:512
  35.2 1.9 %collective-permute-start.4 = (f32[15,2,40,128]{3,2,1,0:T(8,128)S(1)}, f32[15,2,40,128]{3,2,1,0:T(8,128)S(1)}, u32[]{:S(2)}, u32[]{:S(2)}) collective-permute-start(f32[15,2,40,128]{3,2,1,0:T(8,128)S(1)} %get-tuple-element.20), channel_id=1, source_target_pairs={{0,1},{2,3},{4,5},{6,7},{8,9},{10,11},{12,13},{14,15},{16,17},{18,... | collective-permute-start | bytes 1843208 | tf_op jit(solution)/shard_map/ppermute | solution.py:512
  37.1 3.1 %all-to-all-done.arrived = f32[24,1,128]{2,1,0:T(1,128)S(1)} async-done(((f32[24,1,128]{2,1,0:T(1,128)}), f32[24,1,128]{2,1,0:T(1,128)S(1)}, u32[]{:S(2)}, u32[]{:S(2)}) %all-to-all-start) | async-done | bytes 12320 | tf_op jit(solution)/shard_map/all_to_all | solution.py:557
  40.2 18.9 %all_to_all.10.arrived = f32[32,1,128]{2,1,0:T(1,128)S(1)} all-to-all(f32[32,1,128]{2,1,0:T(1,128)S(1)} %shard_map.30), channel_id=1, replica_groups=mesh['region'=12,'x'=4,'y'=8,'core'=2] {'x','y'}, dimensions={0} | all-to-all | bytes 32768 | tf_op jit(solution)/shard_map/all_to_all | solution.py:564
  59.1 0.0 collective-permute-done.3.far
  59.1 0.0 collective-permute-done.4.mate
  59.1 3.2 %shard_map.32 = f32[19,4,16,256]{3,2,1,0:T(8,128)} custom-call(f32[32,1,128]{2,1,0:T(1,128)S(1)} %all_to_all.10.arrived, f32[19,4,16,256]{3,2,1,0:T(8,128)S(1)} %get-tuple-element.13.pops, s32[4,16,256]{2,1,0:T(8,128)S(1)} %get-tuple-element.14.mask, f32[15,8,256]{2,1,0:T(8,128)S(1)} %collective-permute-done.low_y, ...), custom_call_target="tpu_custom_call" | custom-call | tf_op jit(solution)/shard_map/pallas_call | solution.py:566
  (1 shorter events, 0.0 us)
Async XLA Ops:
  1.4 15.3 %collective-permute-start = (f32[15,8,256]{2,1,0:T(8,128)S(1)}, f32[15,8,256]{2,1,0:T(8,128)S(1)}, u32[]{:S(2)}, u32[]{:S(2)}) collective-permute-start(f32[15,8,256]{2,1,0:T(8,128)S(1)} %get-tuple-element.15), channel_id=1, source_target_pairs={{0,64},{64,128},{128,192},{192,256},{256,320},{320,384},{384,448},... | collective-permute-start | bytes 368648 | tf_op jit(solution)/shard_map/ppermute | solution.py:509
  6.2 10.5 %collective-permute-start.1 = (f32[15,8,256]{2,1,0:T(8,128)S(1)}, f32[15,8,256]{2,1,0:T(8,128)S(1)}, u32[]{:S(2)}, u32[]{:S(2)}) collective-permute-start(f32[15,8,256]{2,1,0:T(8,128)S(1)} %get-tuple-element.16), channel_id=1, source_target_pairs={{64,0},{128,64},{192,128},{256,192},{320,256},{384,320},{448,384},... | collective-permute-start | bytes 368648 | tf_op jit(solution)/shard_map/ppermute | solution.py:509
  7.5 9.1 %collective-permute-start.2 = (f32[16,256]{1,0:T(8,128)S(1)}, f32[16,256]{1,0:T(8,128)S(1)}, u32[]{:S(2)}, u32[]{:S(2)}) collective-permute-start(f32[16,256]{1,0:T(8,128)S(1)} %get-tuple-element.17), channel_id=1, source_target_pairs={{1,2},{3,4},{5,6},{7,8},{9,10},{11,12},{13,14},{15,16},{17,18},{19... | collective-permute-start | bytes 49160 | tf_op jit(solution)/shard_map/ppermute | solution.py:512
  18.0 22.2 %all-to-all-start = ((f32[24,1,128]{2,1,0:T(1,128)}), f32[24,1,128]{2,1,0:T(1,128)S(1)}, u32[]{:S(2)}, u32[]{:S(2)}) async-start(f32[24,1,128]{2,1,0:T(1,128)} %shard_map.29.sums), calls=%async_computation | async-start | bytes 24576 | tf_op jit(solution)/shard_map/all_to_all | solution.py:557
  31.9 27.2 %collective-permute-start.3 = (f32[15,2,40,128]{3,2,1,0:T(8,128)}, f32[15,2,40,128]{3,2,1,0:T(8,128)S(1)}, u32[]{:S(2)}, u32[]{:S(2)}) collective-permute-start(f32[15,2,40,128]{3,2,1,0:T(8,128)} %get-tuple-element.19), channel_id=1, source_target_pairs={{1,2},{3,4},{5,6},{7,8},{9,10},{11,12},{13,14},{15,16},{17,18},{19... | collective-permute-start | bytes 1843208 | tf_op jit(solution)/shard_map/ppermute | solution.py:512
  35.2 24.0 %collective-permute-start.4 = (f32[15,2,40,128]{3,2,1,0:T(8,128)S(1)}, f32[15,2,40,128]{3,2,1,0:T(8,128)S(1)}, u32[]{:S(2)}, u32[]{:S(2)}) collective-permute-start(f32[15,2,40,128]{3,2,1,0:T(8,128)S(1)} %get-tuple-element.20), channel_id=1, source_target_pairs={{0,1},{2,3},{4,5},{6,7},{8,9},{10,11},{12,13},{14,15},{16,17},{18,... | collective-permute-start | bytes 1843208 | tf_op jit(solution)/shard_map/ppermute | solution.py:512
